TPU v7x, 32 devices: a whole 2x2x4 slice. The times are simulated.
32 devices in a mesh: seq: 16 (over z, y, x), head: 2 (over core).
Axes of the slice: x: 2, y: 2, z: 4, core: 2. Of those that a mesh axis runs over, the one named last changes fastest.
Arguments:
- values: bfloat16 [2, 1024, 4096], P(None, 'seq', 'head'), may hold values from -6 to 6
- keys_b: bfloat16 [2, 1024, 128], P(None, 'seq'), may hold values from -0.29882812 to 0.29882812
- queries_c: bfloat16 [2, 1024, 128], P(None, 'seq'), may hold values from -0.29882812 to 0.29882812
- forget: float32 [2, 64, 1024], P(None, 'head', 'seq'), may hold values from 0 to 2
- skip: float32 [64], P('head'), may hold values from 0.5 to 1.5
- cotangent: bfloat16 [2, 1024, 4096], P(None, 'seq', 'head'), may hold values from -0.59765625 to 0.59765625
Outputs:
- mixed: bfloat16 [2, 1024, 4096], P(None, 'seq', 'head')
- grad_values: bfloat16 [2, 1024, 4096], P(None, 'seq', 'head')
- grad_bc: float32 [2, 2, 1024, 128], P(None, None, ('seq', 'head'))
All inputs are finite; a program needn't handle non-finite values.
Results may differ from a plain program's by a relative error of at most 0.012.
Values sent between devices are 32-bit elements; how exact they have to be, the bound alone decides.
No kernel may reach another device: no remote copies, remote signals or barrier semaphores. Data moves between devices by JAX's collectives and lax.ppermute only.
A program may use at most 128 MiB of HBM per device.

v0:
```python
import jax
import jax.numpy as jnp
from jax import lax
from jax.sharding import PartitionSpec as P


def carried_in(value, axis, combine, identity, reverse):
    peers, mine = (lax.axis_size(axis), lax.axis_index(axis))
    everything = jax.tree.map(lambda part: lax.all_gather(part, axis), value)
    start = jax.tree.map(
        lambda part, zero: jnp.broadcast_to(jnp.asarray(zero, part.dtype), part.shape),
        value,
        identity,
    )

    def step(k, before):
        at = peers - 1 - k if reverse else k
        reached = at > mine if reverse else at < mine
        new = combine(before, jax.tree.map(lambda part: part[at], everything))
        return jax.tree.map(lambda a, b: jnp.where(reached, a, b), new, before)

    return lax.fori_loop(0, peers, step, start)


def own_state(values, keys_wide, logcum):
    seq_count, rows, wide = values.shape
    head_count = logcum.shape[1]
    tail_decay = jnp.exp(logcum[..., -1:] - logcum)
    scaled = values.astype(jnp.float32).reshape(seq_count, rows, head_count, wide // head_count)
    scaled = scaled * jnp.transpose(tail_decay, (0, 2, 1))[..., None]
    return jnp.einsum("suhp,sun->shpn", scaled, keys_wide, preferred_element_type=jnp.float32)


def read_state(queries_wide, logcum, carried):
    inner_part = jnp.einsum(
        "stn,shpn->sthp", queries_wide, carried, preferred_element_type=jnp.float32
    )
    return inner_part * jnp.transpose(jnp.exp(logcum), (0, 2, 1))[..., None]


def block_pass(values, keys_wide, queries_wide, scores, forget, skip, carried):
    seq_count, rows, wide = values.shape
    head_count = skip.shape[0]
    head_width = wide // head_count
    logcum = jnp.cumsum(-forget, axis=-1)
    causal = jnp.arange(rows)[:, None] >= jnp.arange(rows)[None, :]
    log_gap = logcum[..., :, None] - logcum[..., None, :]
    decay_mask = jnp.where(causal, jnp.exp(jnp.where(causal, log_gap, 0.0)), 0.0)
    weights = (scores[:, None] * decay_mask).astype(jnp.bfloat16)
    by_head = values.reshape(seq_count, rows, head_count, head_width)
    own_part = jnp.einsum("shtu,suhp->sthp", weights, by_head, preferred_element_type=jnp.float32)
    summed = (
        own_part
        + read_state(queries_wide, logcum, carried)
        + skip[:, None] * by_head.astype(jnp.float32)
    )
    mixed = summed.reshape(seq_count, rows, wide).astype(jnp.bfloat16)
    final_state = jnp.exp(logcum[..., -1])[..., None, None] * carried + own_state(
        values, keys_wide, logcum
    )
    return (mixed, final_state)


def chain_step(earlier, later):
    return (earlier[0] * later[0], later[0][..., None, None] * earlier[1] + later[1])


def shards(values, keys_b, queries_c, forget, skip, cotangent):
    seq_count, rows, wide = values.shape
    head_count = skip.shape[0]
    head_width = wide // head_count
    state_size = keys_b.shape[-1]
    keys_wide = keys_b.astype(jnp.float32)
    queries_wide = queries_c.astype(jnp.float32)
    scores = jnp.einsum("stn,sun->stu", queries_c, keys_b, preferred_element_type=jnp.float32)
    logcum = jnp.cumsum(-forget, axis=-1)
    carry_decay = jnp.exp(logcum[..., -1])
    state_local = own_state(values, keys_wide, logcum)
    blank = jnp.zeros((seq_count, head_count, head_width, state_size), jnp.float32)
    unit = jnp.ones((seq_count, head_count), jnp.float32)
    _, read_pull = jax.vjp(lambda state: read_state(queries_wide, logcum, state), blank)
    incoming = cotangent.astype(jnp.float32).reshape(seq_count, rows, head_count, head_width)
    seed = read_pull(incoming)[0]
    carried = carried_in((carry_decay, state_local), "seq", chain_step, (unit, blank), False)[1]
    returned = carried_in((carry_decay, seed), "seq", chain_step, (unit, blank), True)[1]

    def whole(value_part, key_part, query_part, score_part, forget_part):
        return block_pass(value_part, key_part, query_part, score_part, forget_part, skip, carried)

    outputs, pullback = jax.vjp(whole, values, keys_wide, queries_wide, scores, forget)
    grads = pullback((cotangent, returned))
    score_grad = grads[3]
    grad_query = grads[2] + jnp.einsum(
        "stu,sun->stn", score_grad, keys_wide, preferred_element_type=jnp.float32
    )
    grad_key = grads[1] + jnp.einsum(
        "stu,stn->sun", score_grad, queries_wide, preferred_element_type=jnp.float32
    )
    grad_bc = lax.psum_scatter(
        jnp.stack([grad_key, grad_query]), "head", scatter_dimension=2, tiled=True
    )
    return (outputs[0], grads[0], grad_bc)


def solution(mesh):
    in_specs = (
        P(None, "seq", "head"),
        P(None, "seq", None),
        P(None, "seq", None),
        P(None, "head", "seq"),
        P("head"),
        P(None, "seq", "head"),
    )
    out_specs = (
        P(None, "seq", "head"),
        P(None, "seq", "head"),
        P(None, None, ("seq", "head"), None),
    )
    return jax.shard_map(shards, mesh=mesh, in_specs=in_specs, out_specs=out_specs, check_vma=False)
```

profile of v0, /device:TPU:0, one launch (start us, length us, event | category | flops | bytes accessed | tf_op | source)
XLA Modules:
  0.0 774.5 jit_solution(16486950503558162982)
XLA Ops:
  8.7 2.1 reshape.53
  10.8 3.6 fusion.5
  15.6 2.6 fusion.3
  18.3 43.1 %all-gather = f32[32,32,1]{1,2,0:T(1,128)S(1)} all-gather(f32[2,32,1]{1,2,0:T(1,128)S(1)} %bitcast.92), channel_id=2, replica_groups=mesh['seq'=16,'head'=2] {'seq'}, dimensions={0}, use_global_device_ids=true | all-gather | bytes 4352 | tf_op jit(solution)/shard_map/all_gather | solution.py:9
  61.5 2.0 fusion.22
  64.7 303.4 %all-gather.8.cloned.1.call-done = f32[32,32,64,128]{3,2,1,0:T(8,128)} async-done(((f32[2,32,64,128]{3,2,1,0:T(8,128)}), f32[32,32,64,128]{3,2,1,0:T(8,128)}) %all-gather.8.cloned.1.call-update) | async-done | bytes 33554448 | tf_op jit(solution)/shard_map/all_gather | solution.py:9
  368.1 62.8 %while.31 = (s32[]{:T(128)}, f32[2,32,64,128]{3,2,1,0:T(8,128)}, s32[]{:T(128)}, f32[16,2,32]{2,1,0:T(2,128)S(1)}, f32[16,2,32,64,128]{4,3,2,1,0:T(8,128)}, /*index=5*/s32[]{:T(128)}, s32[]{:T(128)}, s32[]{:T(128)}, s32[]{:T(128)}) while((s32[]{:T(128)}, f32[2,32,64,128]{3,2,1,0:T(8,128)}, s32[]{:T(128)}, ...), condition=%wide.region_4.5_spmd.clone, body=%wide.region_3.4_spmd.clone.sunk | while | flops 2097160 | bytes 6292391 | solution.py:22
  368.1 3.2 fusion.51
  371.4 3.9 fusion.51
  375.3 4.4 fusion.51
  379.6 4.5 fusion.51
  384.2 3.9 fusion.51
  388.1 3.9 fusion.51
  392.0 3.9 fusion.51
  395.9 3.9 fusion.51
  399.8 3.9 fusion.51
  403.7 3.9 fusion.51
  407.6 3.9 fusion.51
  411.5 3.9 fusion.51
  415.4 3.9 fusion.51
  419.3 3.9 fusion.51
  423.2 3.9 fusion.51
  427.1 3.9 fusion.51
  430.9 2.5 fusion.15
  433.5 2.1 fusion.9
  435.6 284.4 %all-gather.6.cloned.1.call-done = f32[32,32,64,128]{3,2,1,0:T(8,128)} async-done(((f32[2,32,64,128]{3,2,1,0:T(8,128)}), f32[32,32,64,128]{3,2,1,0:T(8,128)}) %all-gather.6.cloned.1.call-update) | async-done | bytes 33554448 | tf_op jit(solution)/shard_map/all_gather | solution.py:9
  720.0 33.9 %while.30 = (s32[]{:T(128)}, f32[2,32,64,128]{3,2,1,0:T(8,128)S(1)}, s32[]{:T(128)}, f32[16,2,32]{2,1,0:T(2,128)S(1)}, f32[16,2,32,64,128]{4,3,2,1,0:T(8,128)}, /*index=5*/s32[]{:T(128)}, s32[]{:T(128)}) while((s32[]{:T(128)}, f32[2,32,64,128]{3,2,1,0:T(8,128)S(1)}, s32[]{:T(128)}, f32[16,2,32]{2,1,0:T(2,128)S(1)}, ...), condition=%wide.region_2.3_spmd.clone, body=%wide.region_1.2_spmd.clone.sunk | while | flops 2097156 | bytes 6292329 | solution.py:22
  720.0 2.1 fusion.50
  722.1 2.1 fusion.50
  724.2 2.1 fusion.50
  726.4 2.1 fusion.50
  728.5 2.1 fusion.50
  730.6 2.1 fusion.50
  732.7 2.1 fusion.50
  734.8 2.1 fusion.50
  737.0 2.1 fusion.50
  739.1 2.1 fusion.50
  741.2 2.1 fusion.50
  743.3 2.1 fusion.50
  745.5 2.1 fusion.50
  747.6 2.1 fusion.50
  749.7 2.1 fusion.50
  751.8 2.1 fusion.50
  753.9 2.3 fusion.14
  757.2 3.2 fusion.7
  761.2 1.6 convert_element_type.37
  762.8 2.8 fusion.13
  766.3 1.6 add_any.11
  (74 shorter events, 6.6 us)
Async XLA Ops:
  7.2 8.4 %copy-start = (bf16[2,64,128]{2,1,0:T(8,128)(2,1)S(1)}, bf16[2,64,128]{2,1,0:T(8,128)(2,1)}, u32[]{:S(2)}) copy-start(bf16[2,64,128]{2,1,0:T(8,128)(2,1)} %param.11) | copy-start | bytes 98308
  7.2 361.0 %all-gather.8.cloned.1.call-start = ((), (), s32[]{:S(2)}) async-start(), calls=%async_computation.3 | async-start | bytes 35651584 | tf_op jit(solution)/shard_map/all_gather | solution.py:9
  10.8 3.7 copy-start.2
  10.8 3.7 copy-start.7
  14.4 705.6 %all-gather.6.cloned.1.call-start = ((), (), s32[]{:S(2)}) async-start(), calls=%async_computation.2 | async-start | bytes 35651584 | tf_op jit(solution)/shard_map/all_gather | solution.py:9
  15.6 45.8 %copy-start.6 = (bf16[2,64,128]{2,1,0:T(8,128)(2,1)S(1)}, bf16[2,64,128]{2,1,0:T(8,128)(2,1)}, u32[]{:S(2)}) copy-start(bf16[2,64,128]{2,1,0:T(8,128)(2,1)} %param.12) | copy-start | bytes 98308
  18.2 749.7 %reduce-scatter.2.cloned.1.call-start = ((), (), s32[]{:S(2)}) async-start(), calls=%async_computation.1 | async-start | bytes 196608 | tf_op jit(solution)/shard_map/reduce_scatter | solution.py:99
  61.5 2.0 copy-start.3
  430.9 2.5 copy-start.1
  753.9 3.3 copy-start.8
  760.5 2.3 copy-start.4
  760.5 2.3 copy-start.5
Sparse Core Ops, SparseCore 0:
  14.6 353.5 all-gather.7
  370.9 349.0 all-gather.5
  757.4 5.6 reduce-scatter.1
where the time goes:
time: 775 us; the launch traced here: 774 us
  waiting for transfers between devices  588 us (76%)
  other arithmetic  98 us (13%)
  blocking collectives  43.1 us (6%)
  matrix products  22.8 us (3%)
  between operations  14 us (2%)
  local copies, waits for them, and re-layouts  8.07 us (1%)
    all_gather x2, waiting for transfers between devices, carried_in(): everything = jax.tree.map(lambda part: lax.all_gather(part, axis), value)  588 us
    select_n x32, other arithmetic, step(): return jax.tree.map(lambda a, b: jnp.where(reached, a, b), new, before)  96 us
    all_gather x1, blocking collectives, carried_in(): everything = jax.tree.map(lambda part: lax.all_gather(part, axis), value)  43.1 us
  transfers between devices with their start and end apart: 3, of which 2 were waited for; matrix products, arithmetic and copies ran while one was open for 11% of the time, Pallas kernels for 0%

commit v1 on v0

v1 whole, which is shorter than its diff:
```python
import functools

import jax
import jax.numpy as jnp
from jax import lax
from jax.experimental import pallas as pl
from jax.experimental.pallas import tpu as pltpu
from jax.sharding import PartitionSpec as P

F32, BF16 = jnp.float32, jnp.bfloat16
LANES = 128
VMEM = pltpu.CompilerParams(vmem_limit_bytes=48 * 1024 * 1024)


def nn(a, b):
    return lax.dot_general(a, b, (((1,), (0,)), ((), ())), preferred_element_type=F32)


def nt(a, b):
    return lax.dot_general(a, b, (((1,), (1,)), ((), ())), preferred_element_type=F32)


def tn(a, b):
    return lax.dot_general(a, b, (((0,), (0,)), ((), ())), preferred_element_type=F32)


def rows_of(block, rows):
    return pl.ds(pl.multiple_of(block * rows, rows), rows)


def pack_kernel(dims, where, values, cotangent, keys, queries, forget, *pieces):
    g, rows, tiles, heads = dims
    mine = where[0]
    upto = lax.broadcasted_iota(jnp.int32, (rows, rows), 0) <= lax.broadcasted_iota(
        jnp.int32, (rows, rows), 1
    )
    logcum = -lax.dot_general(
        forget[...],
        upto.astype(F32),
        (((1,), (0,)), ((), ())),
        precision=lax.Precision.HIGHEST,
        preferred_element_type=F32,
    )
    held = jnp.concatenate([logcum, jnp.zeros_like(logcum)], axis=1)
    keys_wide = keys[...].astype(F32)
    queries_wide = queries[...].astype(F32)
    for d in range(g):
        to = lax.bitwise_xor(mine, d)
        piece = pieces[d]
        for k in range(tiles):
            lanes = pl.ds(pl.multiple_of((to * tiles + k) * LANES, LANES), LANES)
            piece[k * rows : (k + 1) * rows, :] = values[:, lanes].astype(F32)
            piece[(tiles + k) * rows : (tiles + k + 1) * rows, :] = cotangent[:, lanes].astype(F32)
        piece[2 * tiles * rows : (2 * tiles + 1) * rows, :] = keys_wide
        piece[(2 * tiles + 1) * rows : (2 * tiles + 2) * rows, :] = queries_wide
        part = jnp.zeros((heads, LANES), F32)
        for j in range(g):
            part = jnp.where(to == j, held[j * heads : (j + 1) * heads], part)
        piece[(2 * tiles + 2) * rows : (2 * tiles + 2) * rows + heads, :] = part
        piece[(2 * tiles + 2) * rows + heads :, :] = jnp.zeros((8 - heads, LANES), F32)


def spread(columns, heads, tiles):
    per = heads // tiles
    width = LANES // per
    lane = lax.broadcasted_iota(jnp.int32, (columns.shape[0], LANES), 1)
    out = []
    for k in range(tiles):
        wide = jnp.broadcast_to(columns[:, k * per : k * per + 1], lane.shape)
        for e in range(1, per):
            h = k * per + e
            wide = jnp.where(lane >= e * width, columns[:, h : h + 1], wide)
        out.append(wide)
    return jnp.concatenate(out, axis=1) if tiles > 1 else out[0]


def local_kernel(dims, where, skip, *refs):
    g, rows, tiles, heads = dims
    pieces, refs = refs[:g], refs[g:]
    (mixed, grad_v, grad_c, grad_b, v_tail, dy_head, keys, queries, cols, ahead, behind, decay) = refs[:12]
    v_all, dy_all, log_blocks = refs[12:]
    window = g * rows
    width = tiles * LANES
    head_width = width // heads
    mine = where[0]
    for d in range(g):
        piece = pieces[d]
        at = lax.bitwise_xor(mine, d)
        here = rows_of(at, rows)
        for k in range(tiles):
            lanes = slice(k * LANES, (k + 1) * LANES)
            v_all[here, lanes] = piece[k * rows : (k + 1) * rows, :].astype(BF16)
            dy_all[here, lanes] = piece[(tiles + k) * rows : (tiles + k + 1) * rows, :].astype(BF16)
        keys[here, :] = piece[2 * tiles * rows : (2 * tiles + 1) * rows, :].astype(BF16)
        queries[here, :] = piece[(2 * tiles + 1) * rows : (2 * tiles + 2) * rows, :].astype(BF16)
        log_blocks[at] = piece[(2 * tiles + 2) * rows :, :]
    before = jnp.zeros((8, 1), F32)
    parts = []
    for j in range(g):
        block = log_blocks[j][:, :rows] + before
        before = block[:, rows - 1 : rows]
        parts.append(block)
    log_rows = jnp.concatenate(parts, axis=1)
    log_cols = jnp.transpose(log_rows)[:, :heads]
    last = before
    head_decay = spread(jnp.exp(log_cols), heads, tiles)
    tail_decay = spread(jnp.exp(log_cols[window - 1 : window, :] - log_cols), heads, tiles)
    cols[...] = jnp.zeros_like(cols)
    cols[:, :heads] = log_cols
    decay[...] = jnp.broadcast_to(head_decay[window - 1 : window, :], decay.shape)
    v = v_all[...]
    dy = dy_all[...]
    v_wide = v.astype(F32)
    dy_wide = dy.astype(F32)
    v_tail[...] = (v_wide * tail_decay).astype(BF16)
    dy_head[...] = (dy_wide * head_decay).astype(BF16)
    ahead[...] = tn(keys[...], v_tail[...])
    behind[...] = tn(queries[...], dy_head[...])
    mixed[...] = v_wide * skip[...]
    dy_t = jnp.transpose(dy)
    tile = min(window, 256)
    causal = lax.broadcasted_iota(jnp.int32, (tile, tile), 0) >= lax.broadcasted_iota(
        jnp.int32, (tile, tile), 1
    )
    count = window // tile
    dv_t = [[None] * count for _ in range(heads)]
    for q in range(count):
        t = slice(q * tile, (q + 1) * tile)
        for r in range(q + 1):
            u = slice(r * tile, (r + 1) * tile)
            scores = nt(queries[t, :], keys[u, :])
            score_grad = jnp.zeros((tile, tile), F32)
            for h in range(heads):
                lanes = slice(h * head_width, (h + 1) * head_width)
                gap = log_cols[t, h : h + 1] - log_rows[h : h + 1, u]
                mask = jnp.exp(gap)
                if q == r:
                    mask = jnp.where(causal, jnp.exp(jnp.where(causal, gap, 0.0)), 0.0)
                weights = (scores * mask).astype(BF16)
                mixed[t, lanes] += nn(weights, v_all[u, lanes])
                grown = nn(dy_t[lanes, t], weights)
                dv_t[h][r] = grown if dv_t[h][r] is None else dv_t[h][r] + grown
                score_grad = score_grad + nt(dy_all[t, lanes], v_all[u, lanes]) * mask
            score_grad = score_grad.astype(BF16)
            c_part = nn(score_grad, keys[u, :])
            b_part = tn(score_grad, queries[t, :])
            if r == 0:
                grad_c[t, :] = c_part
            else:
                grad_c[t, :] += c_part
            if q == r:
                grad_b[u, :] = b_part
            else:
                grad_b[u, :] += b_part
    whole_t = jnp.concatenate([jnp.concatenate(parts, axis=1) for parts in dv_t], axis=0)
    grad_v[...] = jnp.transpose(whole_t) + dy_wide * skip[...]


def carry_kernel(dims, where, mixed, grad_v, grad_c, grad_b, v_tail, dy_head, keys, queries, cols, carried, returned, *refs):
    g, rows, tiles, heads = dims
    pieces, (mixed_all, grad_v_all, grad_c_all, grad_b_all) = refs[:g], refs[g:]
    window = g * rows
    mine = where[0]
    log_cols = cols[:, :heads]
    head_decay = spread(jnp.exp(log_cols), heads, tiles)
    tail_decay = spread(jnp.exp(log_cols[window - 1 : window, :] - log_cols), heads, tiles)
    state = carried[...].astype(BF16)
    state_grad = returned[...].astype(BF16)
    mixed_all[...] = mixed[...] + head_decay * nn(queries[...], state)
    grad_v_all[...] = grad_v[...] + tail_decay * nn(keys[...], state_grad)
    grad_c_all[...] = grad_c[...] + nt(dy_head[...], state)
    grad_b_all[...] = grad_b[...] + nt(v_tail[...], state_grad)
    for d in range(g):
        piece = pieces[d]
        here = rows_of(lax.bitwise_xor(mine, d), rows)
        for k in range(tiles):
            lanes = slice(k * LANES, (k + 1) * LANES)
            piece[k * rows : (k + 1) * rows, :] = mixed_all[here, lanes]
            piece[(tiles + k) * rows : (tiles + k + 1) * rows, :] = grad_v_all[here, lanes]
        piece[2 * tiles * rows : (2 * tiles + 1) * rows, :] = grad_b_all[here, :]
        piece[(2 * tiles + 1) * rows : (2 * tiles + 2) * rows, :] = grad_c_all[here, :]


def unpack_kernel(dims, seqs, peers, where, *refs):
    g, rows, tiles, heads = dims
    pieces, refs = refs[: g * seqs], refs[g * seqs :]
    mixed, grad_v, shares, total = refs[0], refs[1], refs[2 : 2 + peers], refs[2 + peers]
    mine, core = where[0], where[1]
    for s in range(seqs):
        for d in range(g):
            piece = pieces[s * g + d]
            come = lax.bitwise_xor(mine, d)
            for k in range(tiles):
                lanes = pl.ds(pl.multiple_of((come * tiles + k) * LANES, LANES), LANES)
                mixed[s, :, lanes] = piece[k * rows : (k + 1) * rows, :].astype(BF16)
                grad_v[s, :, lanes] = piece[(tiles + k) * rows : (tiles + k + 1) * rows, :].astype(BF16)
        for w in range(2):
            at = slice((2 * tiles + w) * rows, (2 * tiles + w + 1) * rows)
            summed = pieces[s * g][at, :]
            for d in range(1, g):
                summed = summed + pieces[s * g + d][at, :]
            total[w, s] = summed
    part = rows // peers
    for e in range(peers):
        here = rows_of(lax.bitwise_xor(core, e), part)
        for s in range(seqs):
            for w in range(2):
                shares[e][w, s] = total[w, s, here, :]


def shards(values, keys_b, queries_c, forget, skip, cotangent):
    seqs, rows, wide = values.shape
    head_count = skip.shape[0]
    head_width = wide // head_count
    state_size = keys_b.shape[-1]
    blocks = lax.axis_size("seq")
    peers = lax.axis_size("head")
    g = max(1, min(8, wide // LANES, blocks))
    windows = blocks // g
    heads = head_count // g
    tiles = wide // g // LANES
    dims = (g, rows, tiles, heads)
    window = g * rows
    width = tiles * LANES
    index = lax.axis_index("seq")
    core = lax.axis_index("head")
    where = jnp.stack([lax.rem(index, g), core]).astype(jnp.int32)
    smem = pl.BlockSpec(memory_space=pltpu.SMEM)
    vmem = pl.BlockSpec(memory_space=pltpu.VMEM)

    def exchange(piece, d):
        if d == 0:
            return piece
        return lax.ppermute(piece, "seq", [(i, i ^ d) for i in range(blocks)])

    def shape(*dims, dtype=F32):
        return jax.ShapeDtypeStruct(dims, dtype)

    def call(kernel, out, ins, scratch=()):
        return pl.pallas_call(
            kernel,
            out_shape=out,
            in_specs=[smem] + [vmem] * (len(ins) - 1),
            out_specs=jax.tree.map(lambda _: vmem, out),
            scratch_shapes=list(scratch),
            compiler_params=VMEM,
        )(*ins)

    sent_rows = (2 * tiles + 2) * rows + 8
    back_rows = (2 * tiles + 2) * rows
    skip_part = lax.dynamic_slice(skip, (lax.rem(index, g) * heads,), (heads,))
    skip_row = jnp.repeat(skip_part, head_width)[None, :]
    got = []
    for s in range(seqs):
        pieces = call(
            functools.partial(pack_kernel, dims),
            [shape(sent_rows, LANES)] * g,
            [where, values[s], cotangent[s], keys_b[s], queries_c[s], forget[s]],
        )
        got.append([exchange(piece, d) for d, piece in enumerate(pieces)])
    back = []
    for s in range(seqs):
        (mixed, grad_v, grad_c, grad_b, v_tail, dy_head, keys, queries, cols, ahead, behind, decay) = call(
            functools.partial(local_kernel, dims),
            [
                shape(window, width),
                shape(window, width),
                shape(window, state_size),
                shape(window, state_size),
                shape(window, width, dtype=BF16),
                shape(window, width, dtype=BF16),
                shape(window, state_size, dtype=BF16),
                shape(window, state_size, dtype=BF16),
                shape(window, LANES),
                shape(state_size, width),
                shape(state_size, width),
                shape(8, width),
            ],
            [where, skip_row] + got[s],
            [
                pltpu.VMEM((window, width), BF16),
                pltpu.VMEM((window, width), BF16),
                pltpu.VMEM((g, 8, LANES), F32),
            ],
        )
        carried = jnp.zeros_like(ahead)
        returned = jnp.zeros_like(behind)
        rise = [(i, i + g) for i in range(blocks - g)]
        fall = [(i + g, i) for i in range(blocks - g)]
        for k in range(windows - 1):
            up = ahead if k == 0 else decay[:1] * carried + ahead
            down = behind if k == 0 else decay[:1] * returned + behind
            carried = lax.ppermute(up, "seq", rise)
            returned = lax.ppermute(down, "seq", fall)
        pieces = call(
            functools.partial(carry_kernel, dims),
            [shape(back_rows, LANES)] * g,
            [where, mixed, grad_v, grad_c, grad_b, v_tail, dy_head, keys, queries, cols, carried, returned],
            [pltpu.VMEM((window, width), F32)] * 2 + [pltpu.VMEM((window, state_size), F32)] * 2,
        )
        back.append([exchange(piece, d) for d, piece in enumerate(pieces)])
    part = rows // peers
    outs = call(
        functools.partial(unpack_kernel, dims, seqs, peers),
        [shape(seqs, rows, wide, dtype=BF16)] * 2 + [shape(2, seqs, part, state_size)] * peers,
        [where] + [piece for pieces in back for piece in pieces],
        [pltpu.VMEM((2, seqs, rows, state_size), F32)],
    )
    grad_bc = outs[2]
    for e in range(1, peers):
        grad_bc = grad_bc + lax.ppermute(outs[2 + e], "head", [(c, c ^ e) for c in range(peers)])
    return outs[0], outs[1], grad_bc


def solution(mesh):
    in_specs = (
        P(None, "seq", "head"),
        P(None, "seq", None),
        P(None, "seq", None),
        P(None, "head", "seq"),
        P("head"),
        P(None, "seq", "head"),
    )
    out_specs = (
        P(None, "seq", "head"),
        P(None, "seq", "head"),
        P(None, None, ("seq", "head"), None),
    )
    return jax.shard_map(shards, mesh=mesh, in_specs=in_specs, out_specs=out_specs, check_vma=False)
```

time: 775 us -> 114 us (0.15)
  waiting for transfers between devices: 588 us -> 40.3 us
  other arithmetic: 98 us -> 0.71 us
  starting transfers between devices: 0.12 us -> 53.4 us
  blocking collectives: 43.1 us -> 0 us
  matrix products: 22.8 us -> 0 us
  Pallas kernels: 0 us -> 15.8 us
  between operations: 14 us -> 0.81 us
    all_gather x2 -> x0, waiting for transfers between devices: 588 us -> none  [carried_in(): everything = jax.tree.map(lambda part: lax.all_gather(part, axis), value)]
    select_n x32 -> x0, other arithmetic: 96 us -> none  [step(): return jax.tree.map(lambda a, b: jnp.where(reached, a, b), new, before)]
    ppermute x0 -> x33, starting transfers between devices: none -> 53.4 us  [the longest x28 40.9 us: exchange(): return lax.ppermute(piece, 'seq', [(i, i ^ d) for i in range(blocks)])]
    all_gather x1 -> x0, blocking collectives: 43.1 us -> none  [carried_in(): everything = jax.tree.map(lambda part: lax.all_gather(part, axis), value)]
    ppermute x0 -> x33, waiting for transfers between devices: none -> 40.3 us  [the longest x28 31.2 us: exchange(): return lax.ppermute(piece, 'seq', [(i, i ^ d) for i in range(blocks)])]
    dot_general x12 -> x0, matrix products: 22.8 us -> none  [the longest x3 9.13 us: read_state(): jnp.einsum('stn,shpn->sthp', queries_wide, carried, preferred_element_typ...]
    pallas_call x0 -> x7, Pallas kernels: none -> 15.8 us  [call(): pl.pallas_call(kernel, out_shape=out, in_specs=[smem] + [vmem] * (len(ins...]
  transfers between devices with their start and end apart: 3 -> 33, of which waited for: 2 -> 13; matrix products, arithmetic and copies ran while one was open for 11% -> 0% of each run, Pallas kernels for 0% -> 12%
where the time goes in v1:
time: 114 us
  starting transfers between devices  53.4 us (47%)
  waiting for transfers between devices  40.3 us (35%)
  Pallas kernels  15.8 us (14%)
  local copies, waits for them, and re-layouts  2.93 us (3%)
    ppermute x28, starting transfers between devices, exchange(): return lax.ppermute(piece, 'seq', [(i, i ^ d) for i in range(blocks)])  40.9 us
    ppermute x28, waiting for transfers between devices, exchange(): return lax.ppermute(piece, 'seq', [(i, i ^ d) for i in range(blocks)])  31.2 us
    pallas_call x7, Pallas kernels, call(): pl.pallas_call(kernel, out_shape=out, in_specs=[smem] + [vmem] * (len(ins...  15.8 us
    ppermute x2, starting transfers between devices, shards(): carried = lax.ppermute(up, 'seq', rise)  9.93 us
    ppermute x2, waiting for transfers between devices, shards(): returned = lax.ppermute(down, 'seq', fall)  7.87 us
    ppermute x2, starting transfers between devices, shards(): returned = lax.ppermute(down, 'seq', fall)  2.57 us
  transfers between devices with their start and end apart: 33, of which 13 were waited for; matrix products, arithmetic and copies ran while one was open for 0% of the time, Pallas kernels for 12%

profile of v1, /device:TPU:0, one launch (start us, length us, event | category | flops | bytes accessed | tf_op | source)
XLA Modules:
  0.0 114.0 jit_solution(16518811495316571426)
XLA Ops:
  0.7 0.7 slice_bitcast_fusion.4
  1.5 1.3 %slice_bitcast_fusion = (bf16[64,2048]{1,0:T(8,128)(2,1)S(1)}, bf16[64,2048]{1,0:T(8,128)(2,1)S(1)}, bf16[64,2048]{1,0:T(8,128)(2,1)S(1)}, bf16[64,2048]{1,0:T(8,128)(2,1)S(1)}) fusion(bf16[2,64,2048]{2,1,0:T(8,128)(2,1)} %param.11, bf16[2,64,2048]{2,1,0:T(8,128)(2,1)} %param.6), kind=kLoop, calls=%fused_computation | loop fusion | bytes 2097152 | tf_op jit(solution)/shard_map/squeeze | solution.py:258
  2.8 0.7 shard_map.88
  3.5 3.0 %collective-permute-start.16 = (f32[392,128]{1,0:T(8,128)S(1)}, f32[392,128]{1,0:T(8,128)S(1)}, u32[]{:S(2)}, u32[]{:S(2)}) collective-permute-start(f32[392,128]{1,0:T(8,128)S(1)} %get-tuple-element.89), channel_id=1, source_target_pairs={{0,2},{2,0},{4,6},{6,4},{8,10},{10,8},{12,14},{14,12},{16,18},{18,... | collective-permute-start | bytes 602120 | tf_op jit(solution)/shard_map/ppermute | solution.py:234
  6.5 1.5 %collective-permute-start.17 = (f32[392,128]{1,0:T(8,128)S(1)}, f32[392,128]{1,0:T(8,128)S(1)}, u32[]{:S(2)}, u32[]{:S(2)}) collective-permute-start(f32[392,128]{1,0:T(8,128)S(1)} %get-tuple-element.90), channel_id=1, source_target_pairs={{0,4},{2,6},{4,0},{6,2},{8,12},{10,14},{12,8},{14,10},{16,20},{18,... | collective-permute-start | bytes 602120 | tf_op jit(solution)/shard_map/ppermute | solution.py:234
  8.1 2.0 %collective-permute-start.19 = (f32[392,128]{1,0:T(8,128)S(1)}, f32[392,128]{1,0:T(8,128)S(1)}, u32[]{:S(2)}, u32[]{:S(2)}) collective-permute-start(f32[392,128]{1,0:T(8,128)S(1)} %get-tuple-element.92), channel_id=1, source_target_pairs={{0,8},{2,10},{4,12},{6,14},{8,0},{10,2},{12,4},{14,6},{16,24},{18,... | collective-permute-start | bytes 602120 | tf_op jit(solution)/shard_map/ppermute | solution.py:234
  10.1 1.4 %collective-permute-start.20 = (f32[392,128]{1,0:T(8,128)S(1)}, f32[392,128]{1,0:T(8,128)S(1)}, u32[]{:S(2)}, u32[]{:S(2)}) collective-permute-start(f32[392,128]{1,0:T(8,128)S(1)} %get-tuple-element.93), channel_id=1, source_target_pairs={{0,10},{2,8},{4,14},{6,12},{8,2},{10,0},{12,6},{14,4},{16,26},{18,... | collective-permute-start | bytes 602120 | tf_op jit(solution)/shard_map/ppermute | solution.py:234
  11.5 0.9 collective-permute-done.16.refs_1_
  12.4 3.1 %collective-permute-start.21 = (f32[392,128]{1,0:T(8,128)S(1)}, f32[392,128]{1,0:T(8,128)S(1)}, u32[]{:S(2)}, u32[]{:S(2)}) collective-permute-start(f32[392,128]{1,0:T(8,128)S(1)} %get-tuple-element.94), channel_id=1, source_target_pairs={{0,12},{2,14},{4,8},{6,10},{8,4},{10,6},{12,0},{14,2},{16,28},{18,... | collective-permute-start | bytes 602120 | tf_op jit(solution)/shard_map/ppermute | solution.py:234
  15.5 1.6 %shard_map.85 = (f32[392,128]{1,0:T(8,128)S(1)}, f32[392,128]{1,0:T(8,128)S(1)}, f32[392,128]{1,0:T(8,128)S(1)}, f32[392,128]{1,0:T(8,128)}, f32[392,128]{1,0:T(...) custom-call(s32[2]{0:T(128)S(1)} %pad_add_fusion.where, ...), custom_call_target="tpu_custom_call" | custom-call | tf_op jit(solution)/shard_map/pallas_call | solution.py:240
  17.1 1.8 %collective-permute-start.22 = (f32[392,128]{1,0:T(8,128)S(1)}, f32[392,128]{1,0:T(8,128)S(1)}, u32[]{:S(2)}, u32[]{:S(2)}) collective-permute-start(f32[392,128]{1,0:T(8,128)S(1)} %get-tuple-element.95), channel_id=1, source_target_pairs={{0,14},{2,12},{4,10},{6,8},{8,6},{10,4},{12,2},{14,0},{16,30},{18,... | collective-permute-start | bytes 602120 | tf_op jit(solution)/shard_map/ppermute | solution.py:234
  18.8 1.2 %collective-permute-done.18.refs_3_ = f32[392,128]{1,0:T(8,128)S(1)} collective-permute-done((f32[392,128]{1,0:T(8,128)S(1)}, f32[392,128]{1,0:T(8,128)S(1)}, u32[]{:S(2)}, u32[]{:S(2)}) %collective-permute-start.18) | collective-permute-done | bytes 200736 | tf_op jit(solution)/shard_map/ppermute | solution.py:234
  20.0 2.5 %collective-permute-start = (f32[392,128]{1,0:T(8,128)S(1)}, f32[392,128]{1,0:T(8,128)S(1)}, u32[]{:S(2)}, u32[]{:S(2)}) collective-permute-start(f32[392,128]{1,0:T(8,128)S(1)} %get-tuple-element.62), channel_id=1, source_target_pairs={{0,2},{2,0},{4,6},{6,4},{8,10},{10,8},{12,14},{14,12},{16,18},{18,... | collective-permute-start | bytes 602120 | tf_op jit(solution)/shard_map/ppermute | solution.py:234
  22.5 0.9 collective-permute-start.1
  23.9 2.1 %collective-permute-done.21.refs_6_ = f32[392,128]{1,0:T(8,128)S(1)} collective-permute-done((f32[392,128]{1,0:T(8,128)S(1)}, f32[392,128]{1,0:T(8,128)S(1)}, u32[]{:S(2)}, u32[]{:S(2)}) %collective-permute-start.21) | collective-permute-done | bytes 200736 | tf_op jit(solution)/shard_map/ppermute | solution.py:234
  26.1 1.6 %collective-permute-start.3 = (f32[392,128]{1,0:T(8,128)}, f32[392,128]{1,0:T(8,128)S(1)}, u32[]{:S(2)}, u32[]{:S(2)}) collective-permute-start(f32[392,128]{1,0:T(8,128)} %get-tuple-element.65), channel_id=1, source_target_pairs={{0,8},{2,10},{4,12},{6,14},{8,0},{10,2},{12,4},{14,6},{16,24},{18,... | collective-permute-start | bytes 602120 | tf_op jit(solution)/shard_map/ppermute | solution.py:234
  27.6 3.6 %collective-permute-done.22.refs_7_ = f32[392,128]{1,0:T(8,128)S(1)} collective-permute-done((f32[392,128]{1,0:T(8,128)S(1)}, f32[392,128]{1,0:T(8,128)S(1)}, u32[]{:S(2)}, u32[]{:S(2)}) %collective-permute-start.22) | collective-permute-done | bytes 200736 | tf_op jit(solution)/shard_map/ppermute | solution.py:234
  31.3 1.6 %collective-permute-start.4 = (f32[392,128]{1,0:T(8,128)}, f32[392,128]{1,0:T(8,128)S(1)}, u32[]{:S(2)}, u32[]{:S(2)}) collective-permute-start(f32[392,128]{1,0:T(8,128)} %get-tuple-element.66), channel_id=1, source_target_pairs={{0,10},{2,8},{4,14},{6,12},{8,2},{10,0},{12,6},{14,4},{16,26},{18,... | collective-permute-start | bytes 602120 | tf_op jit(solution)/shard_map/ppermute | solution.py:234
  32.8 1.4 %collective-permute-start.5 = (f32[392,128]{1,0:T(8,128)}, f32[392,128]{1,0:T(8,128)S(1)}, u32[]{:S(2)}, u32[]{:S(2)}) collective-permute-start(f32[392,128]{1,0:T(8,128)} %get-tuple-element.67), channel_id=1, source_target_pairs={{0,12},{2,14},{4,8},{6,10},{8,4},{10,6},{12,0},{14,2},{16,28},{18,... | collective-permute-start | bytes 602120 | tf_op jit(solution)/shard_map/ppermute | solution.py:234
  34.2 7.3 %collective-permute-done.1.refs_2_ = f32[392,128]{1,0:T(8,128)S(1)} collective-permute-done((f32[392,128]{1,0:T(8,128)S(1)}, f32[392,128]{1,0:T(8,128)S(1)}, u32[]{:S(2)}, u32[]{:S(2)}) %collective-permute-start.1) | collective-permute-done | bytes 200736 | tf_op jit(solution)/shard_map/ppermute | solution.py:234
  41.5 0.7 copy-done.2
  42.4 4.6 %shard_map.89 = (f32[512,256]{1,0:T(8,128)S(1)}, f32[512,256]{1,0:T(8,128)S(1)}, f32[512,128]{1,0:T(8,128)S(1)}, f32[512,128]{1,0:T(8,128)S(1)}, bf16[512,256]{1...) custom-call(s32[2]{0:T(128)S(1)} %pad_add_fusion.where, ...), custom_call_target="tpu_custom_call" | custom-call | tf_op jit(solution)/shard_map/pallas_call | solution.py:240
  47.0 4.5 %collective-permute-start.23 = (f32[128,256]{1,0:T(8,128)S(1)}, f32[128,256]{1,0:T(8,128)S(1)}, u32[]{:S(2)}, u32[]{:S(2)}) collective-permute-start(f32[128,256]{1,0:T(8,128)S(1)} %get-tuple-element.105), channel_id=1, source_target_pairs={{0,16},{2,18},{4,20},{6,22},{8,24},{10,26},{12,28},{14,30},{1,17},... | collective-permute-start | bytes 393224 | tf_op jit(solution)/shard_map/ppermute | solution.py:293
  51.5 1.3 %collective-permute-start.24 = (f32[128,256]{1,0:T(8,128)S(1)}, f32[128,256]{1,0:T(8,128)S(1)}, u32[]{:S(2)}, u32[]{:S(2)}) collective-permute-start(f32[128,256]{1,0:T(8,128)S(1)} %get-tuple-element.106), channel_id=1, source_target_pairs={{16,0},{18,2},{20,4},{22,6},{24,8},{26,10},{28,12},{30,14},{17,1},... | collective-permute-start | bytes 393224 | tf_op jit(solution)/shard_map/ppermute | solution.py:294
  52.8 4.6 %shard_map.86 = (f32[512,256]{1,0:T(8,128)S(1)}, f32[512,256]{1,0:T(8,128)S(1)}, f32[512,128]{1,0:T(8,128)S(1)}, f32[512,128]{1,0:T(8,128)S(1)}, bf16[512,256]{1...) custom-call(s32[2]{0:T(128)S(1)} %pad_add_fusion.where, ...), custom_call_target="tpu_custom_call" | custom-call | tf_op jit(solution)/shard_map/pallas_call | solution.py:240
  57.4 5.4 %collective-permute-start.7 = (f32[128,256]{1,0:T(8,128)S(1)}, f32[128,256]{1,0:T(8,128)S(1)}, u32[]{:S(2)}, u32[]{:S(2)}) collective-permute-start(f32[128,256]{1,0:T(8,128)S(1)} %get-tuple-element.78), channel_id=1, source_target_pairs={{0,16},{2,18},{4,20},{6,22},{8,24},{10,26},{12,28},{14,30},{1,17},... | collective-permute-start | bytes 393224 | tf_op jit(solution)/shard_map/ppermute | solution.py:293
  62.9 1.3 %shard_map.90 = (f32[384,128]{1,0:T(8,128)S(1)}, f32[384,128]{1,0:T(8,128)S(1)}, f32[384,128]{1,0:T(8,128)S(1)}, f32[384,128]{1,0:T(8,128)S(1)}, f32[384,128]{1,...) custom-call(s32[2]{0:T(128)S(1)} %pad_add_fusion.where, ...), custom_call_target="tpu_custom_call" | custom-call | tf_op jit(solution)/shard_map/pallas_call | solution.py:240
  64.2 1.7 %collective-permute-start.25 = (f32[384,128]{1,0:T(8,128)S(1)}, f32[384,128]{1,0:T(8,128)S(1)}, u32[]{:S(2)}, u32[]{:S(2)}) collective-permute-start(f32[384,128]{1,0:T(8,128)S(1)} %get-tuple-element.108), channel_id=1, source_target_pairs={{0,2},{2,0},{4,6},{6,4},{8,10},{10,8},{12,14},{14,12},{16,18},{18,... | collective-permute-start | bytes 589832 | tf_op jit(solution)/shard_map/ppermute | solution.py:234
  65.9 2.6 %collective-permute-start.26 = (f32[384,128]{1,0:T(8,128)S(1)}, f32[384,128]{1,0:T(8,128)S(1)}, u32[]{:S(2)}, u32[]{:S(2)}) collective-permute-start(f32[384,128]{1,0:T(8,128)S(1)} %get-tuple-element.109), channel_id=1, source_target_pairs={{0,4},{2,6},{4,0},{6,2},{8,12},{10,14},{12,8},{14,10},{16,20},{18,... | collective-permute-start | bytes 589832 | tf_op jit(solution)/shard_map/ppermute | solution.py:234
  68.5 0.7 collective-permute-start.28
  69.2 1.3 %collective-permute-start.8 = (f32[128,256]{1,0:T(8,128)S(1)}, f32[128,256]{1,0:T(8,128)S(1)}, u32[]{:S(2)}, u32[]{:S(2)}) collective-permute-start(f32[128,256]{1,0:T(8,128)S(1)} %get-tuple-element.79), channel_id=1, source_target_pairs={{16,0},{18,2},{20,4},{22,6},{24,8},{26,10},{28,12},{30,14},{17,1},... | collective-permute-start | bytes 393224 | tf_op jit(solution)/shard_map/ppermute | solution.py:294
  70.5 7.9 %collective-permute-done.8.returned = f32[128,256]{1,0:T(8,128)S(1)} collective-permute-done((f32[128,256]{1,0:T(8,128)S(1)}, f32[128,256]{1,0:T(8,128)S(1)}, u32[]{:S(2)}, u32[]{:S(2)}) %collective-permute-start.8) | collective-permute-done | bytes 131104 | tf_op jit(solution)/shard_map/ppermute | solution.py:294
  78.4 1.5 %collective-permute-start.29 = (f32[384,128]{1,0:T(8,128)S(1)}, f32[384,128]{1,0:T(8,128)S(1)}, u32[]{:S(2)}, u32[]{:S(2)}) collective-permute-start(f32[384,128]{1,0:T(8,128)S(1)} %get-tuple-element.112), channel_id=1, source_target_pairs={{0,10},{2,8},{4,14},{6,12},{8,2},{10,0},{12,6},{14,4},{16,26},{18,... | collective-permute-start | bytes 589832 | tf_op jit(solution)/shard_map/ppermute | solution.py:234
  79.8 1.2 %shard_map.87 = (f32[384,128]{1,0:T(8,128)S(1)}, f32[384,128]{1,0:T(8,128)S(1)}, f32[384,128]{1,0:T(8,128)S(1)}, f32[384,128]{1,0:T(8,128)S(1)}, f32[384,128]{1,...) custom-call(s32[2]{0:T(128)S(1)} %pad_add_fusion.where, ...), custom_call_target="tpu_custom_call" | custom-call | tf_op jit(solution)/shard_map/pallas_call | solution.py:240
  81.1 2.5 %collective-permute-start.30 = (f32[384,128]{1,0:T(8,128)S(1)}, f32[384,128]{1,0:T(8,128)S(1)}, u32[]{:S(2)}, u32[]{:S(2)}) collective-permute-start(f32[384,128]{1,0:T(8,128)S(1)} %get-tuple-element.113), channel_id=1, source_target_pairs={{0,12},{2,14},{4,8},{6,10},{8,4},{10,6},{12,0},{14,2},{16,28},{18,... | collective-permute-start | bytes 589832 | tf_op jit(solution)/shard_map/ppermute | solution.py:234
  83.6 1.9 %collective-permute-start.9 = (f32[384,128]{1,0:T(8,128)S(1)}, f32[384,128]{1,0:T(8,128)S(1)}, u32[]{:S(2)}, u32[]{:S(2)}) collective-permute-start(f32[384,128]{1,0:T(8,128)S(1)} %get-tuple-element.81), channel_id=1, source_target_pairs={{0,2},{2,0},{4,6},{6,4},{8,10},{10,8},{12,14},{14,12},{16,18},{18,... | collective-permute-start | bytes 589832 | tf_op jit(solution)/shard_map/ppermute | solution.py:234
  85.6 2.5 %collective-permute-start.10 = (f32[384,128]{1,0:T(8,128)S(1)}, f32[384,128]{1,0:T(8,128)S(1)}, u32[]{:S(2)}, u32[]{:S(2)}) collective-permute-start(f32[384,128]{1,0:T(8,128)S(1)} %get-tuple-element.82), channel_id=1, source_target_pairs={{0,4},{2,6},{4,0},{6,2},{8,12},{10,14},{12,8},{14,10},{16,20},{18,... | collective-permute-start | bytes 589832 | tf_op jit(solution)/shard_map/ppermute | solution.py:234
  88.1 1.6 %collective-permute-start.11 = (f32[384,128]{1,0:T(8,128)S(1)}, f32[384,128]{1,0:T(8,128)S(1)}, u32[]{:S(2)}, u32[]{:S(2)}) collective-permute-start(f32[384,128]{1,0:T(8,128)S(1)} %get-tuple-element.83), channel_id=1, source_target_pairs={{0,6},{2,4},{4,2},{6,0},{8,14},{10,12},{12,10},{14,8},{16,22},{18,... | collective-permute-start | bytes 589832 | tf_op jit(solution)/shard_map/ppermute | solution.py:234
  89.7 2.7 %collective-permute-done.30.refs_14_ = f32[384,128]{1,0:T(8,128)S(1)} collective-permute-done((f32[384,128]{1,0:T(8,128)S(1)}, f32[384,128]{1,0:T(8,128)S(1)}, u32[]{:S(2)}, u32[]{:S(2)}) %collective-permute-start.30) | collective-permute-done | bytes 196640 | tf_op jit(solution)/shard_map/ppermute | solution.py:234
  92.4 3.4 %collective-permute-done.31.refs_15_ = f32[384,128]{1,0:T(8,128)S(1)} collective-permute-done((f32[384,128]{1,0:T(8,128)S(1)}, f32[384,128]{1,0:T(8,128)S(1)}, u32[]{:S(2)}, u32[]{:S(2)}) %collective-permute-start.31) | collective-permute-done | bytes 196640 | tf_op jit(solution)/shard_map/ppermute | solution.py:234
  95.8 1.1 collective-permute-start.13
  96.8 2.7 %collective-permute-start.14 = (f32[384,128]{1,0:T(8,128)S(1)}, f32[384,128]{1,0:T(8,128)S(1)}, u32[]{:S(2)}, u32[]{:S(2)}) collective-permute-start(f32[384,128]{1,0:T(8,128)S(1)} %get-tuple-element.86), channel_id=1, source_target_pairs={{0,12},{2,14},{4,8},{6,10},{8,4},{10,6},{12,0},{14,2},{16,28},{18,... | collective-permute-start | bytes 589832 | tf_op jit(solution)/shard_map/ppermute | solution.py:234
  99.5 0.8 collective-permute-start.15
  100.3 4.2 %collective-permute-done.11.refs_3_ = f32[384,128]{1,0:T(8,128)S(1)} collective-permute-done((f32[384,128]{1,0:T(8,128)S(1)}, f32[384,128]{1,0:T(8,128)S(1)}, u32[]{:S(2)}, u32[]{:S(2)}) %collective-permute-start.11) | collective-permute-done | bytes 196640 | tf_op jit(solution)/shard_map/ppermute | solution.py:234
  104.7 3.2 %collective-permute-done.14.refs_6_ = f32[384,128]{1,0:T(8,128)S(1)} collective-permute-done((f32[384,128]{1,0:T(8,128)S(1)}, f32[384,128]{1,0:T(8,128)S(1)}, u32[]{:S(2)}, u32[]{:S(2)}) %collective-permute-start.14) | collective-permute-done | bytes 196640 | tf_op jit(solution)/shard_map/ppermute | solution.py:234
  107.9 2.5 %collective-permute-done.15.refs_7_ = f32[384,128]{1,0:T(8,128)S(1)} collective-permute-done((f32[384,128]{1,0:T(8,128)S(1)}, f32[384,128]{1,0:T(8,128)S(1)}, u32[]{:S(2)}, u32[]{:S(2)}) %collective-permute-start.15) | collective-permute-done | bytes 196640 | tf_op jit(solution)/shard_map/ppermute | solution.py:234
  110.3 1.8 %shard_map.91 = (bf16[2,64,2048]{2,1,0:T(8,128)(2,1)}, bf16[2,64,2048]{2,1,0:T(8,128)(2,1)}, f32[2,2,32,128]{3,2,1,0:T(8,128)S(1)}, f32[2,2,32,128]{3,2,1,0:T(8,128)S(1)}) custom-call(s32[2]{0:T(128)S(1)} %pad_add_fusion.where, f32[384,128]{1,0:T(8,128)S(1)} %get-tuple-element.80.refs_0_, f32[384,128]{1,0:T(8,128)S(1)} %collective-permute-done.9.refs_1_, ...), custom_call_target="tpu_custom_call" | custom-call | tf_op jit(solution)/shard_map/pallas_call | solution.py:240
  112.1 1.3 %collective-permute-done.32 = f32[2,2,32,128]{3,2,1,0:T(8,128)S(1)} collective-permute-done((f32[2,2,32,128]{3,2,1,0:T(8,128)S(1)}, f32[2,2,32,128]{3,2,1,0:T(8,128)S(1)}, u32[]{:S(2)}, u32[]{:S(2)}) %collective-permute-start.32) | collective-permute-done | bytes 65568 | tf_op jit(solution)/shard_map/ppermute | solution.py:311
  (39 shorter events, 1.8 us)
Async XLA Ops:
  0.6 0.8 copy-start
  0.6 0.8 copy-start.1
  3.5 8.8 %collective-permute-start.16 = (f32[392,128]{1,0:T(8,128)S(1)}, f32[392,128]{1,0:T(8,128)S(1)}, u32[]{:S(2)}, u32[]{:S(2)}) collective-permute-start(f32[392,128]{1,0:T(8,128)S(1)} %get-tuple-element.89), channel_id=1, source_target_pairs={{0,2},{2,0},{4,6},{6,4},{8,10},{10,8},{12,14},{14,12},{16,18},{18,... | collective-permute-start | bytes 602120 | tf_op jit(solution)/shard_map/ppermute | solution.py:234
  6.5 10.5 %collective-permute-start.17 = (f32[392,128]{1,0:T(8,128)S(1)}, f32[392,128]{1,0:T(8,128)S(1)}, u32[]{:S(2)}, u32[]{:S(2)}) collective-permute-start(f32[392,128]{1,0:T(8,128)S(1)} %get-tuple-element.90), channel_id=1, source_target_pairs={{0,4},{2,6},{4,0},{6,2},{8,12},{10,14},{12,8},{14,10},{16,20},{18,... | collective-permute-start | bytes 602120 | tf_op jit(solution)/shard_map/ppermute | solution.py:234
  8.1 12.0 %collective-permute-start.18 = (f32[392,128]{1,0:T(8,128)S(1)}, f32[392,128]{1,0:T(8,128)S(1)}, u32[]{:S(2)}, u32[]{:S(2)}) collective-permute-start(f32[392,128]{1,0:T(8,128)S(1)} %get-tuple-element.91), channel_id=1, source_target_pairs={{0,6},{2,4},{4,2},{6,0},{8,14},{10,12},{12,10},{14,8},{16,22},{18,... | collective-permute-start | bytes 602120 | tf_op jit(solution)/shard_map/ppermute | solution.py:234
  8.1 14.4 %collective-permute-start.19 = (f32[392,128]{1,0:T(8,128)S(1)}, f32[392,128]{1,0:T(8,128)S(1)}, u32[]{:S(2)}, u32[]{:S(2)}) collective-permute-start(f32[392,128]{1,0:T(8,128)S(1)} %get-tuple-element.92), channel_id=1, source_target_pairs={{0,8},{2,10},{4,12},{6,14},{8,0},{10,2},{12,4},{14,6},{16,24},{18,... | collective-permute-start | bytes 602120 | tf_op jit(solution)/shard_map/ppermute | solution.py:234
  10.1 13.3 %collective-permute-start.20 = (f32[392,128]{1,0:T(8,128)S(1)}, f32[392,128]{1,0:T(8,128)S(1)}, u32[]{:S(2)}, u32[]{:S(2)}) collective-permute-start(f32[392,128]{1,0:T(8,128)S(1)} %get-tuple-element.93), channel_id=1, source_target_pairs={{0,10},{2,8},{4,14},{6,12},{8,2},{10,0},{12,6},{14,4},{16,26},{18,... | collective-permute-start | bytes 602120 | tf_op jit(solution)/shard_map/ppermute | solution.py:234
  12.4 13.7 %collective-permute-start.21 = (f32[392,128]{1,0:T(8,128)S(1)}, f32[392,128]{1,0:T(8,128)S(1)}, u32[]{:S(2)}, u32[]{:S(2)}) collective-permute-start(f32[392,128]{1,0:T(8,128)S(1)} %get-tuple-element.94), channel_id=1, source_target_pairs={{0,12},{2,14},{4,8},{6,10},{8,4},{10,6},{12,0},{14,2},{16,28},{18,... | collective-permute-start | bytes 602120 | tf_op jit(solution)/shard_map/ppermute | solution.py:234
  17.1 14.2 %collective-permute-start.22 = (f32[392,128]{1,0:T(8,128)S(1)}, f32[392,128]{1,0:T(8,128)S(1)}, u32[]{:S(2)}, u32[]{:S(2)}) collective-permute-start(f32[392,128]{1,0:T(8,128)S(1)} %get-tuple-element.95), channel_id=1, source_target_pairs={{0,14},{2,12},{4,10},{6,8},{8,6},{10,4},{12,2},{14,0},{16,30},{18,... | collective-permute-start | bytes 602120 | tf_op jit(solution)/shard_map/ppermute | solution.py:234
  20.0 12.8 %collective-permute-start = (f32[392,128]{1,0:T(8,128)S(1)}, f32[392,128]{1,0:T(8,128)S(1)}, u32[]{:S(2)}, u32[]{:S(2)}) collective-permute-start(f32[392,128]{1,0:T(8,128)S(1)} %get-tuple-element.62), channel_id=1, source_target_pairs={{0,2},{2,0},{4,6},{6,4},{8,10},{10,8},{12,14},{14,12},{16,18},{18,... | collective-permute-start | bytes 602120 | tf_op jit(solution)/shard_map/ppermute | solution.py:234
  22.5 19.0 %collective-permute-start.1 = (f32[392,128]{1,0:T(8,128)S(1)}, f32[392,128]{1,0:T(8,128)S(1)}, u32[]{:S(2)}, u32[]{:S(2)}) collective-permute-start(f32[392,128]{1,0:T(8,128)S(1)} %get-tuple-element.63), channel_id=1, source_target_pairs={{0,4},{2,6},{4,0},{6,2},{8,12},{10,14},{12,8},{14,10},{16,20},{18,... | collective-permute-start | bytes 602120 | tf_op jit(solution)/shard_map/ppermute | solution.py:234
  23.4 23.6 %collective-permute-start.2 = (f32[392,128]{1,0:T(8,128)}, f32[392,128]{1,0:T(8,128)S(1)}, u32[]{:S(2)}, u32[]{:S(2)}) collective-permute-start(f32[392,128]{1,0:T(8,128)} %get-tuple-element.64), channel_id=1, source_target_pairs={{0,6},{2,4},{4,2},{6,0},{8,14},{10,12},{12,10},{14,8},{16,22},{18,... | collective-permute-start | bytes 602120 | tf_op jit(solution)/shard_map/ppermute | solution.py:234
  26.1 25.4 %collective-permute-start.3 = (f32[392,128]{1,0:T(8,128)}, f32[392,128]{1,0:T(8,128)S(1)}, u32[]{:S(2)}, u32[]{:S(2)}) collective-permute-start(f32[392,128]{1,0:T(8,128)} %get-tuple-element.65), channel_id=1, source_target_pairs={{0,8},{2,10},{4,12},{6,14},{8,0},{10,2},{12,4},{14,6},{16,24},{18,... | collective-permute-start | bytes 602120 | tf_op jit(solution)/shard_map/ppermute | solution.py:234
  31.3 21.6 %collective-permute-start.4 = (f32[392,128]{1,0:T(8,128)}, f32[392,128]{1,0:T(8,128)S(1)}, u32[]{:S(2)}, u32[]{:S(2)}) collective-permute-start(f32[392,128]{1,0:T(8,128)} %get-tuple-element.66), channel_id=1, source_target_pairs={{0,10},{2,8},{4,14},{6,12},{8,2},{10,0},{12,6},{14,4},{16,26},{18,... | collective-permute-start | bytes 602120 | tf_op jit(solution)/shard_map/ppermute | solution.py:234
  32.8 20.0 %collective-permute-start.5 = (f32[392,128]{1,0:T(8,128)}, f32[392,128]{1,0:T(8,128)S(1)}, u32[]{:S(2)}, u32[]{:S(2)}) collective-permute-start(f32[392,128]{1,0:T(8,128)} %get-tuple-element.67), channel_id=1, source_target_pairs={{0,12},{2,14},{4,8},{6,10},{8,4},{10,6},{12,0},{14,2},{16,28},{18,... | collective-permute-start | bytes 602120 | tf_op jit(solution)/shard_map/ppermute | solution.py:234
  41.5 11.3 %collective-permute-start.6 = (f32[392,128]{1,0:T(8,128)S(1)}, f32[392,128]{1,0:T(8,128)S(1)}, u32[]{:S(2)}, u32[]{:S(2)}) collective-permute-start(f32[392,128]{1,0:T(8,128)S(1)} %get-tuple-element.68), channel_id=1, source_target_pairs={{0,14},{2,12},{4,10},{6,8},{8,6},{10,4},{12,2},{14,0},{16,30},{18,... | collective-permute-start | bytes 602120 | tf_op jit(solution)/shard_map/ppermute | solution.py:234
  41.5 0.7 copy-start.2
  47.0 15.9 %collective-permute-start.23 = (f32[128,256]{1,0:T(8,128)S(1)}, f32[128,256]{1,0:T(8,128)S(1)}, u32[]{:S(2)}, u32[]{:S(2)}) collective-permute-start(f32[128,256]{1,0:T(8,128)S(1)} %get-tuple-element.105), channel_id=1, source_target_pairs={{0,16},{2,18},{4,20},{6,22},{8,24},{10,26},{12,28},{14,30},{1,17},... | collective-permute-start | bytes 393224 | tf_op jit(solution)/shard_map/ppermute | solution.py:293
  51.5 11.4 %collective-permute-start.24 = (f32[128,256]{1,0:T(8,128)S(1)}, f32[128,256]{1,0:T(8,128)S(1)}, u32[]{:S(2)}, u32[]{:S(2)}) collective-permute-start(f32[128,256]{1,0:T(8,128)S(1)} %get-tuple-element.106), channel_id=1, source_target_pairs={{16,0},{18,2},{20,4},{22,6},{24,8},{26,10},{28,12},{30,14},{17,1},... | collective-permute-start | bytes 393224 | tf_op jit(solution)/shard_map/ppermute | solution.py:294
  57.4 11.8 %collective-permute-start.7 = (f32[128,256]{1,0:T(8,128)S(1)}, f32[128,256]{1,0:T(8,128)S(1)}, u32[]{:S(2)}, u32[]{:S(2)}) collective-permute-start(f32[128,256]{1,0:T(8,128)S(1)} %get-tuple-element.78), channel_id=1, source_target_pairs={{0,16},{2,18},{4,20},{6,22},{8,24},{10,26},{12,28},{14,30},{1,17},... | collective-permute-start | bytes 393224 | tf_op jit(solution)/shard_map/ppermute | solution.py:293
  64.2 16.9 %collective-permute-start.25 = (f32[384,128]{1,0:T(8,128)S(1)}, f32[384,128]{1,0:T(8,128)S(1)}, u32[]{:S(2)}, u32[]{:S(2)}) collective-permute-start(f32[384,128]{1,0:T(8,128)S(1)} %get-tuple-element.108), channel_id=1, source_target_pairs={{0,2},{2,0},{4,6},{6,4},{8,10},{10,8},{12,14},{14,12},{16,18},{18,... | collective-permute-start | bytes 589832 | tf_op jit(solution)/shard_map/ppermute | solution.py:234
  65.9 17.7 %collective-permute-start.26 = (f32[384,128]{1,0:T(8,128)S(1)}, f32[384,128]{1,0:T(8,128)S(1)}, u32[]{:S(2)}, u32[]{:S(2)}) collective-permute-start(f32[384,128]{1,0:T(8,128)S(1)} %get-tuple-element.109), channel_id=1, source_target_pairs={{0,4},{2,6},{4,0},{6,2},{8,12},{10,14},{12,8},{14,10},{16,20},{18,... | collective-permute-start | bytes 589832 | tf_op jit(solution)/shard_map/ppermute | solution.py:234
  68.5 15.1 %collective-permute-start.27 = (f32[384,128]{1,0:T(8,128)S(1)}, f32[384,128]{1,0:T(8,128)S(1)}, u32[]{:S(2)}, u32[]{:S(2)}) collective-permute-start(f32[384,128]{1,0:T(8,128)S(1)} %get-tuple-element.110), channel_id=1, source_target_pairs={{0,6},{2,4},{4,2},{6,0},{8,14},{10,12},{12,10},{14,8},{16,22},{18,... | collective-permute-start | bytes 589832 | tf_op jit(solution)/shard_map/ppermute | solution.py:234
  68.5 17.1 %collective-permute-start.28 = (f32[384,128]{1,0:T(8,128)S(1)}, f32[384,128]{1,0:T(8,128)S(1)}, u32[]{:S(2)}, u32[]{:S(2)}) collective-permute-start(f32[384,128]{1,0:T(8,128)S(1)} %get-tuple-element.111), channel_id=1, source_target_pairs={{0,8},{2,10},{4,12},{6,14},{8,0},{10,2},{12,4},{14,6},{16,24},{18,... | collective-permute-start | bytes 589832 | tf_op jit(solution)/shard_map/ppermute | solution.py:234
  69.2 9.2 %collective-permute-start.8 = (f32[128,256]{1,0:T(8,128)S(1)}, f32[128,256]{1,0:T(8,128)S(1)}, u32[]{:S(2)}, u32[]{:S(2)}) collective-permute-start(f32[128,256]{1,0:T(8,128)S(1)} %get-tuple-element.79), channel_id=1, source_target_pairs={{16,0},{18,2},{20,4},{22,6},{24,8},{26,10},{28,12},{30,14},{17,1},... | collective-permute-start | bytes 393224 | tf_op jit(solution)/shard_map/ppermute | solution.py:294
  78.4 9.7 %collective-permute-start.29 = (f32[384,128]{1,0:T(8,128)S(1)}, f32[384,128]{1,0:T(8,128)S(1)}, u32[]{:S(2)}, u32[]{:S(2)}) collective-permute-start(f32[384,128]{1,0:T(8,128)S(1)} %get-tuple-element.112), channel_id=1, source_target_pairs={{0,10},{2,8},{4,14},{6,12},{8,2},{10,0},{12,6},{14,4},{16,26},{18,... | collective-permute-start | bytes 589832 | tf_op jit(solution)/shard_map/ppermute | solution.py:234
  81.1 11.3 %collective-permute-start.30 = (f32[384,128]{1,0:T(8,128)S(1)}, f32[384,128]{1,0:T(8,128)S(1)}, u32[]{:S(2)}, u32[]{:S(2)}) collective-permute-start(f32[384,128]{1,0:T(8,128)S(1)} %get-tuple-element.113), channel_id=1, source_target_pairs={{0,12},{2,14},{4,8},{6,10},{8,4},{10,6},{12,0},{14,2},{16,28},{18,... | collective-permute-start | bytes 589832 | tf_op jit(solution)/shard_map/ppermute | solution.py:234
  83.6 12.2 %collective-permute-start.31 = (f32[384,128]{1,0:T(8,128)S(1)}, f32[384,128]{1,0:T(8,128)S(1)}, u32[]{:S(2)}, u32[]{:S(2)}) collective-permute-start(f32[384,128]{1,0:T(8,128)S(1)} %get-tuple-element.114), channel_id=1, source_target_pairs={{0,14},{2,12},{4,10},{6,8},{8,6},{10,4},{12,2},{14,0},{16,30},{18,... | collective-permute-start | bytes 589832 | tf_op jit(solution)/shard_map/ppermute | solution.py:234
  83.6 13.2 %collective-permute-start.9 = (f32[384,128]{1,0:T(8,128)S(1)}, f32[384,128]{1,0:T(8,128)S(1)}, u32[]{:S(2)}, u32[]{:S(2)}) collective-permute-start(f32[384,128]{1,0:T(8,128)S(1)} %get-tuple-element.81), channel_id=1, source_target_pairs={{0,2},{2,0},{4,6},{6,4},{8,10},{10,8},{12,14},{14,12},{16,18},{18,... | collective-permute-start | bytes 589832 | tf_op jit(solution)/shard_map/ppermute | solution.py:234
  85.6 14.0 %collective-permute-start.10 = (f32[384,128]{1,0:T(8,128)S(1)}, f32[384,128]{1,0:T(8,128)S(1)}, u32[]{:S(2)}, u32[]{:S(2)}) collective-permute-start(f32[384,128]{1,0:T(8,128)S(1)} %get-tuple-element.82), channel_id=1, source_target_pairs={{0,4},{2,6},{4,0},{6,2},{8,12},{10,14},{12,8},{14,10},{16,20},{18,... | collective-permute-start | bytes 589832 | tf_op jit(solution)/shard_map/ppermute | solution.py:234
  88.1 16.4 %collective-permute-start.11 = (f32[384,128]{1,0:T(8,128)S(1)}, f32[384,128]{1,0:T(8,128)S(1)}, u32[]{:S(2)}, u32[]{:S(2)}) collective-permute-start(f32[384,128]{1,0:T(8,128)S(1)} %get-tuple-element.83), channel_id=1, source_target_pairs={{0,6},{2,4},{4,2},{6,0},{8,14},{10,12},{12,10},{14,8},{16,22},{18,... | collective-permute-start | bytes 589832 | tf_op jit(solution)/shard_map/ppermute | solution.py:234
  92.4 12.1 %collective-permute-start.12 = (f32[384,128]{1,0:T(8,128)S(1)}, f32[384,128]{1,0:T(8,128)S(1)}, u32[]{:S(2)}, u32[]{:S(2)}) collective-permute-start(f32[384,128]{1,0:T(8,128)S(1)} %get-tuple-element.84), channel_id=1, source_target_pairs={{0,8},{2,10},{4,12},{6,14},{8,0},{10,2},{12,4},{14,6},{16,24},{18,... | collective-permute-start | bytes 589832 | tf_op jit(solution)/shard_map/ppermute | solution.py:234
  95.8 8.9 %collective-permute-start.13 = (f32[384,128]{1,0:T(8,128)S(1)}, f32[384,128]{1,0:T(8,128)S(1)}, u32[]{:S(2)}, u32[]{:S(2)}) collective-permute-start(f32[384,128]{1,0:T(8,128)S(1)} %get-tuple-element.85), channel_id=1, source_target_pairs={{0,10},{2,8},{4,14},{6,12},{8,2},{10,0},{12,6},{14,4},{16,26},{18,... | collective-permute-start | bytes 589832 | tf_op jit(solution)/shard_map/ppermute | solution.py:234
  96.8 11.0 %collective-permute-start.14 = (f32[384,128]{1,0:T(8,128)S(1)}, f32[384,128]{1,0:T(8,128)S(1)}, u32[]{:S(2)}, u32[]{:S(2)}) collective-permute-start(f32[384,128]{1,0:T(8,128)S(1)} %get-tuple-element.86), channel_id=1, source_target_pairs={{0,12},{2,14},{4,8},{6,10},{8,4},{10,6},{12,0},{14,2},{16,28},{18,... | collective-permute-start | bytes 589832 | tf_op jit(solution)/shard_map/ppermute | solution.py:234
  99.5 10.8 %collective-permute-start.15 = (f32[384,128]{1,0:T(8,128)S(1)}, f32[384,128]{1,0:T(8,128)S(1)}, u32[]{:S(2)}, u32[]{:S(2)}) collective-permute-start(f32[384,128]{1,0:T(8,128)S(1)} %get-tuple-element.87), channel_id=1, source_target_pairs={{0,14},{2,12},{4,10},{6,8},{8,6},{10,4},{12,2},{14,0},{16,30},{18,... | collective-permute-start | bytes 589832 | tf_op jit(solution)/shard_map/ppermute | solution.py:234
  112.1 1.3 %collective-permute-start.32 = (f32[2,2,32,128]{3,2,1,0:T(8,128)S(1)}, f32[2,2,32,128]{3,2,1,0:T(8,128)S(1)}, u32[]{:S(2)}, u32[]{:S(2)}) collective-permute-start(f32[2,2,32,128]{3,2,1,0:T(8,128)S(1)} %get-tuple-element.118), channel_id=1, source_target_pairs={{0,1},{1,0},{2,3},{3,2},{4,5},{5,4},{6,7},{7,6},{8,9},{9,8},{10,11... | collective-permute-start | bytes 196616 | tf_op jit(solution)/shard_map/ppermute | solution.py:311

commit v2 on v1

v2 whole, which is shorter than its diff:
```python
import functools

import jax
import jax.numpy as jnp
from jax import lax
from jax.experimental import pallas as pl
from jax.experimental.pallas import tpu as pltpu
from jax.sharding import PartitionSpec as P

F32, BF16 = jnp.float32, jnp.bfloat16
LANES = 128
EXTRA = 8
MIB = 1024 * 1024


def nn(a, b):
    return lax.dot_general(a, b, (((1,), (0,)), ((), ())), preferred_element_type=F32)


def nt(a, b):
    return lax.dot_general(a, b, (((1,), (1,)), ((), ())), preferred_element_type=F32)


def tn(a, b):
    return lax.dot_general(a, b, (((0,), (0,)), ((), ())), preferred_element_type=F32)


def rows_of(block, rows):
    return pl.ds(pl.multiple_of(block * rows, rows), rows)


def partners(g):
    order = [0]
    for d in range(g // 2, g - 1):
        order += [d, g - 1 - d]
    return order + [g - 1] * (g > 1)


def place(g):
    index = lax.axis_index("seq")
    return lax.rem(index, g), lax.rem(lax.axis_index("head"), 2), lax.div(index, g)


def pick(flag, one, zero):
    if isinstance(flag, bool):
        return one if flag else zero
    return jnp.where(flag, one, zero)


def spread(columns, heads, tiles):
    per = heads // tiles
    width = LANES // per
    lane = lax.broadcasted_iota(jnp.int32, (columns.shape[0], LANES), 1)
    out = []
    for k in range(tiles):
        wide = jnp.broadcast_to(columns[:, k * per : k * per + 1], lane.shape)
        for e in range(1, per):
            h = k * per + e
            wide = jnp.where(lane >= e * width, columns[:, h : h + 1], wide)
        out.append(wide)
    return jnp.concatenate(out, axis=1) if tiles > 1 else out[0]


def pack_kernel(dims, shared, values, cotangent, keys, queries, forget, skip, *refs):
    g, rows, tiles, heads = dims
    pieces, (v_now, dy_now, b_now, c_now, f_now, s_now, arrived) = refs[:g], refs[g:]
    mine, core, _ = place(g)
    seq = core if shared else 1 - core
    half = values.shape[2] // 2
    moves = [(forget.at[seq], f_now), (skip, s_now)]
    if shared:
        moves += [(keys.at[seq], b_now), (queries.at[seq], c_now)]
    for whole, now in ((values, v_now), (cotangent, dy_now)):
        for k in range(2):
            lanes = pl.ds(k * half, half)
            moves.append((whole.at[seq, :, lanes], now.at[:, lanes]))
    copies = [pltpu.make_async_copy(a, b, arrived.at[n]) for n, (a, b) in enumerate(moves)]
    for copy in copies:
        copy.start()
    upto = lax.broadcasted_iota(jnp.int32, (rows, rows), 0) <= lax.broadcasted_iota(
        jnp.int32, (rows, rows), 1
    )
    for copy in copies:
        copy.wait()
    count = skip.shape[1]
    own = lax.broadcasted_iota(jnp.int32, (count, count), 0) == lax.broadcasted_iota(
        jnp.int32, (count, count), 1
    )
    skips = jnp.sum(jnp.where(own, s_now[...], 0.0), axis=1, keepdims=True)
    logcum = -lax.dot_general(
        f_now[...],
        upto.astype(F32),
        (((1,), (0,)), ((), ())),
        precision=lax.Precision.HIGHEST,
        preferred_element_type=F32,
    )
    held = jnp.concatenate([logcum, jnp.broadcast_to(skips, logcum.shape)], axis=1)
    for piece, d in zip(pieces, partners(g)):
        to = lax.bitwise_xor(mine, d)
        for k in range(tiles):
            lanes = pl.ds(pl.multiple_of((to * tiles + k) * LANES, LANES), LANES)
            piece[k * rows : (k + 1) * rows, :] = v_now[:, lanes].astype(F32)
            piece[(tiles + k) * rows : (tiles + k + 1) * rows, :] = dy_now[:, lanes].astype(F32)
        part = held[:heads]
        for j in range(1, g):
            part = jnp.where(to == j, held[j * heads : (j + 1) * heads], part)
        end = 2 * tiles * rows
        piece[end : end + heads, :] = part
        if heads < EXTRA:
            piece[end + heads : end + EXTRA, :] = jnp.zeros((EXTRA - heads, LANES), F32)
        if shared:
            piece[end + EXTRA : end + EXTRA + rows, :] = b_now[...].astype(F32)
            piece[end + EXTRA + rows : end + EXTRA + 2 * rows, :] = c_now[...].astype(F32)


def gather_kernel(dims, shared, *refs):
    g, rows, tiles, heads = dims
    pieces, refs = refs[:g], refs[g:]
    if shared:
        v_all, dy_all, log_rows, skip_row, keys, queries = refs[:6]
    else:
        keys, queries, v_all, dy_all, log_rows, skip_row = refs[:6]
    v_tail, dy_head, first, second, decay, blocks = refs[6:]
    window = g * rows
    mine, _, at_window = place(g)
    end = 2 * tiles * rows
    for piece, d in zip(pieces, partners(g)):
        at = lax.bitwise_xor(mine, d)
        here = rows_of(at, rows)
        for k in range(tiles):
            lanes = slice(k * LANES, (k + 1) * LANES)
            v_all[here, lanes] = piece[k * rows : (k + 1) * rows, :].astype(BF16)
            dy_all[here, lanes] = piece[(tiles + k) * rows : (tiles + k + 1) * rows, :].astype(BF16)
        blocks[at] = piece[end : end + EXTRA, :]
        if shared:
            keys[here, :] = piece[end + EXTRA : end + EXTRA + rows, :].astype(BF16)
            queries[here, :] = piece[end + EXTRA + rows : end + EXTRA + 2 * rows, :].astype(BF16)
    before = jnp.zeros((EXTRA, 1), F32)
    parts = []
    for j in range(g):
        block = blocks[j][:, :rows] + before
        before = block[:, rows - 1 : rows]
        parts.append(block)
    logs = jnp.concatenate(parts, axis=1)
    log_rows[...] = logs
    cols = jnp.transpose(logs)[:, :heads]
    skips = jnp.transpose(blocks[0])[rows : rows + 1, :heads]
    skip_row[...] = jnp.broadcast_to(spread(skips, heads, tiles), skip_row.shape)
    last = cols[window - 1 : window, :]
    v_tail[...] = (v_all[...].astype(F32) * spread(jnp.exp(last - cols), heads, tiles)).astype(BF16)
    dy_head[...] = (dy_all[...].astype(F32) * spread(jnp.exp(cols), heads, tiles)).astype(BF16)
    ahead = tn(keys[...], v_tail[...])
    behind = tn(queries[...], dy_head[...])
    odd = lax.rem(at_window, 2) == 1
    first[...] = jnp.where(odd, behind, ahead)
    second[...] = jnp.where(odd, ahead, behind)
    decay[...] = jnp.broadcast_to(spread(jnp.exp(last), heads, tiles), decay.shape)


def local_kernel(dims, v_all, dy_all, log_rows, skip_row, keys, queries, mixed, grad_v, grad_b, grad_c):
    g, rows, tiles, heads = dims
    window = g * rows
    head_width = tiles * LANES // heads
    log_cols = jnp.transpose(log_rows[...])[:, :heads]
    skips = skip_row[:1, :]
    mixed[...] = v_all[...].astype(F32) * skips
    dy_t = jnp.transpose(dy_all[...])
    tile = min(window, 256)
    causal = lax.broadcasted_iota(jnp.int32, (tile, tile), 0) >= lax.broadcasted_iota(
        jnp.int32, (tile, tile), 1
    )
    count = window // tile
    dv_t = [[None] * count for _ in range(heads)]
    for q in range(count):
        t = slice(q * tile, (q + 1) * tile)
        for r in range(q + 1):
            u = slice(r * tile, (r + 1) * tile)
            scores = nt(queries[t, :], keys[u, :])
            score_grad = jnp.zeros((tile, tile), F32)
            for h in range(heads):
                lanes = slice(h * head_width, (h + 1) * head_width)
                gap = log_cols[t, h : h + 1] - log_rows[h : h + 1, u]
                if q == r:
                    mask = jnp.where(causal, jnp.exp(jnp.where(causal, gap, 0.0)), 0.0)
                else:
                    mask = jnp.exp(gap)
                weights = (scores * mask).astype(BF16)
                mixed[t, lanes] += nn(weights, v_all[u, lanes])
                grown = nn(dy_t[lanes, t], weights)
                dv_t[h][r] = grown if dv_t[h][r] is None else dv_t[h][r] + grown
                score_grad = score_grad + nt(dy_all[t, lanes], v_all[u, lanes]) * mask
            score_grad = score_grad.astype(BF16)
            c_part = nn(score_grad, keys[u, :])
            b_part = tn(score_grad, queries[t, :])
            if r == 0:
                grad_c[t, :] = c_part
            else:
                grad_c[t, :] += c_part
            if q == r:
                grad_b[u, :] = b_part
            else:
                grad_b[u, :] += b_part
    whole_t = jnp.concatenate([jnp.concatenate(parts, axis=1) for parts in dv_t], axis=0)
    grad_v[...] = jnp.transpose(whole_t) + dy_all[...].astype(F32) * skips


def step_kernel(decay, state, total, moved):
    moved[...] = decay[:1, :] * state[...] + total[...]


def halves_of(dims, windows, half):
    _, _, at = place(dims[0])
    if windows != 4:
        return half == 0, None
    low = at < 2
    return (low if half == 0 else at >= 2), (at == 1) | (at == 2)


def half_kernel(dims, windows, half, last_part, log_rows, mixed, grad_v, grad_b, grad_c, *refs):
    g, rows, tiles, heads = dims
    if last_part:
        other, refs = refs[0], refs[1:]
    keys, queries, v_tail, dy_head, refs = *refs[:4], refs[4:]
    states, refs = refs[: len(refs) - g - 2], refs[len(refs) - g - 2 :]
    pieces, total, whole = refs[:g], refs[g], refs[g + 1]
    window = g * rows
    mine, _, _ = place(g)
    forward, inner = halves_of(dims, windows, half)
    if inner is None:
        state = states[0][...]
    elif half == 0:
        state = jnp.where(inner, states[0][...], 0.0)
    else:
        state = jnp.where(inner, states[0][...], states[1][...])
    state = state.astype(BF16)
    cols = jnp.transpose(log_rows[...])[:, :heads]
    last = cols[window - 1 : window, :]
    gain = spread(jnp.exp(pick(forward, cols, last - cols)), heads, tiles)
    more = gain * nn(pick(forward, queries[...], keys[...]), state)
    whole[...] = pick(forward, mixed[...], grad_v[...]) + more
    summed = pick(forward, grad_c[...], grad_b[...]) + nt(pick(forward, dy_head[...], v_tail[...]), state)
    if last_part:
        summed = summed + other[...]
    total[...] = summed
    for piece, d in zip(pieces, partners(g)):
        here = rows_of(lax.bitwise_xor(mine, d), rows)
        for k in range(tiles):
            piece[k * rows : (k + 1) * rows, :] = whole[here, k * LANES : (k + 1) * LANES]
        if last_part:
            piece[tiles * rows : (tiles + 1) * rows, :] = total[here, :]


def unpack_kernel(dims, windows, half, last_part, *refs):
    g, rows, tiles, heads = dims
    pieces, refs = refs[:g], refs[g:]
    if last_part or half:
        refs = refs[2:]
    mixed, grad_v, *shares, now, sent = refs
    if last_part:
        shares, total = shares[:-1], shares[-1]
    mine, core, _ = place(g)
    seq = 1 - core if last_part else core
    forward, _ = halves_of(dims, windows, half)
    for piece, d in zip(pieces, partners(g)):
        come = lax.bitwise_xor(mine, d)
        for k in range(tiles):
            lanes = pl.ds(pl.multiple_of((come * tiles + k) * LANES, LANES), LANES)
            now[:, lanes] = piece[k * rows : (k + 1) * rows, :].astype(BF16)

    def send(whole):
        part = now.shape[1] // 4
        copies = []
        for k in range(4):
            lanes = pl.ds(k * part, part)
            copies.append(pltpu.make_async_copy(now.at[:, lanes], whole.at[seq, :, lanes], sent.at[k]))
        for copy in copies:
            copy.start()
        for copy in copies:
            copy.wait()

    if isinstance(forward, bool):
        send(mixed if forward else grad_v)
    else:
        pl.when(forward)(lambda: send(mixed))
        pl.when(jnp.logical_not(forward))(lambda: send(grad_v))
    if last_part:
        at = slice(tiles * rows, (tiles + 1) * rows)
        total[...] = functools.reduce(jnp.add, [piece[at, :] for piece in pieces])
        for e, share in enumerate(shares):
            part = rows // len(shares)
            share[...] = total[rows_of(lax.bitwise_xor(lax.axis_index("head"), e), part), :]


def shards(values, keys_b, queries_c, forget, skip, cotangent):
    seqs, rows, wide = values.shape
    head_count = skip.shape[0]
    state_size = keys_b.shape[-1]
    blocks = lax.axis_size("seq")
    peers = lax.axis_size("head")
    g = max(1, min(4, wide // LANES, blocks))
    windows = blocks // g
    heads = head_count // g
    tiles = wide // g // LANES
    dims = (g, rows, tiles, heads)
    window = g * rows
    width = tiles * LANES
    index = lax.axis_index("seq")
    vmem = pl.BlockSpec(memory_space=pltpu.VMEM)

    def swap(send, pieces):
        return [send(piece, d) for d, piece in zip(partners(g), pieces)]

    def same(piece, d):
        if d == 0:
            return piece
        return lax.ppermute(piece, "seq", [(i, i ^ d) for i in range(blocks)])

    def cross(piece, d):
        perm = [
            (i * peers + c, (i ^ d) * peers + (c ^ 1)) for i in range(blocks) for c in range(peers)
        ]
        return lax.ppermute(piece, ("seq", "head"), perm)

    def shape(*dims, dtype=F32):
        return jax.ShapeDtypeStruct(dims, dtype)

    hbm = pl.BlockSpec(memory_space=pltpu.HBM)

    def call(kernel, out, ins, scratch=(), after=(), far=(), far_out=(), aliases={}, limit=48):
        count, extra = len(ins), len(after)

        def body(*refs):
            kernel(*refs[:count], *refs[count + extra :])

        outs = pl.pallas_call(
            body,
            out_shape=out,
            in_specs=[hbm if n in far else vmem for n in range(count)] + [hbm] * extra,
            out_specs=[hbm if n in far_out else vmem for n in range(len(out))],
            scratch_shapes=list(scratch),
            input_output_aliases=aliases,
            compiler_params=pltpu.CompilerParams(vmem_limit_bytes=limit * MIB),
        )(*ins, *after)
        return list(outs)

    base = 2 * tiles * rows
    got = []
    for shared in (True, False):
        pieces = call(
            functools.partial(pack_kernel, dims, shared),
            [shape(base + EXTRA + (2 * rows if shared else 0), LANES)] * g,
            [values, cotangent, keys_b, queries_c, forget, skip[None, :]],
            [
                pltpu.VMEM((rows, wide), BF16),
                pltpu.VMEM((rows, wide), BF16),
                pltpu.VMEM((rows, state_size), BF16),
                pltpu.VMEM((rows, state_size), BF16),
                pltpu.VMEM((head_count, rows), F32),
                pltpu.VMEM((1, head_count), F32),
                pltpu.SemaphoreType.DMA((8,)),
            ],
            after=[] if shared else got[0][1:2],
            far=range(6),
            limit=62 if shared else 48,
        )
        got.append(swap(same if shared else cross, pieces))
    rise = [(i, i + g) for i in range(blocks - g)]
    fall = [(i + g, i) for i in range(blocks - g)]
    map_shapes = [shape(window, state_size, dtype=BF16)] * 2
    own_shapes = [
        shape(window, width, dtype=BF16),
        shape(window, width, dtype=BF16),
        shape(EXTRA, window),
        shape(8, width),
    ]
    state_shape = shape(state_size, width)
    near = [(i, i ^ g) for i in range(blocks)]
    middle = [(i, i ^ (3 * g) if i // g in (1, 2) else i) for i in range(blocks)]
    maps, sums, back = [], {}, {}
    own, weighted, ends, state, results = ({} for _ in range(5))

    def gather(n, after=()):
        outs = call(
            functools.partial(gather_kernel, dims, n == 0),
            own_shapes
            + (map_shapes if n == 0 else [])
            + [shape(window, width, dtype=BF16)] * 2
            + [state_shape] * 2
            + [shape(8, width)],
            got[n] + maps,
            [pltpu.VMEM((g, EXTRA, LANES), F32)],
            after=after,
        )
        own[n], outs = outs[:4], outs[4:]
        if n == 0:
            maps.extend(outs[:2])
            outs = outs[2:]
        weighted[n], ends[n] = outs[:2], outs[2:]

    def local(n, after=()):
        results[n] = call(
            functools.partial(local_kernel, dims),
            [shape(window, width)] * 2 + [shape(window, state_size)] * 2,
            own[n] + maps,
            after=after,
        )

    def hop(n, k, after=()):
        first, second, decay = ends[n]
        if k == 0:
            state[n] = [lax.ppermute(first, "seq", near)]
            return []
        moved = call(
            step_kernel, [state_shape], [decay, state[n][-1], second if k == 1 else first], after=after
        )
        state[n].append(lax.ppermute(moved[0], "seq", middle if k == 1 else near))
        return moved

    def chain(n):
        first, second, decay = ends[n]
        odd = lax.rem(lax.div(index, g), 2) == 1
        total = [jnp.where(odd, second, first), jnp.where(odd, first, second)]
        state[n] = [jnp.zeros_like(first)] * 2
        for k in range(windows - 1):
            moved = [decay[:1] * a + b for a, b in zip(state[n], total)]
            state[n] = [lax.ppermute(moved[0], "seq", rise), lax.ppermute(moved[1], "seq", fall)]

    def finish(n, half, after=()):
        if windows == 4:
            states = state[n][:1] if half == 0 else state[n][1:]
        else:
            states = state[n][half : half + 1]
        outs = call(
            functools.partial(half_kernel, dims, windows, half, n == 1),
            [shape((tiles + n) * rows, LANES)] * g + [shape(window, state_size)],
            [own[n][2]] + results[n] + (sums[half] if n else []) + maps + weighted[n] + states,
            [pltpu.VMEM((window, width), F32)],
            after=after,
        )
        sums[half] = outs[g:]
        back[n, half] = swap(cross if n else same, outs[:g])

    gather(0)
    if windows == 4:
        hop(0, 0)
        local(0)
        moved = hop(0, 1, after=results[0][:1])
        finish(0, 0, after=moved)
        gather(1, after=sums[0])
        hop(1, 0)
        moved = hop(0, 2, after=ends[1][:1])
        local(1, after=moved)
        moved = hop(1, 1, after=results[1][:1])
        finish(1, 0, after=moved)
        finish(0, 1, after=sums[0])
        hop(1, 2, after=sums[1])
        finish(1, 1)
    else:
        gather(1)
        for n in range(2):
            chain(n)
            local(n)
            finish(n, 0)
            finish(n, 1)
    part = rows // peers
    outs, slices = [], []
    for n, half in ((0, 0), (1, 0), (0, 1), (1, 1)):
        more = [shape(part, state_size)] * peers if n else []
        outs = call(
            functools.partial(unpack_kernel, dims, windows, half, n == 1),
            [shape(seqs, rows, wide, dtype=BF16)] * 2 + more,
            back[n, half] + outs,
            [pltpu.VMEM((rows, state_size), F32)] * n
            + [pltpu.VMEM((rows, wide), BF16), pltpu.SemaphoreType.DMA((4,))],
            far=(g, g + 1),
            far_out=(0, 1),
            aliases={g: 0, g + 1: 1} if outs else {},
        )
        outs, shares = outs[:2], outs[2:]
        if n:
            come = [lax.ppermute(shares[e], "head", [(c, c ^ e) for c in range(peers)]) for e in range(1, peers)]
            ours = functools.reduce(jnp.add, come[1::2], shares[0])
            theirs = functools.reduce(jnp.add, come[2::2], come[0])
            even = lax.rem(lax.axis_index("head"), 2) == 0
            slices.append((jnp.where(even, theirs, ours), jnp.where(even, ours, theirs)))
    mixed, grad_v = outs
    low = lax.div(index, g) < 2 if windows == 4 else True
    grad_bc = jnp.stack(
        [jnp.stack([pick(low, a, b) for a, b in zip(*order)]) for order in (slices[::-1], slices)]
    )
    return mixed, grad_v, grad_bc


def solution(mesh):
    in_specs = (
        P(None, "seq", "head"),
        P(None, "seq", None),
        P(None, "seq", None),
        P(None, "head", "seq"),
        P("head"),
        P(None, "seq", "head"),
    )
    out_specs = (
        P(None, "seq", "head"),
        P(None, "seq", "head"),
        P(None, None, ("seq", "head"), None),
    )
    return jax.shard_map(shards, mesh=mesh, in_specs=in_specs, out_specs=out_specs, check_vma=False)
```

time: 114 us -> 90.5 us (0.79)
  starting transfers between devices: 53.4 us -> 38.7 us
  waiting for transfers between devices: 40.3 us -> 35 us
  local copies, waits for them, and re-layouts: 2.93 us -> 0.03 us
    ppermute x33 -> x29, starting transfers between devices: 53.4 us -> 38.7 us  [the longest x9 11.7 us: same(): return lax.ppermute(piece, 'seq', [(i, i ^ d) for i in range(blocks)])]
    ppermute x33 -> x29, waiting for transfers between devices: 40.3 us -> 35 us  [the longest x9 23.5 us: same(): return lax.ppermute(piece, 'seq', [(i, i ^ d) for i in range(blocks)])]
    squeeze x3 -> x0, local copies, waits for them, and re-layouts: 2.03 us -> none  [the longest x1 1.28 us: shards(): cotangent[s]]
    pallas_call x7 -> x18, Pallas kernels: 15.8 us -> 15.1 us  [call(): pl.pallas_call(body, out_shape=out, in_specs=[hbm if n in far else vmem f...]
  transfers between devices with their start and end apart: 33 -> 29, of which waited for: 13 -> 13; matrix products, arithmetic and copies ran while one was open for 0% -> 0% of each run, Pallas kernels for 12% -> 14%
where the time goes in v2:
time: 90.5 us; the launch traced here: 90.3 us
  starting transfers between devices  38.7 us (43%)
  waiting for transfers between devices  35 us (39%)
  Pallas kernels  15.1 us (17%)
  between operations  0.93 us (1%)
    ppermute x9, waiting for transfers between devices, same(): return lax.ppermute(piece, 'seq', [(i, i ^ d) for i in range(blocks)])  23.5 us
    pallas_call x18, Pallas kernels, call(): pl.pallas_call(body, out_shape=out, in_specs=[hbm if n in far else vmem f...  15.1 us
    ppermute x9, starting transfers between devices, same(): return lax.ppermute(piece, 'seq', [(i, i ^ d) for i in range(blocks)])  11.7 us
    ppermute x4, starting transfers between devices, hop(): state[n].append(lax.ppermute(moved[0], 'seq', middle if k == 1 else near))  10.6 us
    ppermute x12, starting transfers between devices, cross(): return lax.ppermute(piece, ('seq', 'head'), perm)  8.97 us
    ppermute x2, starting transfers between devices, hop(): state[n] = [lax.ppermute(first, 'seq', near)]  6.86 us
    ppermute x2, waiting for transfers between devices, hop(): state[n] = [lax.ppermute(first, 'seq', near)]  5.8 us
    ppermute x12, waiting for transfers between devices, cross(): return lax.ppermute(piece, ('seq', 'head'), perm)  3.37 us
  transfers between devices with their start and end apart: 29, of which 13 were waited for; matrix products, arithmetic and copies ran while one was open for 0% of the time, Pallas kernels for 14%

profile of v2, /device:TPU:0, one launch (start us, length us, event | category | flops | bytes accessed | tf_op | source)
XLA Modules:
  0.0 90.3 jit_solution(14778467754854663756)
XLA Ops:
  0.7 2.5 %shard_map.85 = (f32[648,128]{1,0:T(8,128)}, f32[648,128]{1,0:T(8,128)}, f32[648,128]{1,0:T(8,128)}, f32[648,128]{1,0:T(8,128)}) custom-call(bf16[2,64,2048]{2,1,0:T(8,128)(2,1)} %refs_0_.3, bf16[2,64,2048]{2,1,0:T(8,128)(2,1)} %refs_1_.3, bf16[2,64,128]{2,1,0:T(8,128)(2,1)} %refs_2_.3, bf16[2,64,128]{2,1,0:T(8,128)(2,1)} %refs_3_.3, f32[2,32,64]{2,1,0:T(8,128)} %refs_4_.3, ...), custom_call_target="tpu_custom_call" | custom-call | tf_op jit(solution)/shard_map/pallas_call | solution.py:335
  3.2 3.0 %collective-permute-start = (f32[648,128]{1,0:T(8,128)}, f32[648,128]{1,0:T(8,128)S(1)}, u32[]{:S(2)}, u32[]{:S(2)}) collective-permute-start(f32[648,128]{1,0:T(8,128)} %get-tuple-element.70), channel_id=1, source_target_pairs={{0,4},{2,6},{4,0},{6,2},{8,12},{10,14},{12,8},{14,10},{16,20},{18,... | collective-permute-start | bytes 995336 | tf_op jit(solution)/shard_map/ppermute | solution.py:316
  6.3 1.5 %collective-permute-start.5 = (f32[648,128]{1,0:T(8,128)}, f32[648,128]{1,0:T(8,128)S(1)}, u32[]{:S(2)}, u32[]{:S(2)}) collective-permute-start(f32[648,128]{1,0:T(8,128)} %get-tuple-element.76), channel_id=1, source_target_pairs={{0,2},{2,0},{4,6},{6,4},{8,10},{10,8},{12,14},{14,12},{16,18},{18,... | collective-permute-start | bytes 995336 | tf_op jit(solution)/shard_map/ppermute | solution.py:316
  7.8 6.5 %collective-permute-done.refs_6_.refs_1_ = f32[648,128]{1,0:T(8,128)S(1)} collective-permute-done((f32[648,128]{1,0:T(8,128)}, f32[648,128]{1,0:T(8,128)S(1)}, u32[]{:S(2)}, u32[]{:S(2)}) %collective-permute-start) | collective-permute-done | bytes 331808 | tf_op jit(solution)/shard_map/ppermute | solution.py:316
  14.3 0.4 shard_map.86
  14.8 2.1 %collective-permute-start.2 = (f32[520,128]{1,0:T(8,128)S(1)}, f32[520,128]{1,0:T(8,128)S(1)}, u32[]{:S(2)}, u32[]{:S(2)}) collective-permute-start(f32[520,128]{1,0:T(8,128)S(1)} %get-tuple-element.72), channel_id=1, source_target_pairs={{0,5},{1,4},{2,7},{3,6},{4,1},{5,0},{6,3},{7,2},{8,13},{9,12},{10,... | collective-permute-start | bytes 798728 | tf_op jit(solution)/shard_map/ppermute | solution.py:322
  16.9 1.2 %collective-permute-start.3 = (f32[520,128]{1,0:T(8,128)S(1)}, f32[520,128]{1,0:T(8,128)S(1)}, u32[]{:S(2)}, u32[]{:S(2)}) collective-permute-start(f32[520,128]{1,0:T(8,128)S(1)} %get-tuple-element.73), channel_id=1, source_target_pairs={{0,3},{1,2},{2,1},{3,0},{4,7},{5,6},{6,5},{7,4},{8,11},{9,10},{10,... | collective-permute-start | bytes 798728 | tf_op jit(solution)/shard_map/ppermute | solution.py:322
  18.1 5.7 %collective-permute-done.6.refs_3_ = f32[648,128]{1,0:T(8,128)S(1)} collective-permute-done((f32[648,128]{1,0:T(8,128)}, f32[648,128]{1,0:T(8,128)S(1)}, u32[]{:S(2)}, u32[]{:S(2)}) %collective-permute-start.6) | collective-permute-done | bytes 331808 | tf_op jit(solution)/shard_map/ppermute | solution.py:316
  23.8 1.4 %shard_map.87 = (bf16[256,512]{1,0:T(8,128)(2,1)S(1)}, bf16[256,512]{1,0:T(8,128)(2,1)S(1)}, f32[8,256]{1,0:T(8,128)S(1)}, f32[8,512]{1,0:T(8,128)S(1)}, bf16[25...) custom-call(f32[648,128]{1,0:T(8,128)S(1)} %copy-done.2, ...), custom_call_target="tpu_custom_call" | custom-call | tf_op jit(solution)/shard_map/pallas_call | solution.py:335
  25.3 2.1 %collective-permute-start.7 = (f32[128,512]{1,0:T(8,128)S(1)}, f32[128,512]{1,0:T(8,128)S(1)}, u32[]{:S(2)}, u32[]{:S(2)}) collective-permute-start(f32[128,512]{1,0:T(8,128)S(1)} %get-tuple-element.90.refs_2_), channel_id=1, source_target_pairs={{0,8},{2,10},{4,12},{6,14},{8,0},{10,2},{12,4},{14,6},{16,24},{18,... | collective-permute-start | bytes 786440 | tf_op jit(solution)/shard_map/ppermute | solution.py:411
  27.4 1.4 %shard_map.88 = (f32[256,512]{1,0:T(8,128)S(1)}, f32[256,512]{1,0:T(8,128)S(1)}, f32[256,128]{1,0:T(8,128)S(1)}, f32[256,128]{1,0:T(8,128)S(1)}) custom-call(bf16[256,512]{1,0:T(8,128)(2,1)S(1)} %get-tuple-element.81.refs_0_, bf16[256,512]{1,0:T(8,128)(2,1)S(1)} %get-tuple-element.82.refs_1_, f32[8,256]{1,0:T(8,128)S(1)} %get-tuple-element.80.refs_2_.refs_0_, ...), custom_call_target="tpu_custom_call" | custom-call | tf_op jit(solution)/shard_map/pallas_call | solution.py:335
  28.8 2.9 %collective-permute-done.7.refs_1_.refs_9_ = f32[128,512]{1,0:T(8,128)S(1)} collective-permute-done((f32[128,512]{1,0:T(8,128)S(1)}, f32[128,512]{1,0:T(8,128)S(1)}, u32[]{:S(2)}, u32[]{:S(2)}) %collective-permute-start.7) | collective-permute-done | bytes 262176 | tf_op jit(solution)/shard_map/ppermute | solution.py:411
  31.8 0.7 collective-permute-start.8
  32.5 0.7 shard_map.90
  33.3 1.4 %shard_map.91 = (bf16[256,512]{1,0:T(8,128)(2,1)S(1)}, bf16[256,512]{1,0:T(8,128)(2,1)S(1)}, f32[8,256]{1,0:T(8,128)S(1)}, f32[8,512]{1,0:T(8,128)S(1)}, bf16[25...) custom-call(f32[520,128]{1,0:T(8,128)S(1)} %collective-permute-done., ...), custom_call_target="tpu_custom_call" | custom-call | tf_op jit(solution)/shard_map/pallas_call | solution.py:335
  34.7 4.8 %collective-permute-start.10 = (f32[128,512]{1,0:T(8,128)S(1)}, f32[128,512]{1,0:T(8,128)S(1)}, u32[]{:S(2)}, u32[]{:S(2)}) collective-permute-start(f32[128,512]{1,0:T(8,128)S(1)} %get-tuple-element.98.refs_3_.refs_2_), channel_id=1, source_target_pairs={{0,8},{2,10},{4,12},{6,14},{8,0},{10,2},{12,4},{14,6},{16,24},{18,... | collective-permute-start | bytes 786440 | tf_op jit(solution)/shard_map/ppermute | solution.py:411
  39.5 2.6 %collective-permute-start.9 = (f32[128,512]{1,0:T(8,128)S(1)}, f32[128,512]{1,0:T(8,128)S(1)}, u32[]{:S(2)}, u32[]{:S(2)}) collective-permute-start(f32[128,512]{1,0:T(8,128)S(1)} %shard_map.92.refs_6_), channel_id=1, source_target_pairs={{0,8},{2,10},{4,12},{6,14},{8,0},{10,2},{12,4},{14,6},{16,24},{18,... | collective-permute-start | bytes 786440 | tf_op jit(solution)/shard_map/ppermute | solution.py:416
  42.2 1.4 %shard_map.93 = (f32[256,512]{1,0:T(8,128)S(1)}, f32[256,512]{1,0:T(8,128)S(1)}, f32[256,128]{1,0:T(8,128)S(1)}, f32[256,128]{1,0:T(8,128)S(1)}) custom-call(bf16[256,512]{1,0:T(8,128)(2,1)S(1)} %get-tuple-element.95.refs_0_, bf16[256,512]{1,0:T(8,128)(2,1)S(1)} %get-tuple-element.96.refs_1_, f32[8,256]{1,0:T(8,128)S(1)} %get-tuple-element.94.refs_2_.refs_0_, ...), custom_call_target="tpu_custom_call" | custom-call | tf_op jit(solution)/shard_map/pallas_call | solution.py:335
  43.6 2.9 %collective-permute-done.10.refs_1_.refs_10_ = f32[128,512]{1,0:T(8,128)S(1)} collective-permute-done((f32[128,512]{1,0:T(8,128)S(1)}, f32[128,512]{1,0:T(8,128)S(1)}, u32[]{:S(2)}, u32[]{:S(2)}) %collective-permute-start.10) | collective-permute-done | bytes 262176 | tf_op jit(solution)/shard_map/ppermute | solution.py:411
  46.5 0.7 collective-permute-start.11
  47.1 0.7 shard_map.95
  47.8 1.4 %collective-permute-done.9.refs_10_ = f32[128,512]{1,0:T(8,128)S(1)} collective-permute-done((f32[128,512]{1,0:T(8,128)S(1)}, f32[128,512]{1,0:T(8,128)S(1)}, u32[]{:S(2)}, u32[]{:S(2)}) %collective-permute-start.9) | collective-permute-done | bytes 262176 | tf_op jit(solution)/shard_map/ppermute | solution.py:416
  49.2 0.7 shard_map.96
  50.0 6.6 %collective-permute-start.12 = (f32[128,512]{1,0:T(8,128)S(1)}, f32[128,512]{1,0:T(8,128)S(1)}, u32[]{:S(2)}, u32[]{:S(2)}) collective-permute-start(f32[128,512]{1,0:T(8,128)S(1)} %shard_map.97), channel_id=1, source_target_pairs={{0,8},{2,10},{4,12},{6,14},{8,0},{10,2},{12,4},{14,6},{16,24},{18,... | collective-permute-start | bytes 786440 | tf_op jit(solution)/shard_map/ppermute | solution.py:416
  56.5 1.5 %collective-permute-start.24 = (f32[256,128]{1,0:T(8,128)S(1)}, f32[256,128]{1,0:T(8,128)S(1)}, u32[]{:S(2)}, u32[]{:S(2)}) collective-permute-start(f32[256,128]{1,0:T(8,128)S(1)} %get-tuple-element.122), channel_id=1, source_target_pairs={{0,4},{2,6},{4,0},{6,2},{8,12},{10,14},{12,8},{14,10},{16,20},{18,... | collective-permute-start | bytes 393224 | tf_op jit(solution)/shard_map/ppermute | solution.py:316
  58.1 1.5 %collective-permute-start.25 = (f32[256,128]{1,0:T(8,128)S(1)}, f32[256,128]{1,0:T(8,128)S(1)}, u32[]{:S(2)}, u32[]{:S(2)}) collective-permute-start(f32[256,128]{1,0:T(8,128)S(1)} %get-tuple-element.123), channel_id=1, source_target_pairs={{0,2},{2,0},{4,6},{6,4},{8,10},{10,8},{12,14},{14,12},{16,18},{18,... | collective-permute-start | bytes 393224 | tf_op jit(solution)/shard_map/ppermute | solution.py:316
  59.6 0.5 collective-permute-start.26
  60.0 1.5 %collective-permute-done.24.refs_1_ = f32[256,128]{1,0:T(8,128)S(1)} collective-permute-done((f32[256,128]{1,0:T(8,128)S(1)}, f32[256,128]{1,0:T(8,128)S(1)}, u32[]{:S(2)}, u32[]{:S(2)}) %collective-permute-start.24) | collective-permute-done | bytes 131104 | tf_op jit(solution)/shard_map/ppermute | solution.py:316
  61.7 1.4 %collective-permute-done.25.refs_2_ = f32[256,128]{1,0:T(8,128)S(1)} collective-permute-done((f32[256,128]{1,0:T(8,128)S(1)}, f32[256,128]{1,0:T(8,128)S(1)}, u32[]{:S(2)}, u32[]{:S(2)}) %collective-permute-start.25) | collective-permute-done | bytes 131104 | tf_op jit(solution)/shard_map/ppermute | solution.py:316
  63.0 1.2 %collective-permute-start.22 = (f32[320,128]{1,0:T(8,128)S(1)}, f32[320,128]{1,0:T(8,128)S(1)}, u32[]{:S(2)}, u32[]{:S(2)}) collective-permute-start(f32[320,128]{1,0:T(8,128)S(1)} %get-tuple-element.119), channel_id=1, source_target_pairs={{0,3},{1,2},{2,1},{3,0},{4,7},{5,6},{6,5},{7,4},{8,11},{9,10},{10,... | collective-permute-start | bytes 491528 | tf_op jit(solution)/shard_map/ppermute | solution.py:322
  64.3 1.3 %collective-permute-done.26.refs_3_ = f32[256,128]{1,0:T(8,128)S(1)} collective-permute-done((f32[256,128]{1,0:T(8,128)S(1)}, f32[256,128]{1,0:T(8,128)S(1)}, u32[]{:S(2)}, u32[]{:S(2)}) %collective-permute-start.26) | collective-permute-done | bytes 131104 | tf_op jit(solution)/shard_map/ppermute | solution.py:316
  65.5 0.7 collective-permute-start.17
  66.3 1.5 %collective-permute-start.18 = (f32[256,128]{1,0:T(8,128)S(1)}, f32[256,128]{1,0:T(8,128)S(1)}, u32[]{:S(2)}, u32[]{:S(2)}) collective-permute-start(f32[256,128]{1,0:T(8,128)S(1)} %get-tuple-element.115), channel_id=1, source_target_pairs={{0,2},{2,0},{4,6},{6,4},{8,10},{10,8},{12,14},{14,12},{16,18},{18,... | collective-permute-start | bytes 393224 | tf_op jit(solution)/shard_map/ppermute | solution.py:316
  67.8 1.2 %shard_map.98 = (f32[320,128]{1,0:T(8,128)S(1)}, f32[320,128]{1,0:T(8,128)S(1)}, f32[320,128]{1,0:T(8,128)S(1)}, f32[320,128]{1,0:T(8,128)S(1)}, f32[256,128]{1,0:T(8,128)}) custom-call(f32[8,256]{1,0:T(8,128)S(1)} %get-tuple-element.94.refs_2_.refs_0_, f32[256,512]{1,0:T(8,128)S(1)} %get-tuple-element.99.refs_3_.refs_1_, ...), custom_call_target="tpu_custom_call" | custom-call | tf_op jit(solution)/shard_map/pallas_call | solution.py:335
  68.9 0.8 collective-permute-start.13
  69.9 3.2 %collective-permute-done.23.refs_3_ = f32[320,128]{1,0:T(8,128)S(1)} collective-permute-done((f32[320,128]{1,0:T(8,128)S(1)}, f32[320,128]{1,0:T(8,128)S(1)}, u32[]{:S(2)}, u32[]{:S(2)}) %collective-permute-start.23) | collective-permute-done | bytes 163872 | tf_op jit(solution)/shard_map/ppermute | solution.py:322
  73.1 1.2 %collective-permute-start.15 = (f32[320,128]{1,0:T(8,128)S(1)}, f32[320,128]{1,0:T(8,128)S(1)}, u32[]{:S(2)}, u32[]{:S(2)}) collective-permute-start(f32[320,128]{1,0:T(8,128)S(1)} %get-tuple-element.111), channel_id=1, source_target_pairs={{0,3},{1,2},{2,1},{3,0},{4,7},{5,6},{6,5},{7,4},{8,11},{9,10},{10,... | collective-permute-start | bytes 491528 | tf_op jit(solution)/shard_map/ppermute | solution.py:322
  74.2 0.8 collective-permute-done.17.refs_1_
  75.0 2.0 %collective-permute-start.16 = (f32[320,128]{1,0:T(8,128)S(1)}, f32[320,128]{1,0:T(8,128)S(1)}, u32[]{:S(2)}, u32[]{:S(2)}) collective-permute-start(f32[320,128]{1,0:T(8,128)S(1)} %get-tuple-element.112), channel_id=1, source_target_pairs={{0,7},{1,6},{2,5},{3,4},{4,3},{5,2},{6,1},{7,0},{8,15},{9,14},{10,... | collective-permute-start | bytes 491528 | tf_op jit(solution)/shard_map/ppermute | solution.py:322
  77.1 1.4 %collective-permute-start.19 = (f32[256,128]{1,0:T(8,128)S(1)}, f32[256,128]{1,0:T(8,128)S(1)}, u32[]{:S(2)}, u32[]{:S(2)}) collective-permute-start(f32[256,128]{1,0:T(8,128)S(1)} %get-tuple-element.116), channel_id=1, source_target_pairs={{0,6},{2,4},{4,2},{6,0},{8,14},{10,12},{12,10},{14,8},{16,22},{18,... | collective-permute-start | bytes 393224 | tf_op jit(solution)/shard_map/ppermute | solution.py:316
  78.5 0.8 shard_map.99
  79.3 0.8 shard_map.100
  80.1 6.5 %collective-permute-done.19.refs_3_ = f32[256,128]{1,0:T(8,128)S(1)} collective-permute-done((f32[256,128]{1,0:T(8,128)S(1)}, f32[256,128]{1,0:T(8,128)S(1)}, u32[]{:S(2)}, u32[]{:S(2)}) %collective-permute-start.19) | collective-permute-done | bytes 131104 | tf_op jit(solution)/shard_map/ppermute | solution.py:316
  86.6 0.8 shard_map.101
  87.4 0.8 shard_map.102
  88.2 0.6 collective-permute-start.27
  88.8 0.8 collective-permute-done.27
  89.7 0.6 pad_maximum_fusion
  (45 shorter events, 0.9 us)
Async XLA Ops:
  0.6 13.6 %copy-start = (bf16[2,64,2048]{2,1,0:T(8,128)(2,1)S(1)}, bf16[2,64,2048]{2,1,0:T(8,128)(2,1)}, u32[]{:S(2)}) copy-start(bf16[2,64,2048]{2,1,0:T(8,128)(2,1)} %refs_0_.3) | copy-start | bytes 1572868
  0.6 13.6 %copy-start.1 = (bf16[2,64,2048]{2,1,0:T(8,128)(2,1)S(1)}, bf16[2,64,2048]{2,1,0:T(8,128)(2,1)}, u32[]{:S(2)}) copy-start(bf16[2,64,2048]{2,1,0:T(8,128)(2,1)} %refs_1_.3) | copy-start | bytes 1572868
  0.7 13.6 %copy-start.3 = (bf16[2,64,128]{2,1,0:T(8,128)(2,1)S(1)}, bf16[2,64,128]{2,1,0:T(8,128)(2,1)}, u32[]{:S(2)}) copy-start(bf16[2,64,128]{2,1,0:T(8,128)(2,1)} %refs_2_.3) | copy-start | bytes 98308
  0.7 13.6 %copy-start.4 = (bf16[2,64,128]{2,1,0:T(8,128)(2,1)S(1)}, bf16[2,64,128]{2,1,0:T(8,128)(2,1)}, u32[]{:S(2)}) copy-start(bf16[2,64,128]{2,1,0:T(8,128)(2,1)} %refs_3_.3) | copy-start | bytes 98308
  0.7 13.6 %copy-start.5 = (f32[2,32,64]{2,1,0:T(8,128)S(1)}, f32[2,32,64]{2,1,0:T(8,128)}, u32[]{:S(2)}) copy-start(f32[2,32,64]{2,1,0:T(8,128)} %refs_4_.3) | copy-start | bytes 49156
  3.2 11.0 %collective-permute-start = (f32[648,128]{1,0:T(8,128)}, f32[648,128]{1,0:T(8,128)S(1)}, u32[]{:S(2)}, u32[]{:S(2)}) collective-permute-start(f32[648,128]{1,0:T(8,128)} %get-tuple-element.70), channel_id=1, source_target_pairs={{0,4},{2,6},{4,0},{6,2},{8,12},{10,14},{12,8},{14,10},{16,20},{18,... | collective-permute-start | bytes 995336 | tf_op jit(solution)/shard_map/ppermute | solution.py:316
  6.3 8.0 %copy-start.6 = (f32[32]{0:T(128)S(1)}, f32[32]{0:T(128)}, u32[]{:S(2)}) copy-start(f32[32]{0:T(128)} %param.10) | copy-start | bytes 388
  6.3 11.8 %collective-permute-start.5 = (f32[648,128]{1,0:T(8,128)}, f32[648,128]{1,0:T(8,128)S(1)}, u32[]{:S(2)}, u32[]{:S(2)}) collective-permute-start(f32[648,128]{1,0:T(8,128)} %get-tuple-element.76), channel_id=1, source_target_pairs={{0,2},{2,0},{4,6},{6,4},{8,10},{10,8},{12,14},{14,12},{16,18},{18,... | collective-permute-start | bytes 995336 | tf_op jit(solution)/shard_map/ppermute | solution.py:316
  7.8 16.1 %copy-start.2 = (f32[648,128]{1,0:T(8,128)S(1)}, f32[648,128]{1,0:T(8,128)}, u32[]{:S(2)}) copy-start(f32[648,128]{1,0:T(8,128)} %get-tuple-element.75.refs_0_) | copy-start | bytes 995332
  7.8 16.1 %collective-permute-start.6 = (f32[648,128]{1,0:T(8,128)}, f32[648,128]{1,0:T(8,128)S(1)}, u32[]{:S(2)}, u32[]{:S(2)}) collective-permute-start(f32[648,128]{1,0:T(8,128)} %get-tuple-element.77), channel_id=1, source_target_pairs={{0,6},{2,4},{4,2},{6,0},{8,14},{10,12},{12,10},{14,8},{16,22},{18,... | collective-permute-start | bytes 995336 | tf_op jit(solution)/shard_map/ppermute | solution.py:316
  14.7 18.4 %collective-permute-start.1 = (f32[520,128]{1,0:T(8,128)S(1)}, f32[520,128]{1,0:T(8,128)S(1)}, u32[]{:S(2)}, u32[]{:S(2)}) collective-permute-start(f32[520,128]{1,0:T(8,128)S(1)} %get-tuple-element.71), channel_id=1, source_target_pairs={{0,1},{1,0},{2,3},{3,2},{4,5},{5,4},{6,7},{7,6},{8,9},{9,8},{10,11... | collective-permute-start | bytes 798728 | tf_op jit(solution)/shard_map/ppermute | solution.py:322
  14.8 18.3 %collective-permute-start.2 = (f32[520,128]{1,0:T(8,128)S(1)}, f32[520,128]{1,0:T(8,128)S(1)}, u32[]{:S(2)}, u32[]{:S(2)}) collective-permute-start(f32[520,128]{1,0:T(8,128)S(1)} %get-tuple-element.72), channel_id=1, source_target_pairs={{0,5},{1,4},{2,7},{3,6},{4,1},{5,0},{6,3},{7,2},{8,13},{9,12},{10,... | collective-permute-start | bytes 798728 | tf_op jit(solution)/shard_map/ppermute | solution.py:322
  16.9 16.2 %collective-permute-start.3 = (f32[520,128]{1,0:T(8,128)S(1)}, f32[520,128]{1,0:T(8,128)S(1)}, u32[]{:S(2)}, u32[]{:S(2)}) collective-permute-start(f32[520,128]{1,0:T(8,128)S(1)} %get-tuple-element.73), channel_id=1, source_target_pairs={{0,3},{1,2},{2,1},{3,0},{4,7},{5,6},{6,5},{7,4},{8,11},{9,10},{10,... | collective-permute-start | bytes 798728 | tf_op jit(solution)/shard_map/ppermute | solution.py:322
  18.1 15.2 %collective-permute-start.4 = (f32[520,128]{1,0:T(8,128)S(1)}, f32[520,128]{1,0:T(8,128)S(1)}, u32[]{:S(2)}, u32[]{:S(2)}) collective-permute-start(f32[520,128]{1,0:T(8,128)S(1)} %get-tuple-element.74), channel_id=1, source_target_pairs={{0,7},{1,6},{2,5},{3,4},{4,3},{5,2},{6,1},{7,0},{8,15},{9,14},{10,... | collective-permute-start | bytes 798728 | tf_op jit(solution)/shard_map/ppermute | solution.py:322
  25.3 6.4 %collective-permute-start.7 = (f32[128,512]{1,0:T(8,128)S(1)}, f32[128,512]{1,0:T(8,128)S(1)}, u32[]{:S(2)}, u32[]{:S(2)}) collective-permute-start(f32[128,512]{1,0:T(8,128)S(1)} %get-tuple-element.90.refs_2_), channel_id=1, source_target_pairs={{0,8},{2,10},{4,12},{6,14},{8,0},{10,2},{12,4},{14,6},{16,24},{18,... | collective-permute-start | bytes 786440 | tf_op jit(solution)/shard_map/ppermute | solution.py:411
  31.8 7.7 %collective-permute-start.8 = (f32[128,512]{1,0:T(8,128)S(1)}, f32[128,512]{1,0:T(8,128)S(1)}, u32[]{:S(2)}, u32[]{:S(2)}) collective-permute-start(f32[128,512]{1,0:T(8,128)S(1)} %shard_map.89.refs_10_), channel_id=1, source_target_pairs={{0,0},{2,2},{4,4},{6,6},{8,16},{10,18},{12,20},{14,22},{16,8},{18,... | collective-permute-start | bytes 786440 | tf_op jit(solution)/shard_map/ppermute | solution.py:416
  34.7 11.7 %collective-permute-start.10 = (f32[128,512]{1,0:T(8,128)S(1)}, f32[128,512]{1,0:T(8,128)S(1)}, u32[]{:S(2)}, u32[]{:S(2)}) collective-permute-start(f32[128,512]{1,0:T(8,128)S(1)} %get-tuple-element.98.refs_3_.refs_2_), channel_id=1, source_target_pairs={{0,8},{2,10},{4,12},{6,14},{8,0},{10,2},{12,4},{14,6},{16,24},{18,... | collective-permute-start | bytes 786440 | tf_op jit(solution)/shard_map/ppermute | solution.py:411
  39.5 9.7 %collective-permute-start.9 = (f32[128,512]{1,0:T(8,128)S(1)}, f32[128,512]{1,0:T(8,128)S(1)}, u32[]{:S(2)}, u32[]{:S(2)}) collective-permute-start(f32[128,512]{1,0:T(8,128)S(1)} %shard_map.92.refs_6_), channel_id=1, source_target_pairs={{0,8},{2,10},{4,12},{6,14},{8,0},{10,2},{12,4},{14,6},{16,24},{18,... | collective-permute-start | bytes 786440 | tf_op jit(solution)/shard_map/ppermute | solution.py:416
  46.5 3.4 %collective-permute-start.11 = (f32[128,512]{1,0:T(8,128)S(1)}, f32[128,512]{1,0:T(8,128)S(1)}, u32[]{:S(2)}, u32[]{:S(2)}) collective-permute-start(f32[128,512]{1,0:T(8,128)S(1)} %shard_map.94.refs_11_), channel_id=1, source_target_pairs={{0,0},{2,2},{4,4},{6,6},{8,16},{10,18},{12,20},{14,22},{16,8},{18,... | collective-permute-start | bytes 786440 | tf_op jit(solution)/shard_map/ppermute | solution.py:416
  50.0 16.3 %collective-permute-start.12 = (f32[128,512]{1,0:T(8,128)S(1)}, f32[128,512]{1,0:T(8,128)S(1)}, u32[]{:S(2)}, u32[]{:S(2)}) collective-permute-start(f32[128,512]{1,0:T(8,128)S(1)} %shard_map.97), channel_id=1, source_target_pairs={{0,8},{2,10},{4,12},{6,14},{8,0},{10,2},{12,4},{14,6},{16,24},{18,... | collective-permute-start | bytes 786440 | tf_op jit(solution)/shard_map/ppermute | solution.py:416
  56.5 5.0 %collective-permute-start.24 = (f32[256,128]{1,0:T(8,128)S(1)}, f32[256,128]{1,0:T(8,128)S(1)}, u32[]{:S(2)}, u32[]{:S(2)}) collective-permute-start(f32[256,128]{1,0:T(8,128)S(1)} %get-tuple-element.122), channel_id=1, source_target_pairs={{0,4},{2,6},{4,0},{6,2},{8,12},{10,14},{12,8},{14,10},{16,20},{18,... | collective-permute-start | bytes 393224 | tf_op jit(solution)/shard_map/ppermute | solution.py:316
  58.1 5.0 %collective-permute-start.25 = (f32[256,128]{1,0:T(8,128)S(1)}, f32[256,128]{1,0:T(8,128)S(1)}, u32[]{:S(2)}, u32[]{:S(2)}) collective-permute-start(f32[256,128]{1,0:T(8,128)S(1)} %get-tuple-element.123), channel_id=1, source_target_pairs={{0,2},{2,0},{4,6},{6,4},{8,10},{10,8},{12,14},{14,12},{16,18},{18,... | collective-permute-start | bytes 393224 | tf_op jit(solution)/shard_map/ppermute | solution.py:316
  59.6 6.0 %collective-permute-start.26 = (f32[256,128]{1,0:T(8,128)S(1)}, f32[256,128]{1,0:T(8,128)S(1)}, u32[]{:S(2)}, u32[]{:S(2)}) collective-permute-start(f32[256,128]{1,0:T(8,128)S(1)} %get-tuple-element.124), channel_id=1, source_target_pairs={{0,6},{2,4},{4,2},{6,0},{8,14},{10,12},{12,10},{14,8},{16,22},{18,... | collective-permute-start | bytes 393224 | tf_op jit(solution)/shard_map/ppermute | solution.py:316
  60.0 5.5 %collective-permute-start.20 = (f32[320,128]{1,0:T(8,128)S(1)}, f32[320,128]{1,0:T(8,128)S(1)}, u32[]{:S(2)}, u32[]{:S(2)}) collective-permute-start(f32[320,128]{1,0:T(8,128)S(1)} %get-tuple-element.117), channel_id=1, source_target_pairs={{0,1},{1,0},{2,3},{3,2},{4,5},{5,4},{6,7},{7,6},{8,9},{9,8},{10,11... | collective-permute-start | bytes 491528 | tf_op jit(solution)/shard_map/ppermute | solution.py:322
  61.5 7.4 %collective-permute-start.21 = (f32[320,128]{1,0:T(8,128)S(1)}, f32[320,128]{1,0:T(8,128)S(1)}, u32[]{:S(2)}, u32[]{:S(2)}) collective-permute-start(f32[320,128]{1,0:T(8,128)S(1)} %get-tuple-element.118), channel_id=1, source_target_pairs={{0,5},{1,4},{2,7},{3,6},{4,1},{5,0},{6,3},{7,2},{8,13},{9,12},{10,... | collective-permute-start | bytes 491528 | tf_op jit(solution)/shard_map/ppermute | solution.py:322
  63.0 6.7 %collective-permute-start.22 = (f32[320,128]{1,0:T(8,128)S(1)}, f32[320,128]{1,0:T(8,128)S(1)}, u32[]{:S(2)}, u32[]{:S(2)}) collective-permute-start(f32[320,128]{1,0:T(8,128)S(1)} %get-tuple-element.119), channel_id=1, source_target_pairs={{0,3},{1,2},{2,1},{3,0},{4,7},{5,6},{6,5},{7,4},{8,11},{9,10},{10,... | collective-permute-start | bytes 491528 | tf_op jit(solution)/shard_map/ppermute | solution.py:322
  65.5 7.6 %collective-permute-start.23 = (f32[320,128]{1,0:T(8,128)S(1)}, f32[320,128]{1,0:T(8,128)S(1)}, u32[]{:S(2)}, u32[]{:S(2)}) collective-permute-start(f32[320,128]{1,0:T(8,128)S(1)} %get-tuple-element.120), channel_id=1, source_target_pairs={{0,7},{1,6},{2,5},{3,4},{4,3},{5,2},{6,1},{7,0},{8,15},{9,14},{10,... | collective-permute-start | bytes 491528 | tf_op jit(solution)/shard_map/ppermute | solution.py:322
  65.5 9.5 %collective-permute-start.17 = (f32[256,128]{1,0:T(8,128)S(1)}, f32[256,128]{1,0:T(8,128)S(1)}, u32[]{:S(2)}, u32[]{:S(2)}) collective-permute-start(f32[256,128]{1,0:T(8,128)S(1)} %get-tuple-element.114), channel_id=1, source_target_pairs={{0,4},{2,6},{4,0},{6,2},{8,12},{10,14},{12,8},{14,10},{16,20},{18,... | collective-permute-start | bytes 393224 | tf_op jit(solution)/shard_map/ppermute | solution.py:316
  66.3 10.8 %collective-permute-start.18 = (f32[256,128]{1,0:T(8,128)S(1)}, f32[256,128]{1,0:T(8,128)S(1)}, u32[]{:S(2)}, u32[]{:S(2)}) collective-permute-start(f32[256,128]{1,0:T(8,128)S(1)} %get-tuple-element.115), channel_id=1, source_target_pairs={{0,2},{2,0},{4,6},{6,4},{8,10},{10,8},{12,14},{14,12},{16,18},{18,... | collective-permute-start | bytes 393224 | tf_op jit(solution)/shard_map/ppermute | solution.py:316
  68.9 18.5 %collective-permute-start.13 = (f32[320,128]{1,0:T(8,128)S(1)}, f32[320,128]{1,0:T(8,128)S(1)}, u32[]{:S(2)}, u32[]{:S(2)}) collective-permute-start(f32[320,128]{1,0:T(8,128)S(1)} %get-tuple-element.109), channel_id=1, source_target_pairs={{0,1},{1,0},{2,3},{3,2},{4,5},{5,4},{6,7},{7,6},{8,9},{9,8},{10,11... | collective-permute-start | bytes 491528 | tf_op jit(solution)/shard_map/ppermute | solution.py:322
  69.8 17.6 %collective-permute-start.14 = (f32[320,128]{1,0:T(8,128)S(1)}, f32[320,128]{1,0:T(8,128)S(1)}, u32[]{:S(2)}, u32[]{:S(2)}) collective-permute-start(f32[320,128]{1,0:T(8,128)S(1)} %get-tuple-element.110), channel_id=1, source_target_pairs={{0,5},{1,4},{2,7},{3,6},{4,1},{5,0},{6,3},{7,2},{8,13},{9,12},{10,... | collective-permute-start | bytes 491528 | tf_op jit(solution)/shard_map/ppermute | solution.py:322
  73.1 14.3 %collective-permute-start.15 = (f32[320,128]{1,0:T(8,128)S(1)}, f32[320,128]{1,0:T(8,128)S(1)}, u32[]{:S(2)}, u32[]{:S(2)}) collective-permute-start(f32[320,128]{1,0:T(8,128)S(1)} %get-tuple-element.111), channel_id=1, source_target_pairs={{0,3},{1,2},{2,1},{3,0},{4,7},{5,6},{6,5},{7,4},{8,11},{9,10},{10,... | collective-permute-start | bytes 491528 | tf_op jit(solution)/shard_map/ppermute | solution.py:322
  75.0 12.4 %collective-permute-start.16 = (f32[320,128]{1,0:T(8,128)S(1)}, f32[320,128]{1,0:T(8,128)S(1)}, u32[]{:S(2)}, u32[]{:S(2)}) collective-permute-start(f32[320,128]{1,0:T(8,128)S(1)} %get-tuple-element.112), channel_id=1, source_target_pairs={{0,7},{1,6},{2,5},{3,4},{4,3},{5,2},{6,1},{7,0},{8,15},{9,14},{10,... | collective-permute-start | bytes 491528 | tf_op jit(solution)/shard_map/ppermute | solution.py:322
  77.1 9.5 %collective-permute-start.19 = (f32[256,128]{1,0:T(8,128)S(1)}, f32[256,128]{1,0:T(8,128)S(1)}, u32[]{:S(2)}, u32[]{:S(2)}) collective-permute-start(f32[256,128]{1,0:T(8,128)S(1)} %get-tuple-element.116), channel_id=1, source_target_pairs={{0,6},{2,4},{4,2},{6,0},{8,14},{10,12},{12,10},{14,8},{16,22},{18,... | collective-permute-start | bytes 393224 | tf_op jit(solution)/shard_map/ppermute | solution.py:316
  86.6 2.2 %collective-permute-start.28 = (f32[32,128]{1,0:T(8,128)S(1)}, f32[32,128]{1,0:T(8,128)S(1)}, u32[]{:S(2)}, u32[]{:S(2)}) collective-permute-start(f32[32,128]{1,0:T(8,128)S(1)} %get-tuple-element.135), channel_id=1, source_target_pairs={{0,1},{1,0},{2,3},{3,2},{4,5},{5,4},{6,7},{7,6},{8,9},{9,8},{10,11... | collective-permute-start | bytes 49160 | tf_op jit(solution)/shard_map/ppermute | solution.py:481
  88.2 1.4 %collective-permute-start.27 = (f32[32,128]{1,0:T(8,128)S(1)}, f32[32,128]{1,0:T(8,128)S(1)}, u32[]{:S(2)}, u32[]{:S(2)}) collective-permute-start(f32[32,128]{1,0:T(8,128)S(1)} %get-tuple-element.133), channel_id=1, source_target_pairs={{0,1},{1,0},{2,3},{3,2},{4,5},{5,4},{6,7},{7,6},{8,9},{9,8},{10,11... | collective-permute-start | bytes 49160 | tf_op jit(solution)/shard_map/ppermute | solution.py:481

commit v3 on v2

--- a/solution.py
+++ b/solution.py
@@ -30,10 +30,7 @@
 
 
 def partners(g):
-    order = [0]
-    for d in range(g // 2, g - 1):
-        order += [d, g - 1 - d]
-    return order + [g - 1] * (g > 1)
+    return [0, 2, 1, 3] if g == 4 else list(range(g))
 
 
 def place(g):
@@ -120,7 +117,7 @@
         v_all, dy_all, log_rows, skip_row, keys, queries = refs[:6]
     else:
         keys, queries, v_all, dy_all, log_rows, skip_row = refs[:6]
-    v_tail, dy_head, first, second, decay, blocks = refs[6:]
+    weighted, first, blocks = refs[6:]
     window = g * rows
     mine, _, at_window = place(g)
     end = 2 * tiles * rows
@@ -147,14 +144,23 @@
     skips = jnp.transpose(blocks[0])[rows : rows + 1, :heads]
     skip_row[...] = jnp.broadcast_to(spread(skips, heads, tiles), skip_row.shape)
     last = cols[window - 1 : window, :]
-    v_tail[...] = (v_all[...].astype(F32) * spread(jnp.exp(last - cols), heads, tiles)).astype(BF16)
-    dy_head[...] = (dy_all[...].astype(F32) * spread(jnp.exp(cols), heads, tiles)).astype(BF16)
-    ahead = tn(keys[...], v_tail[...])
-    behind = tn(queries[...], dy_head[...])
     odd = lax.rem(at_window, 2) == 1
-    first[...] = jnp.where(odd, behind, ahead)
-    second[...] = jnp.where(odd, ahead, behind)
-    decay[...] = jnp.broadcast_to(spread(jnp.exp(last), heads, tiles), decay.shape)
+    gain = spread(jnp.exp(jnp.where(odd, cols, last - cols)), heads, tiles)
+    weighted[...] = (jnp.where(odd, dy_all[...], v_all[...]).astype(F32) * gain).astype(BF16)
+    states = first.shape[0] - EXTRA
+    first[:states, :] = tn(jnp.where(odd, queries[...], keys[...]), weighted[...])
+    first[states:, :] = jnp.broadcast_to(spread(jnp.exp(last), heads, tiles), (EXTRA, tiles * LANES))
+
+
+def second_kernel(dims, v_all, dy_all, log_rows, keys, queries, weighted, second):
+    g, rows, tiles, heads = dims
+    _, _, at_window = place(g)
+    odd = lax.rem(at_window, 2) == 1
+    cols = jnp.transpose(log_rows[...])[:, :heads]
+    last = cols[g * rows - 1 :, :]
+    gain = spread(jnp.exp(jnp.where(odd, last - cols, cols)), heads, tiles)
+    weighted[...] = (jnp.where(odd, v_all[...], dy_all[...]).astype(F32) * gain).astype(BF16)
+    second[...] = tn(jnp.where(odd, keys[...], queries[...]), weighted[...])
 
 
 def local_kernel(dims, v_all, dy_all, log_rows, skip_row, keys, queries, mixed, grad_v, grad_b, grad_c):
@@ -204,8 +210,14 @@
     grad_v[...] = jnp.transpose(whole_t) + dy_all[...].astype(F32) * skips
 
 
-def step_kernel(decay, state, total, moved):
-    moved[...] = decay[:1, :] * state[...] + total[...]
+def step_kernel(first, second, near, pair):
+    states = pair.shape[0]
+    pair[...] = first[states : states + 1, :] * near[:states, :] + second[...]
+
+
+def last_kernel(first, far, moved):
+    states = moved.shape[0]
+    moved[...] = first[states : states + 1, :] * far[...] + first[:states, :]
 
 
 def halves_of(dims, windows, half):
@@ -216,29 +228,37 @@
     return (low if half == 0 else at >= 2), (at == 1) | (at == 2)
 
 
-def half_kernel(dims, windows, half, last_part, log_rows, mixed, grad_v, grad_b, grad_c, *refs):
+def half_kernel(dims, windows, half, last_part, doubled, log_rows, mixed, grad_v, grad_b, grad_c, *refs):
     g, rows, tiles, heads = dims
     if last_part:
         other, refs = refs[0], refs[1:]
-    keys, queries, v_tail, dy_head, refs = *refs[:4], refs[4:]
+    keys, queries, to_first, to_second, refs = *refs[:4], refs[4:]
     states, refs = refs[: len(refs) - g - 2], refs[len(refs) - g - 2 :]
     pieces, total, whole = refs[:g], refs[g], refs[g + 1]
     window = g * rows
-    mine, _, _ = place(g)
+    mine, _, at_window = place(g)
     forward, inner = halves_of(dims, windows, half)
     if inner is None:
         state = states[0][...]
-    elif half == 0:
-        state = jnp.where(inner, states[0][...], 0.0)
     else:
-        state = jnp.where(inner, states[0][...], states[1][...])
+        count = keys.shape[1]
+        near = states[0][:count, :]
+        if half == 0:
+            state = jnp.where(inner, near, 0.0)
+        else:
+            outer = states[2][...]
+            if doubled:
+                outer = states[0][count : count + 1, :] * outer + near
+            state = jnp.where(inner, states[1][...], outer)
     state = state.astype(BF16)
     cols = jnp.transpose(log_rows[...])[:, :heads]
     last = cols[window - 1 : window, :]
     gain = spread(jnp.exp(pick(forward, cols, last - cols)), heads, tiles)
     more = gain * nn(pick(forward, queries[...], keys[...]), state)
     whole[...] = pick(forward, mixed[...], grad_v[...]) + more
-    summed = pick(forward, grad_c[...], grad_b[...]) + nt(pick(forward, dy_head[...], v_tail[...]), state)
+    odd = lax.rem(at_window, 2) == 1
+    used = odd if forward is True else jnp.logical_not(odd) if forward is False else odd == forward
+    summed = pick(forward, grad_c[...], grad_b[...]) + nt(jnp.where(used, to_first[...], to_second[...]), state)
     if last_part:
         summed = summed + other[...]
     total[...] = summed
@@ -250,14 +270,21 @@
             piece[tiles * rows : (tiles + 1) * rows, :] = total[here, :]
 
 
+def sum_kernel(dims, *refs):
+    g, rows, tiles, heads = dims
+    pieces, shares, total = refs[:g], refs[g:-1], refs[-1]
+    at = slice(tiles * rows, (tiles + 1) * rows)
+    total[...] = functools.reduce(jnp.add, [piece[at, :] for piece in pieces])
+    for e, share in enumerate(shares):
+        part = rows // len(shares)
+        share[...] = total[rows_of(lax.bitwise_xor(lax.axis_index("head"), e), part), :]
+
+
 def unpack_kernel(dims, windows, half, last_part, *refs):
     g, rows, tiles, heads = dims
     pieces, refs = refs[:g], refs[g:]
-    if last_part or half:
-        refs = refs[2:]
-    mixed, grad_v, *shares, now, sent = refs
-    if last_part:
-        shares, total = shares[:-1], shares[-1]
+    mixed, grad_v, done, now, sent = refs[-5:]
+    done[...] = jnp.zeros_like(done)
     mine, core, _ = place(g)
     seq = 1 - core if last_part else core
     forward, _ = halves_of(dims, windows, half)
@@ -283,12 +310,6 @@
     else:
         pl.when(forward)(lambda: send(mixed))
         pl.when(jnp.logical_not(forward))(lambda: send(grad_v))
-    if last_part:
-        at = slice(tiles * rows, (tiles + 1) * rows)
-        total[...] = functools.reduce(jnp.add, [piece[at, :] for piece in pieces])
-        for e, share in enumerate(shares):
-            part = rows // len(shares)
-            share[...] = total[rows_of(lax.bitwise_xor(lax.axis_index("head"), e), part), :]
 
 
 def shards(values, keys_b, queries_c, forget, skip, cotangent):
@@ -339,6 +360,11 @@
             out_specs=[hbm if n in far_out else vmem for n in range(len(out))],
             scratch_shapes=list(scratch),
             input_output_aliases=aliases,
+            cost_estimate=pl.CostEstimate(
+                flops=0,
+                bytes_accessed=sum(a.size * a.dtype.itemsize for a in list(ins) + list(out)),
+                transcendentals=0,
+            ),
             compiler_params=pltpu.CompilerParams(vmem_limit_bytes=limit * MIB),
         )(*ins, *after)
         return list(outs)
@@ -359,7 +385,6 @@
                 pltpu.VMEM((1, head_count), F32),
                 pltpu.SemaphoreType.DMA((8,)),
             ],
-            after=[] if shared else got[0][1:2],
             far=range(6),
             limit=62 if shared else 48,
         )
@@ -376,6 +401,7 @@
     state_shape = shape(state_size, width)
     near = [(i, i ^ g) for i in range(blocks)]
     middle = [(i, i ^ (3 * g) if i // g in (1, 2) else i) for i in range(blocks)]
+    outer = [(i, i ^ (2 * g)) for i in range(blocks) if i // g in (1, 2)]
     maps, sums, back = [], {}, {}
     own, weighted, ends, state, results = ({} for _ in range(5))
 
@@ -384,9 +410,7 @@
             functools.partial(gather_kernel, dims, n == 0),
             own_shapes
             + (map_shapes if n == 0 else [])
-            + [shape(window, width, dtype=BF16)] * 2
-            + [state_shape] * 2
-            + [shape(8, width)],
+            + [shape(window, width, dtype=BF16), shape(state_size + EXTRA, width)],
             got[n] + maps,
             [pltpu.VMEM((g, EXTRA, LANES), F32)],
             after=after,
@@ -395,7 +419,17 @@
         if n == 0:
             maps.extend(outs[:2])
             outs = outs[2:]
-        weighted[n], ends[n] = outs[:2], outs[2:]
+        weighted[n], ends[n] = outs[:1], outs[1:]
+
+    def second(n, after=()):
+        outs = call(
+            functools.partial(second_kernel, dims),
+            [shape(window, width, dtype=BF16), state_shape],
+            own[n][:3] + maps,
+            after=after,
+        )
+        weighted[n] += outs[:1]
+        ends[n] += outs[1:]
 
     def local(n, after=()):
         results[n] = call(
@@ -405,33 +439,40 @@
             after=after,
         )
 
-    def hop(n, k, after=()):
-        first, second, decay = ends[n]
-        if k == 0:
-            state[n] = [lax.ppermute(first, "seq", near)]
-            return []
-        moved = call(
-            step_kernel, [state_shape], [decay, state[n][-1], second if k == 1 else first], after=after
-        )
+    def meet(n):
+        state[n] = [lax.ppermute(ends[n][0], "seq", near)]
+
+    def cross_pairs(n, after=()):
+        pair = call(step_kernel, [state_shape], ends[n] + state[n], after=after)
+        state[n] += [lax.ppermute(pair[0], "seq", perm) for perm in (middle, outer)]
+        return pair
+
+    def step(n, k, after=()):
+        first, other = ends[n]
+        if k == 1:
+            moved = call(step_kernel, [state_shape], [first, other, state[n][-1]], after=after)
+        else:
+            moved = call(last_kernel, [state_shape], [first, state[n][-1]], after=after)
         state[n].append(lax.ppermute(moved[0], "seq", middle if k == 1 else near))
         return moved
 
     def chain(n):
-        first, second, decay = ends[n]
+        first, other = ends[n]
+        first, decay = first[:state_size], first[state_size : state_size + 1]
         odd = lax.rem(lax.div(index, g), 2) == 1
-        total = [jnp.where(odd, second, first), jnp.where(odd, first, second)]
+        total = [jnp.where(odd, other, first), jnp.where(odd, first, other)]
         state[n] = [jnp.zeros_like(first)] * 2
         for k in range(windows - 1):
-            moved = [decay[:1] * a + b for a, b in zip(state[n], total)]
+            moved = [decay * a + b for a, b in zip(state[n], total)]
             state[n] = [lax.ppermute(moved[0], "seq", rise), lax.ppermute(moved[1], "seq", fall)]
 
     def finish(n, half, after=()):
         if windows == 4:
-            states = state[n][:1] if half == 0 else state[n][1:]
+            states = state[n][:1] if half == 0 else state[n]
         else:
             states = state[n][half : half + 1]
         outs = call(
-            functools.partial(half_kernel, dims, windows, half, n == 1),
+            functools.partial(half_kernel, dims, windows, half, n == 1, n == 1),
             [shape((tiles + n) * rows, LANES)] * g + [shape(window, state_size)],
             [own[n][2]] + results[n] + (sums[half] if n else []) + maps + weighted[n] + states,
             [pltpu.VMEM((window, width), F32)],
@@ -442,41 +483,49 @@
 
     gather(0)
     if windows == 4:
-        hop(0, 0)
+        meet(0)
+        second(0)
         local(0)
-        moved = hop(0, 1, after=results[0][:1])
+        gather(1, after=results[0][:1])
+        meet(1)
+        second(1)
+        moved = step(0, 1, after=ends[1][:1])
         finish(0, 0, after=moved)
-        gather(1, after=sums[0])
-        hop(1, 0)
-        moved = hop(0, 2, after=ends[1][:1])
-        local(1, after=moved)
-        moved = hop(1, 1, after=results[1][:1])
-        finish(1, 0, after=moved)
-        finish(0, 1, after=sums[0])
-        hop(1, 2, after=sums[1])
-        finish(1, 1)
+        local(1)
+        cross_pairs(1, after=back[0, 0][1:3] + state[0][1:] + results[1][:1])
+        finish(1, 0)
+        step(0, 2)
+        finish(0, 1, after=back[1, 0][1:2])
+        finish(1, 1, after=back[1, 0][2:] + back[0, 1][1:3])
     else:
         gather(1)
         for n in range(2):
+            second(n)
             chain(n)
             local(n)
             finish(n, 0)
             finish(n, 1)
     part = rows // peers
-    outs, slices = [], []
-    for n, half in ((0, 0), (1, 0), (0, 1), (1, 1)):
-        more = [shape(part, state_size)] * peers if n else []
+    outs, slices, done = [], [], []
+    for n, half in ((0, 0), (0, 1), (1, 0), (1, 1)):
+        if n:
+            shares = call(
+                functools.partial(sum_kernel, dims),
+                [shape(part, state_size)] * peers,
+                back[n, half],
+                [pltpu.VMEM((rows, state_size), F32)],
+                after=done,
+            )
         outs = call(
             functools.partial(unpack_kernel, dims, windows, half, n == 1),
-            [shape(seqs, rows, wide, dtype=BF16)] * 2 + more,
+            [shape(seqs, rows, wide, dtype=BF16)] * 2 + [shape(8, LANES)],
             back[n, half] + outs,
-            [pltpu.VMEM((rows, state_size), F32)] * n
-            + [pltpu.VMEM((rows, wide), BF16), pltpu.SemaphoreType.DMA((4,))],
+            [pltpu.VMEM((rows, wide), BF16), pltpu.SemaphoreType.DMA((4,))],
             far=(g, g + 1),
             far_out=(0, 1),
             aliases={g: 0, g + 1: 1} if outs else {},
         )
-        outs, shares = outs[:2], outs[2:]
+        outs, done = outs[:2], outs[2:]
         if n:
             come = [lax.ppermute(shares[e], "head", [(c, c ^ e) for c in range(peers)]) for e in range(1, peers)]
             ours = functools.reduce(jnp.add, come[1::2], shares[0])

time: 90.5 us -> 80.8 us (0.89)
  waiting for transfers between devices: 35 us -> 27.1 us
  starting transfers between devices: 38.7 us -> 33.7 us
  Pallas kernels: 15.1 us -> 17.6 us
    ppermute x9, waiting for transfers between devices: 23.5 us -> 12.8 us  [same(): return lax.ppermute(piece, 'seq', [(i, i ^ d) for i in range(blocks)])]
    ppermute x6, starting transfers between devices: 17.4 us -> 9.37 us  [the longest x2 3.73 us: meet(): state[n] = [lax.ppermute(ends[n][0], 'seq', near)]]
    ppermute x12, waiting for transfers between devices: 3.37 us -> 10.5 us  [cross(): return lax.ppermute(piece, ('seq', 'head'), perm)]
    ppermute x6, waiting for transfers between devices: 7.23 us -> 3.74 us  [the longest x2 2.02 us: step(): state[n].append(lax.ppermute(moved[0], 'seq', middle if k == 1 else near))]
    pallas_call x18 -> x21, Pallas kernels: 15.1 us -> 17.6 us  [call(): pl.pallas_call(body, out_shape=out, in_specs=[hbm if n in far else vmem f...]
    ppermute x12, starting transfers between devices: 8.97 us -> 11.1 us  [cross(): return lax.ppermute(piece, ('seq', 'head'), perm)]
  transfers between devices with their start and end apart: 29 -> 29, of which waited for: 13 -> 13; matrix products, arithmetic and copies ran while one was open for 0% -> 0% of each run, Pallas kernels for 14% -> 19%
where the time goes in v3:
time: 80.8 us; the launch traced here: 80 us
  starting transfers between devices  33.7 us (42%)
  waiting for transfers between devices  27.1 us (34%)
  Pallas kernels  17.6 us (22%)
  between operations  0.96 us (1%)
    pallas_call x21, Pallas kernels, call(): pl.pallas_call(body, out_shape=out, in_specs=[hbm if n in far else vmem f...  17.6 us
    ppermute x9, waiting for transfers between devices, same(): return lax.ppermute(piece, 'seq', [(i, i ^ d) for i in range(blocks)])  12.8 us
    ppermute x9, starting transfers between devices, same(): return lax.ppermute(piece, 'seq', [(i, i ^ d) for i in range(blocks)])  12.6 us
    ppermute x12, starting transfers between devices, cross(): return lax.ppermute(piece, ('seq', 'head'), perm)  11.1 us
    ppermute x12, waiting for transfers between devices, cross(): return lax.ppermute(piece, ('seq', 'head'), perm)  10.5 us
    ppermute x2, starting transfers between devices, meet(): state[n] = [lax.ppermute(ends[n][0], 'seq', near)]  3.73 us
    ppermute x2, starting transfers between devices, step(): state[n].append(lax.ppermute(moved[0], 'seq', middle if k == 1 else near))  3.69 us
    ppermute x2, waiting for transfers between devices, step(): state[n].append(lax.ppermute(moved[0], 'seq', middle if k == 1 else near))  2.02 us
  transfers between devices with their start and end apart: 29, of which 13 were waited for; matrix products, arithmetic and copies ran while one was open for 0% of the time, Pallas kernels for 19%

profile of v3, /device:TPU:0, one launch (start us, length us, event | category | flops | bytes accessed | tf_op | source)
XLA Modules:
  0.0 80.0 jit_solution(17337453476757510396)
XLA Ops:
  0.7 2.5 %shard_map.86 = (f32[648,128]{1,0:T(8,128)}, f32[648,128]{1,0:T(8,128)}, f32[648,128]{1,0:T(8,128)}, f32[648,128]{1,0:T(8,128)}) custom-call(bf16[2,64,2048]{2,1,0:T(8,128)(2,1)} %refs_0_.3, bf16[2,64,2048]{2,1,0:T(8,128)(2,1)} %refs_1_.3, bf16[2,64,128]{2,1,0:T(8,128)(2,1)} %refs_2_.3, bf16[2,64,128]{2,1,0:T(8,128)(2,1)} %refs_3_.3, f32[2,32,64]{2,1,0:T(8,128)} %refs_4_.3, ...), custom_call_target="tpu_custom_call" | custom-call | bytes 2457728 | tf_op jit(solution)/shard_map/pallas_call | solution.py:356
  3.2 3.0 %collective-permute-start.4 = (f32[648,128]{1,0:T(8,128)}, f32[648,128]{1,0:T(8,128)S(1)}, u32[]{:S(2)}, u32[]{:S(2)}) collective-permute-start(f32[648,128]{1,0:T(8,128)} %get-tuple-element.74), channel_id=1, source_target_pairs={{0,4},{2,6},{4,0},{6,2},{8,12},{10,14},{12,8},{14,10},{16,20},{18,... | collective-permute-start | bytes 995336 | tf_op jit(solution)/shard_map/ppermute | solution.py:337
  6.3 1.5 %collective-permute-start.5 = (f32[648,128]{1,0:T(8,128)}, f32[648,128]{1,0:T(8,128)S(1)}, u32[]{:S(2)}, u32[]{:S(2)}) collective-permute-start(f32[648,128]{1,0:T(8,128)} %get-tuple-element.75), channel_id=1, source_target_pairs={{0,2},{2,0},{4,6},{6,4},{8,10},{10,8},{12,14},{14,12},{16,18},{18,... | collective-permute-start | bytes 995336 | tf_op jit(solution)/shard_map/ppermute | solution.py:337
  8.3 2.1 %collective-permute-start.1 = (f32[520,128]{1,0:T(8,128)S(1)}, f32[520,128]{1,0:T(8,128)S(1)}, u32[]{:S(2)}, u32[]{:S(2)}) collective-permute-start(f32[520,128]{1,0:T(8,128)S(1)} %get-tuple-element.70), channel_id=1, source_target_pairs={{0,5},{1,4},{2,7},{3,6},{4,1},{5,0},{6,3},{7,2},{8,13},{9,12},{10,... | collective-permute-start | bytes 798728 | tf_op jit(solution)/shard_map/ppermute | solution.py:343
  10.4 5.4 %collective-permute-done.4.refs_1_ = f32[648,128]{1,0:T(8,128)S(1)} collective-permute-done((f32[648,128]{1,0:T(8,128)}, f32[648,128]{1,0:T(8,128)S(1)}, u32[]{:S(2)}, u32[]{:S(2)}) %collective-permute-start.4) | collective-permute-done | bytes 331808 | tf_op jit(solution)/shard_map/ppermute | solution.py:337
  15.8 1.4 %collective-permute-done.5.refs_2_ = f32[648,128]{1,0:T(8,128)S(1)} collective-permute-done((f32[648,128]{1,0:T(8,128)}, f32[648,128]{1,0:T(8,128)S(1)}, u32[]{:S(2)}, u32[]{:S(2)}) %collective-permute-start.5) | collective-permute-done | bytes 331808 | tf_op jit(solution)/shard_map/ppermute | solution.py:337
  17.2 2.6 %collective-permute-start.3 = (f32[520,128]{1,0:T(8,128)S(1)}, f32[520,128]{1,0:T(8,128)S(1)}, u32[]{:S(2)}, u32[]{:S(2)}) collective-permute-start(f32[520,128]{1,0:T(8,128)S(1)} %get-tuple-element.72), channel_id=1, source_target_pairs={{0,7},{1,6},{2,5},{3,4},{4,3},{5,2},{6,1},{7,0},{8,15},{9,14},{10,... | collective-permute-start | bytes 798728 | tf_op jit(solution)/shard_map/ppermute | solution.py:343
  19.8 4.1 %collective-permute-done.6.refs_3_ = f32[648,128]{1,0:T(8,128)S(1)} collective-permute-done((f32[648,128]{1,0:T(8,128)}, f32[648,128]{1,0:T(8,128)S(1)}, u32[]{:S(2)}, u32[]{:S(2)}) %collective-permute-start.6) | collective-permute-done | bytes 331808 | tf_op jit(solution)/shard_map/ppermute | solution.py:337
  23.8 1.1 %shard_map.87 = (bf16[256,512]{1,0:T(8,128)(2,1)S(1)}, bf16[256,512]{1,0:T(8,128)(2,1)S(1)}, f32[8,256]{1,0:T(8,128)S(1)}, f32[8,512]{1,0:T(8,128)S(1)}, bf16[25...) custom-call(f32[648,128]{1,0:T(8,128)S(1)} %copy-done.2, ...), custom_call_target="tpu_custom_call" | custom-call | bytes 2547712 | tf_op jit(solution)/shard_map/pallas_call | solution.py:356
  24.9 2.1 %collective-permute-start.7 = (f32[136,512]{1,0:T(8,128)S(1)}, f32[136,512]{1,0:T(8,128)S(1)}, u32[]{:S(2)}, u32[]{:S(2)}) collective-permute-start(f32[136,512]{1,0:T(8,128)S(1)} %get-tuple-element.97.refs_0_), channel_id=1, source_target_pairs={{0,8},{2,10},{4,12},{6,14},{8,0},{10,2},{12,4},{14,6},{16,24},{18,... | collective-permute-start | bytes 835592 | tf_op jit(solution)/shard_map/ppermute | solution.py:443
  27.0 1.4 %shard_map.88 = (f32[256,512]{1,0:T(8,128)S(1)}, f32[256,512]{1,0:T(8,128)S(1)}, f32[256,128]{1,0:T(8,128)S(1)}, f32[256,128]{1,0:T(8,128)S(1)}) custom-call(bf16[256,512]{1,0:T(8,128)(2,1)S(1)} %get-tuple-element.79.refs_0_, bf16[256,512]{1,0:T(8,128)(2,1)S(1)} %get-tuple-element.80.refs_1_, f32[8,256]{1,0:T(8,128)S(1)} %get-tuple-element.81.refs_2_.refs_0_, ...), custom_call_target="tpu_custom_call" | custom-call | bytes 1990656 | tf_op jit(solution)/shard_map/pallas_call | solution.py:356
  28.5 0.6 collective-permute-done.2.refs_2_
  29.1 4.2 %collective-permute-done.3.refs_3_ = f32[520,128]{1,0:T(8,128)S(1)} collective-permute-done((f32[520,128]{1,0:T(8,128)S(1)}, f32[520,128]{1,0:T(8,128)S(1)}, u32[]{:S(2)}, u32[]{:S(2)}) %collective-permute-start.3) | collective-permute-done | bytes 266272 | tf_op jit(solution)/shard_map/ppermute | solution.py:343
  33.3 1.1 %shard_map.89 = (bf16[256,512]{1,0:T(8,128)(2,1)S(1)}, bf16[256,512]{1,0:T(8,128)(2,1)S(1)}, f32[8,256]{1,0:T(8,128)S(1)}, f32[8,512]{1,0:T(8,128)S(1)}, bf16[25...) custom-call(f32[520,128]{1,0:T(8,128)S(1)} %collective-permute-done.refs_0_, ...), custom_call_target="tpu_custom_call" | custom-call | bytes 2285568 | tf_op jit(solution)/shard_map/pallas_call | solution.py:356
  34.4 1.6 %collective-permute-start.10 = (f32[136,512]{1,0:T(8,128)S(1)}, f32[136,512]{1,0:T(8,128)S(1)}, u32[]{:S(2)}, u32[]{:S(2)}) collective-permute-start(f32[136,512]{1,0:T(8,128)S(1)} %get-tuple-element.99.refs_3_.refs_0_), channel_id=1, source_target_pairs={{0,8},{2,10},{4,12},{6,14},{8,0},{10,2},{12,4},{14,6},{16,24},{18,... | collective-permute-start | bytes 835592 | tf_op jit(solution)/shard_map/ppermute | solution.py:443
  36.0 0.8 shard_map.91
  36.9 0.7 collective-permute-start.8
  37.5 0.7 shard_map.94
  38.2 1.0 %collective-permute-start.12 = (f32[256,128]{1,0:T(8,128)S(1)}, f32[256,128]{1,0:T(8,128)S(1)}, u32[]{:S(2)}, u32[]{:S(2)}) collective-permute-start(f32[256,128]{1,0:T(8,128)S(1)} %get-tuple-element.106), channel_id=1, source_target_pairs={{0,4},{2,6},{4,0},{6,2},{8,12},{10,14},{12,8},{14,10},{16,20},{18,... | collective-permute-start | bytes 393224 | tf_op jit(solution)/shard_map/ppermute | solution.py:337
  39.3 1.5 %collective-permute-start.13 = (f32[256,128]{1,0:T(8,128)S(1)}, f32[256,128]{1,0:T(8,128)S(1)}, u32[]{:S(2)}, u32[]{:S(2)}) collective-permute-start(f32[256,128]{1,0:T(8,128)S(1)} %get-tuple-element.107), channel_id=1, source_target_pairs={{0,2},{2,0},{4,6},{6,4},{8,10},{10,8},{12,14},{14,12},{16,18},{18,... | collective-permute-start | bytes 393224 | tf_op jit(solution)/shard_map/ppermute | solution.py:337
  40.8 0.8 shard_map.95
  41.5 1.4 %shard_map.90 = (f32[256,512]{1,0:T(8,128)S(1)}, f32[256,512]{1,0:T(8,128)S(1)}, f32[256,128]{1,0:T(8,128)S(1)}, f32[256,128]{1,0:T(8,128)S(1)}) custom-call(bf16[256,512]{1,0:T(8,128)(2,1)S(1)} %get-tuple-element.85.refs_0_, bf16[256,512]{1,0:T(8,128)(2,1)S(1)} %get-tuple-element.86.refs_1_, f32[8,256]{1,0:T(8,128)S(1)} %get-tuple-element.84.refs_2_.refs_0_, ...), custom_call_target="tpu_custom_call" | custom-call | bytes 1990656 | tf_op jit(solution)/shard_map/pallas_call | solution.py:356
  42.9 0.7 collective-permute-done.10.refs_10_.refs_2_
  43.6 1.2 %shard_map.96 = (f32[320,128]{1,0:T(8,128)S(1)}, f32[320,128]{1,0:T(8,128)S(1)}, f32[320,128]{1,0:T(8,128)S(1)}, f32[320,128]{1,0:T(8,128)S(1)}, f32[256,128]{1,0:T(8,128)}) custom-call(f32[8,256]{1,0:T(8,128)S(1)} %get-tuple-element.84.refs_2_.refs_0_, f32[256,512]{1,0:T(8,128)S(1)} %get-tuple-element.88.refs_1_.refs_6_, ...), custom_call_target="tpu_custom_call" | custom-call | bytes 3170304 | tf_op jit(solution)/shard_map/pallas_call | solution.py:356
  44.8 1.1 %collective-permute-start.11 = (f32[320,128]{1,0:T(8,128)S(1)}, f32[320,128]{1,0:T(8,128)S(1)}, u32[]{:S(2)}, u32[]{:S(2)}) collective-permute-start(f32[320,128]{1,0:T(8,128)S(1)} %get-tuple-element.103), channel_id=1, source_target_pairs={{0,5},{1,4},{2,7},{3,6},{4,1},{5,0},{6,3},{7,2},{8,13},{9,12},{10,... | collective-permute-start | bytes 491528 | tf_op jit(solution)/shard_map/ppermute | solution.py:343
  45.9 3.0 %collective-permute-start.9 = (f32[128,512]{1,0:T(8,128)S(1)}, f32[128,512]{1,0:T(8,128)S(1)}, u32[]{:S(2)}, u32[]{:S(2)}) collective-permute-start(f32[128,512]{1,0:T(8,128)S(1)} %shard_map.93), channel_id=1, source_target_pairs={{0,8},{2,10},{4,12},{6,14},{8,0},{10,2},{12,4},{14,6},{16,24},{18,... | collective-permute-start | bytes 786440 | tf_op jit(solution)/shard_map/ppermute | solution.py:456
  49.0 0.7 collective-permute-start.14
  49.7 0.8 collective-permute-start.16
  50.5 2.0 %collective-permute-start.17 = (f32[320,128]{1,0:T(8,128)S(1)}, f32[320,128]{1,0:T(8,128)S(1)}, u32[]{:S(2)}, u32[]{:S(2)}) collective-permute-start(f32[320,128]{1,0:T(8,128)S(1)} %get-tuple-element.109), channel_id=1, source_target_pairs={{0,7},{1,6},{2,5},{3,4},{4,3},{5,2},{6,1},{7,0},{8,15},{9,14},{10,... | collective-permute-start | bytes 491528 | tf_op jit(solution)/shard_map/ppermute | solution.py:343
  52.4 1.3 %collective-permute-start.15 = (f32[128,512]{1,0:T(8,128)S(1)}, f32[128,512]{1,0:T(8,128)S(1)}, u32[]{:S(2)}, u32[]{:S(2)}) collective-permute-start(f32[128,512]{1,0:T(8,128)S(1)} %shard_map.98), channel_id=1, source_target_pairs={{8,24},{10,26},{12,28},{14,30},{16,0},{18,2},{20,4},{22,6},{9,25},... | collective-permute-start | bytes 786440 | tf_op jit(solution)/shard_map/ppermute | solution.py:447
  53.7 2.0 %collective-permute-done.9.refs_11_ = f32[128,512]{1,0:T(8,128)S(1)} collective-permute-done((f32[128,512]{1,0:T(8,128)S(1)}, f32[128,512]{1,0:T(8,128)S(1)}, u32[]{:S(2)}, u32[]{:S(2)}) %collective-permute-start.9) | collective-permute-done | bytes 262176 | tf_op jit(solution)/shard_map/ppermute | solution.py:456
  55.7 0.7 shard_map.97
  56.4 1.6 %collective-permute-start.18 = (f32[256,128]{1,0:T(8,128)S(1)}, f32[256,128]{1,0:T(8,128)S(1)}, u32[]{:S(2)}, u32[]{:S(2)}) collective-permute-start(f32[256,128]{1,0:T(8,128)S(1)} %get-tuple-element.110), channel_id=1, source_target_pairs={{0,4},{2,6},{4,0},{6,2},{8,12},{10,14},{12,8},{14,10},{16,20},{18,... | collective-permute-start | bytes 393224 | tf_op jit(solution)/shard_map/ppermute | solution.py:337
  58.0 0.9 %collective-permute-start.19 = (f32[256,128]{1,0:T(8,128)S(1)}, f32[256,128]{1,0:T(8,128)S(1)}, u32[]{:S(2)}, u32[]{:S(2)}) collective-permute-start(f32[256,128]{1,0:T(8,128)S(1)} %get-tuple-element.111), channel_id=1, source_target_pairs={{0,2},{2,0},{4,6},{6,4},{8,10},{10,8},{12,14},{14,12},{16,18},{18,... | collective-permute-start | bytes 393224 | tf_op jit(solution)/shard_map/ppermute | solution.py:337
  58.9 1.6 %collective-permute-done.17.refs_14_.refs_3_ = f32[320,128]{1,0:T(8,128)S(1)} collective-permute-done((f32[320,128]{1,0:T(8,128)S(1)}, f32[320,128]{1,0:T(8,128)S(1)}, u32[]{:S(2)}, u32[]{:S(2)}) %collective-permute-start.17) | collective-permute-done | bytes 163872 | tf_op jit(solution)/shard_map/ppermute | solution.py:343
  60.6 0.6 collective-permute-start.26
  61.2 2.3 %collective-permute-start.25 = (f32[256,128]{1,0:T(8,128)S(1)}, f32[256,128]{1,0:T(8,128)S(1)}, u32[]{:S(2)}, u32[]{:S(2)}) collective-permute-start(f32[256,128]{1,0:T(8,128)S(1)} %get-tuple-element.118), channel_id=1, source_target_pairs={{0,6},{2,4},{4,2},{6,0},{8,14},{10,12},{12,10},{14,8},{16,22},{18,... | collective-permute-start | bytes 393224 | tf_op jit(solution)/shard_map/ppermute | solution.py:337
  63.5 1.0 %collective-permute-done.15.refs_12_ = f32[128,512]{1,0:T(8,128)S(1)} collective-permute-done((f32[128,512]{1,0:T(8,128)S(1)}, f32[128,512]{1,0:T(8,128)S(1)}, u32[]{:S(2)}, u32[]{:S(2)}) %collective-permute-start.15) | collective-permute-done | bytes 262176 | tf_op jit(solution)/shard_map/ppermute | solution.py:447
  64.5 1.2 %shard_map.99 = (f32[320,128]{1,0:T(8,128)S(1)}, f32[320,128]{1,0:T(8,128)S(1)}, f32[320,128]{1,0:T(8,128)S(1)}, f32[320,128]{1,0:T(8,128)S(1)}, f32[256,128]{1,0:T(8,128)}) custom-call(f32[8,256]{1,0:T(8,128)S(1)} %get-tuple-element.84.refs_2_.refs_0_, f32[256,512]{1,0:T(8,128)S(1)} %get-tuple-element.88.refs_1_.refs_6_, ...), custom_call_target="tpu_custom_call" | custom-call | bytes 3694592 | tf_op jit(solution)/shard_map/pallas_call | solution.py:356
  66.2 1.1 %collective-permute-start.21 = (f32[320,128]{1,0:T(8,128)S(1)}, f32[320,128]{1,0:T(8,128)S(1)}, u32[]{:S(2)}, u32[]{:S(2)}) collective-permute-start(f32[320,128]{1,0:T(8,128)S(1)} %get-tuple-element.113), channel_id=1, source_target_pairs={{0,5},{1,4},{2,7},{3,6},{4,1},{5,0},{6,3},{7,2},{8,13},{9,12},{10,... | collective-permute-start | bytes 491528 | tf_op jit(solution)/shard_map/ppermute | solution.py:343
  67.7 1.0 %collective-permute-start.22 = (f32[320,128]{1,0:T(8,128)S(1)}, f32[320,128]{1,0:T(8,128)S(1)}, u32[]{:S(2)}, u32[]{:S(2)}) collective-permute-start(f32[320,128]{1,0:T(8,128)S(1)} %get-tuple-element.114), channel_id=1, source_target_pairs={{0,3},{1,2},{2,1},{3,0},{4,7},{5,6},{6,5},{7,4},{8,11},{9,10},{10,... | collective-permute-start | bytes 491528 | tf_op jit(solution)/shard_map/ppermute | solution.py:343
  68.7 1.6 %collective-permute-done.25.refs_3_ = f32[256,128]{1,0:T(8,128)S(1)} collective-permute-done((f32[256,128]{1,0:T(8,128)S(1)}, f32[256,128]{1,0:T(8,128)S(1)}, u32[]{:S(2)}, u32[]{:S(2)}) %collective-permute-start.25) | collective-permute-done | bytes 131104 | tf_op jit(solution)/shard_map/ppermute | solution.py:337
  70.3 1.4 %shard_map.100 = (bf16[2,64,2048]{2,1,0:T(8,128)(2,1)}, bf16[2,64,2048]{2,1,0:T(8,128)(2,1)}, f32[8,128]{1,0:T(8,128)}) custom-call(f32[256,128]{1,0:T(8,128)S(1)} %get-tuple-element.119.refs_0_, f32[256,128]{1,0:T(8,128)S(1)} %collective-permute-done.12.refs_3_.refs_1_, f32[256,128]{1,0:T(8,128)S(1)} %collective-permute-done.13.refs_4_.refs_2_, ...), custom_call_target="tpu_custom_call" | custom-call | bytes 1576960 | tf_op jit(solution)/shard_map/pallas_call | solution.py:356
  71.7 0.8 shard_map.101
  72.9 0.8 shard_map.102
  74.0 3.8 %collective-permute-done.23.refs_3_ = f32[320,128]{1,0:T(8,128)S(1)} collective-permute-done((f32[320,128]{1,0:T(8,128)S(1)}, f32[320,128]{1,0:T(8,128)S(1)}, u32[]{:S(2)}, u32[]{:S(2)}) %collective-permute-start.23) | collective-permute-done | bytes 163872 | tf_op jit(solution)/shard_map/ppermute | solution.py:343
  77.9 1.4 %shard_map.103 = (bf16[2,64,2048]{2,1,0:T(8,128)(2,1)}, bf16[2,64,2048]{2,1,0:T(8,128)(2,1)}, f32[8,128]{1,0:T(8,128)}) custom-call(f32[320,128]{1,0:T(8,128)S(1)} %collective-permute-done.20.refs_0_, f32[320,128]{1,0:T(8,128)S(1)} %collective-permute-done.21.refs_1_, ...), custom_call_target="tpu_custom_call", output_to_operand_aliasing={{0}: (4, {}), {1}: (5, {})} | custom-call | bytes 2756608 | tf_op jit(solution)/shard_map/pallas_call | solution.py:356
  79.4 0.6 pad_maximum_fusion
  (48 shorter events, 2.5 us)
Async XLA Ops:
  0.6 7.2 %copy-start = (bf16[2,64,2048]{2,1,0:T(8,128)(2,1)S(1)}, bf16[2,64,2048]{2,1,0:T(8,128)(2,1)}, u32[]{:S(2)}) copy-start(bf16[2,64,2048]{2,1,0:T(8,128)(2,1)} %refs_0_.3) | copy-start | bytes 1572868
  0.6 7.2 %copy-start.1 = (bf16[2,64,2048]{2,1,0:T(8,128)(2,1)S(1)}, bf16[2,64,2048]{2,1,0:T(8,128)(2,1)}, u32[]{:S(2)}) copy-start(bf16[2,64,2048]{2,1,0:T(8,128)(2,1)} %refs_1_.3) | copy-start | bytes 1572868
  0.7 7.2 %copy-start.3 = (bf16[2,64,128]{2,1,0:T(8,128)(2,1)S(1)}, bf16[2,64,128]{2,1,0:T(8,128)(2,1)}, u32[]{:S(2)}) copy-start(bf16[2,64,128]{2,1,0:T(8,128)(2,1)} %refs_2_.3) | copy-start | bytes 98308
  0.7 7.2 %copy-start.4 = (bf16[2,64,128]{2,1,0:T(8,128)(2,1)S(1)}, bf16[2,64,128]{2,1,0:T(8,128)(2,1)}, u32[]{:S(2)}) copy-start(bf16[2,64,128]{2,1,0:T(8,128)(2,1)} %refs_3_.3) | copy-start | bytes 98308
  0.7 7.2 %copy-start.5 = (f32[2,32,64]{2,1,0:T(8,128)S(1)}, f32[2,32,64]{2,1,0:T(8,128)}, u32[]{:S(2)}) copy-start(f32[2,32,64]{2,1,0:T(8,128)} %refs_4_.3) | copy-start | bytes 49156
  3.2 12.6 %collective-permute-start.4 = (f32[648,128]{1,0:T(8,128)}, f32[648,128]{1,0:T(8,128)S(1)}, u32[]{:S(2)}, u32[]{:S(2)}) collective-permute-start(f32[648,128]{1,0:T(8,128)} %get-tuple-element.74), channel_id=1, source_target_pairs={{0,4},{2,6},{4,0},{6,2},{8,12},{10,14},{12,8},{14,10},{16,20},{18,... | collective-permute-start | bytes 995336 | tf_op jit(solution)/shard_map/ppermute | solution.py:337
  6.3 1.6 %copy-start.6 = (f32[32]{0:T(128)S(1)}, f32[32]{0:T(128)}, u32[]{:S(2)}) copy-start(f32[32]{0:T(128)} %param.10) | copy-start | bytes 388
  6.3 10.9 %collective-permute-start.5 = (f32[648,128]{1,0:T(8,128)}, f32[648,128]{1,0:T(8,128)S(1)}, u32[]{:S(2)}, u32[]{:S(2)}) collective-permute-start(f32[648,128]{1,0:T(8,128)} %get-tuple-element.75), channel_id=1, source_target_pairs={{0,2},{2,0},{4,6},{6,4},{8,10},{10,8},{12,14},{14,12},{16,18},{18,... | collective-permute-start | bytes 995336 | tf_op jit(solution)/shard_map/ppermute | solution.py:337
  7.8 16.1 %copy-start.2 = (f32[648,128]{1,0:T(8,128)S(1)}, f32[648,128]{1,0:T(8,128)}, u32[]{:S(2)}) copy-start(f32[648,128]{1,0:T(8,128)} %get-tuple-element.73.refs_0_) | copy-start | bytes 995332
  7.8 16.1 %collective-permute-start.6 = (f32[648,128]{1,0:T(8,128)}, f32[648,128]{1,0:T(8,128)S(1)}, u32[]{:S(2)}, u32[]{:S(2)}) collective-permute-start(f32[648,128]{1,0:T(8,128)} %get-tuple-element.76), channel_id=1, source_target_pairs={{0,6},{2,4},{4,2},{6,0},{8,14},{10,12},{12,10},{14,8},{16,22},{18,... | collective-permute-start | bytes 995336 | tf_op jit(solution)/shard_map/ppermute | solution.py:337
  8.2 20.2 %collective-permute-start = (f32[520,128]{1,0:T(8,128)S(1)}, f32[520,128]{1,0:T(8,128)S(1)}, u32[]{:S(2)}, u32[]{:S(2)}) collective-permute-start(f32[520,128]{1,0:T(8,128)S(1)} %get-tuple-element.69), channel_id=1, source_target_pairs={{0,1},{1,0},{2,3},{3,2},{4,5},{5,4},{6,7},{7,6},{8,9},{9,8},{10,11... | collective-permute-start | bytes 798728 | tf_op jit(solution)/shard_map/ppermute | solution.py:343
  8.3 20.1 %collective-permute-start.1 = (f32[520,128]{1,0:T(8,128)S(1)}, f32[520,128]{1,0:T(8,128)S(1)}, u32[]{:S(2)}, u32[]{:S(2)}) collective-permute-start(f32[520,128]{1,0:T(8,128)S(1)} %get-tuple-element.70), channel_id=1, source_target_pairs={{0,5},{1,4},{2,7},{3,6},{4,1},{5,0},{6,3},{7,2},{8,13},{9,12},{10,... | collective-permute-start | bytes 798728 | tf_op jit(solution)/shard_map/ppermute | solution.py:343
  15.8 13.3 %collective-permute-start.2 = (f32[520,128]{1,0:T(8,128)S(1)}, f32[520,128]{1,0:T(8,128)S(1)}, u32[]{:S(2)}, u32[]{:S(2)}) collective-permute-start(f32[520,128]{1,0:T(8,128)S(1)} %get-tuple-element.71), channel_id=1, source_target_pairs={{0,3},{1,2},{2,1},{3,0},{4,7},{5,6},{6,5},{7,4},{8,11},{9,10},{10,... | collective-permute-start | bytes 798728 | tf_op jit(solution)/shard_map/ppermute | solution.py:343
  17.2 16.1 %collective-permute-start.3 = (f32[520,128]{1,0:T(8,128)S(1)}, f32[520,128]{1,0:T(8,128)S(1)}, u32[]{:S(2)}, u32[]{:S(2)}) collective-permute-start(f32[520,128]{1,0:T(8,128)S(1)} %get-tuple-element.72), channel_id=1, source_target_pairs={{0,7},{1,6},{2,5},{3,4},{4,3},{5,2},{6,1},{7,0},{8,15},{9,14},{10,... | collective-permute-start | bytes 798728 | tf_op jit(solution)/shard_map/ppermute | solution.py:343
  24.9 11.9 %collective-permute-start.7 = (f32[136,512]{1,0:T(8,128)S(1)}, f32[136,512]{1,0:T(8,128)S(1)}, u32[]{:S(2)}, u32[]{:S(2)}) collective-permute-start(f32[136,512]{1,0:T(8,128)S(1)} %get-tuple-element.97.refs_0_), channel_id=1, source_target_pairs={{0,8},{2,10},{4,12},{6,14},{8,0},{10,2},{12,4},{14,6},{16,24},{18,... | collective-permute-start | bytes 835592 | tf_op jit(solution)/shard_map/ppermute | solution.py:443
  34.4 9.2 %collective-permute-start.10 = (f32[136,512]{1,0:T(8,128)S(1)}, f32[136,512]{1,0:T(8,128)S(1)}, u32[]{:S(2)}, u32[]{:S(2)}) collective-permute-start(f32[136,512]{1,0:T(8,128)S(1)} %get-tuple-element.99.refs_3_.refs_0_), channel_id=1, source_target_pairs={{0,8},{2,10},{4,12},{6,14},{8,0},{10,2},{12,4},{14,6},{16,24},{18,... | collective-permute-start | bytes 835592 | tf_op jit(solution)/shard_map/ppermute | solution.py:443
  36.9 9.1 %collective-permute-start.8 = (f32[128,512]{1,0:T(8,128)S(1)}, f32[128,512]{1,0:T(8,128)S(1)}, u32[]{:S(2)}, u32[]{:S(2)}) collective-permute-start(f32[128,512]{1,0:T(8,128)S(1)} %shard_map.92.refs_10_), channel_id=1, source_target_pairs={{0,0},{2,2},{4,4},{6,6},{8,16},{10,18},{12,20},{14,22},{16,8},{18,... | collective-permute-start | bytes 786440 | tf_op jit(solution)/shard_map/ppermute | solution.py:456
  38.2 10.7 %collective-permute-start.12 = (f32[256,128]{1,0:T(8,128)S(1)}, f32[256,128]{1,0:T(8,128)S(1)}, u32[]{:S(2)}, u32[]{:S(2)}) collective-permute-start(f32[256,128]{1,0:T(8,128)S(1)} %get-tuple-element.106), channel_id=1, source_target_pairs={{0,4},{2,6},{4,0},{6,2},{8,12},{10,14},{12,8},{14,10},{16,20},{18,... | collective-permute-start | bytes 393224 | tf_op jit(solution)/shard_map/ppermute | solution.py:337
  39.3 9.7 %collective-permute-start.13 = (f32[256,128]{1,0:T(8,128)S(1)}, f32[256,128]{1,0:T(8,128)S(1)}, u32[]{:S(2)}, u32[]{:S(2)}) collective-permute-start(f32[256,128]{1,0:T(8,128)S(1)} %get-tuple-element.107), channel_id=1, source_target_pairs={{0,2},{2,0},{4,6},{6,4},{8,10},{10,8},{12,14},{14,12},{16,18},{18,... | collective-permute-start | bytes 393224 | tf_op jit(solution)/shard_map/ppermute | solution.py:337
  44.8 7.6 %collective-permute-start.11 = (f32[320,128]{1,0:T(8,128)S(1)}, f32[320,128]{1,0:T(8,128)S(1)}, u32[]{:S(2)}, u32[]{:S(2)}) collective-permute-start(f32[320,128]{1,0:T(8,128)S(1)} %get-tuple-element.103), channel_id=1, source_target_pairs={{0,5},{1,4},{2,7},{3,6},{4,1},{5,0},{6,3},{7,2},{8,13},{9,12},{10,... | collective-permute-start | bytes 491528 | tf_op jit(solution)/shard_map/ppermute | solution.py:343
  45.9 9.8 %collective-permute-start.9 = (f32[128,512]{1,0:T(8,128)S(1)}, f32[128,512]{1,0:T(8,128)S(1)}, u32[]{:S(2)}, u32[]{:S(2)}) collective-permute-start(f32[128,512]{1,0:T(8,128)S(1)} %shard_map.93), channel_id=1, source_target_pairs={{0,8},{2,10},{4,12},{6,14},{8,0},{10,2},{12,4},{14,6},{16,24},{18,... | collective-permute-start | bytes 786440 | tf_op jit(solution)/shard_map/ppermute | solution.py:456
  49.0 12.2 %collective-permute-start.14 = (f32[128,512]{1,0:T(8,128)S(1)}, f32[128,512]{1,0:T(8,128)S(1)}, u32[]{:S(2)}, u32[]{:S(2)}) collective-permute-start(f32[128,512]{1,0:T(8,128)S(1)} %shard_map.98), channel_id=1, source_target_pairs={{0,0},{2,2},{4,4},{6,6},{8,16},{10,18},{12,20},{14,22},{16,8},{18,... | collective-permute-start | bytes 786440 | tf_op jit(solution)/shard_map/ppermute | solution.py:447
  49.7 8.3 %collective-permute-start.16 = (f32[320,128]{1,0:T(8,128)S(1)}, f32[320,128]{1,0:T(8,128)S(1)}, u32[]{:S(2)}, u32[]{:S(2)}) collective-permute-start(f32[320,128]{1,0:T(8,128)S(1)} %get-tuple-element.108), channel_id=1, source_target_pairs={{0,3},{1,2},{2,1},{3,0},{4,7},{5,6},{6,5},{7,4},{8,11},{9,10},{10,... | collective-permute-start | bytes 491528 | tf_op jit(solution)/shard_map/ppermute | solution.py:343
  50.5 10.1 %collective-permute-start.17 = (f32[320,128]{1,0:T(8,128)S(1)}, f32[320,128]{1,0:T(8,128)S(1)}, u32[]{:S(2)}, u32[]{:S(2)}) collective-permute-start(f32[320,128]{1,0:T(8,128)S(1)} %get-tuple-element.109), channel_id=1, source_target_pairs={{0,7},{1,6},{2,5},{3,4},{4,3},{5,2},{6,1},{7,0},{8,15},{9,14},{10,... | collective-permute-start | bytes 491528 | tf_op jit(solution)/shard_map/ppermute | solution.py:343
  52.4 12.1 %collective-permute-start.15 = (f32[128,512]{1,0:T(8,128)S(1)}, f32[128,512]{1,0:T(8,128)S(1)}, u32[]{:S(2)}, u32[]{:S(2)}) collective-permute-start(f32[128,512]{1,0:T(8,128)S(1)} %shard_map.98), channel_id=1, source_target_pairs={{8,24},{10,26},{12,28},{14,30},{16,0},{18,2},{20,4},{22,6},{9,25},... | collective-permute-start | bytes 786440 | tf_op jit(solution)/shard_map/ppermute | solution.py:447
  56.4 8.1 %collective-permute-start.18 = (f32[256,128]{1,0:T(8,128)S(1)}, f32[256,128]{1,0:T(8,128)S(1)}, u32[]{:S(2)}, u32[]{:S(2)}) collective-permute-start(f32[256,128]{1,0:T(8,128)S(1)} %get-tuple-element.110), channel_id=1, source_target_pairs={{0,4},{2,6},{4,0},{6,2},{8,12},{10,14},{12,8},{14,10},{16,20},{18,... | collective-permute-start | bytes 393224 | tf_op jit(solution)/shard_map/ppermute | solution.py:337
  58.0 6.5 %collective-permute-start.19 = (f32[256,128]{1,0:T(8,128)S(1)}, f32[256,128]{1,0:T(8,128)S(1)}, u32[]{:S(2)}, u32[]{:S(2)}) collective-permute-start(f32[256,128]{1,0:T(8,128)S(1)} %get-tuple-element.111), channel_id=1, source_target_pairs={{0,2},{2,0},{4,6},{6,4},{8,10},{10,8},{12,14},{14,12},{16,18},{18,... | collective-permute-start | bytes 393224 | tf_op jit(solution)/shard_map/ppermute | solution.py:337
  60.6 7.2 %collective-permute-start.26 = (f32[256,128]{1,0:T(8,128)S(1)}, f32[256,128]{1,0:T(8,128)S(1)}, u32[]{:S(2)}, u32[]{:S(2)}) collective-permute-start(f32[256,128]{1,0:T(8,128)S(1)} %get-tuple-element.120), channel_id=1, source_target_pairs={{0,6},{2,4},{4,2},{6,0},{8,14},{10,12},{12,10},{14,8},{16,22},{18,... | collective-permute-start | bytes 393224 | tf_op jit(solution)/shard_map/ppermute | solution.py:337
  61.2 9.1 %collective-permute-start.25 = (f32[256,128]{1,0:T(8,128)S(1)}, f32[256,128]{1,0:T(8,128)S(1)}, u32[]{:S(2)}, u32[]{:S(2)}) collective-permute-start(f32[256,128]{1,0:T(8,128)S(1)} %get-tuple-element.118), channel_id=1, source_target_pairs={{0,6},{2,4},{4,2},{6,0},{8,14},{10,12},{12,10},{14,8},{16,22},{18,... | collective-permute-start | bytes 393224 | tf_op jit(solution)/shard_map/ppermute | solution.py:337
  64.5 8.0 %collective-permute-start.24 = (f32[320,128]{1,0:T(8,128)S(1)}, f32[320,128]{1,0:T(8,128)S(1)}, u32[]{:S(2)}, u32[]{:S(2)}) collective-permute-start(f32[320,128]{1,0:T(8,128)S(1)} %get-tuple-element.116), channel_id=1, source_target_pairs={{0,1},{1,0},{2,3},{3,2},{4,5},{5,4},{6,7},{7,6},{8,9},{9,8},{10,11... | collective-permute-start | bytes 491528 | tf_op jit(solution)/shard_map/ppermute | solution.py:343
  65.7 8.0 %collective-permute-start.20 = (f32[320,128]{1,0:T(8,128)S(1)}, f32[320,128]{1,0:T(8,128)S(1)}, u32[]{:S(2)}, u32[]{:S(2)}) collective-permute-start(f32[320,128]{1,0:T(8,128)S(1)} %get-tuple-element.112), channel_id=1, source_target_pairs={{0,1},{1,0},{2,3},{3,2},{4,5},{5,4},{6,7},{7,6},{8,9},{9,8},{10,11... | collective-permute-start | bytes 491528 | tf_op jit(solution)/shard_map/ppermute | solution.py:343
  66.2 7.5 %collective-permute-start.21 = (f32[320,128]{1,0:T(8,128)S(1)}, f32[320,128]{1,0:T(8,128)S(1)}, u32[]{:S(2)}, u32[]{:S(2)}) collective-permute-start(f32[320,128]{1,0:T(8,128)S(1)} %get-tuple-element.113), channel_id=1, source_target_pairs={{0,5},{1,4},{2,7},{3,6},{4,1},{5,0},{6,3},{7,2},{8,13},{9,12},{10,... | collective-permute-start | bytes 491528 | tf_op jit(solution)/shard_map/ppermute | solution.py:343
  67.7 6.2 %collective-permute-start.22 = (f32[320,128]{1,0:T(8,128)S(1)}, f32[320,128]{1,0:T(8,128)S(1)}, u32[]{:S(2)}, u32[]{:S(2)}) collective-permute-start(f32[320,128]{1,0:T(8,128)S(1)} %get-tuple-element.114), channel_id=1, source_target_pairs={{0,3},{1,2},{2,1},{3,0},{4,7},{5,6},{6,5},{7,4},{8,11},{9,10},{10,... | collective-permute-start | bytes 491528 | tf_op jit(solution)/shard_map/ppermute | solution.py:343
  70.3 7.5 %collective-permute-start.23 = (f32[320,128]{1,0:T(8,128)S(1)}, f32[320,128]{1,0:T(8,128)S(1)}, u32[]{:S(2)}, u32[]{:S(2)}) collective-permute-start(f32[320,128]{1,0:T(8,128)S(1)} %get-tuple-element.115), channel_id=1, source_target_pairs={{0,7},{1,6},{2,5},{3,4},{4,3},{5,2},{6,1},{7,0},{8,15},{9,14},{10,... | collective-permute-start | bytes 491528 | tf_op jit(solution)/shard_map/ppermute | solution.py:343
  72.5 6.8 %collective-permute-start.28 = (f32[32,128]{1,0:T(8,128)S(1)}, f32[32,128]{1,0:T(8,128)S(1)}, u32[]{:S(2)}, u32[]{:S(2)}) collective-permute-start(f32[32,128]{1,0:T(8,128)S(1)} %get-tuple-element.133), channel_id=1, source_target_pairs={{0,1},{1,0},{2,3},{3,2},{4,5},{5,4},{6,7},{7,6},{8,9},{9,8},{10,11... | collective-permute-start | bytes 49160 | tf_op jit(solution)/shard_map/ppermute | solution.py:530
  77.7 1.6 %collective-permute-start.27 = (f32[32,128]{1,0:T(8,128)S(1)}, f32[32,128]{1,0:T(8,128)S(1)}, u32[]{:S(2)}, u32[]{:S(2)}) collective-permute-start(f32[32,128]{1,0:T(8,128)S(1)} %get-tuple-element.130), channel_id=1, source_target_pairs={{0,1},{1,0},{2,3},{3,2},{4,5},{5,4},{6,7},{7,6},{8,9},{9,8},{10,11... | collective-permute-start | bytes 49160 | tf_op jit(solution)/shard_map/ppermute | solution.py:530

commit v4 on v3

--- a/solution.py
+++ b/solution.py
@@ -280,11 +280,12 @@
         share[...] = total[rows_of(lax.bitwise_xor(lax.axis_index("head"), e), part), :]
 
 
-def unpack_kernel(dims, windows, half, last_part, *refs):
+def unpack_kernel(dims, windows, half, last_part, marked, *refs):
     g, rows, tiles, heads = dims
     pieces, refs = refs[:g], refs[g:]
-    mixed, grad_v, done, now, sent = refs[-5:]
-    done[...] = jnp.zeros_like(done)
+    mixed, grad_v, *done, now, sent = refs[-5:] if marked else refs[-4:]
+    for mark in done:
+        mark[...] = jnp.zeros_like(mark)
     mine, core, _ = place(g)
     seq = 1 - core if last_part else core
     forward, _ = halves_of(dims, windows, half)
@@ -508,17 +509,18 @@
     part = rows // peers
     outs, slices, done = [], [], []
     for n, half in ((0, 0), (0, 1), (1, 0), (1, 1)):
+        marked = (n, half) != (1, 1)
         if n:
             shares = call(
                 functools.partial(sum_kernel, dims),
                 [shape(part, state_size)] * peers,
                 back[n, half],
                 [pltpu.VMEM((rows, state_size), F32)],
-                after=done,
+                after=done + sums[half],
             )
         outs = call(
-            functools.partial(unpack_kernel, dims, windows, half, n == 1),
-            [shape(seqs, rows, wide, dtype=BF16)] * 2 + [shape(8, LANES)],
+            functools.partial(unpack_kernel, dims, windows, half, n == 1, marked),
+            [shape(seqs, rows, wide, dtype=BF16)] * 2 + [shape(8, LANES)] * marked,
             back[n, half] + outs,
             [pltpu.VMEM((rows, wide), BF16), pltpu.SemaphoreType.DMA((4,))],
             far=(g, g + 1),

time: 80.8 us -> 80.2 us (level)
  Pallas kernels: 17.6 us -> 16 us
  starting transfers between devices: 33.7 us -> 34.6 us
    pallas_call x21, Pallas kernels: 17.6 us -> 16 us  [call(): pl.pallas_call(body, out_shape=out, in_specs=[hbm if n in far else vmem f...]
    ppermute x12, waiting for transfers between devices: 10.5 us -> 9.48 us  [cross(): return lax.ppermute(piece, ('seq', 'head'), perm)]
  transfers between devices with their start and end apart: 29 -> 29, of which waited for: 13 -> 13; matrix products, arithmetic and copies ran while one was open for 0% -> 0% of each run, Pallas kernels for 19% -> 17%
where the time goes in v4:
time: 80.2 us; the launch traced here: 79.1 us
  starting transfers between devices  34.6 us (43%)
  waiting for transfers between devices  26.9 us (34%)
  Pallas kernels  16 us (20%)
  between operations  0.97 us (1%)
    pallas_call x21, Pallas kernels, call(): pl.pallas_call(body, out_shape=out, in_specs=[hbm if n in far else vmem f...  16 us
    ppermute x9, waiting for transfers between devices, same(): return lax.ppermute(piece, 'seq', [(i, i ^ d) for i in range(blocks)])  13 us
    ppermute x9, starting transfers between devices, same(): return lax.ppermute(piece, 'seq', [(i, i ^ d) for i in range(blocks)])  13 us
    ppermute x12, starting transfers between devices, cross(): return lax.ppermute(piece, ('seq', 'head'), perm)  10.8 us
    ppermute x12, waiting for transfers between devices, cross(): return lax.ppermute(piece, ('seq', 'head'), perm)  9.48 us
    ppermute x2, starting transfers between devices, step(): state[n].append(lax.ppermute(moved[0], 'seq', middle if k == 1 else near))  4.15 us
    ppermute x2, starting transfers between devices, meet(): state[n] = [lax.ppermute(ends[n][0], 'seq', near)]  3.73 us
    ppermute x2, waiting for transfers between devices, step(): state[n].append(lax.ppermute(moved[0], 'seq', middle if k == 1 else near))  2.07 us
  transfers between devices with their start and end apart: 29, of which 13 were waited for; matrix products, arithmetic and copies ran while one was open for 0% of the time, Pallas kernels for 17%

profile of v4, /device:TPU:0, one launch (start us, length us, event | category | flops | bytes accessed | tf_op | source)
XLA Modules:
  0.0 79.1 jit_solution(3342617116599761048)
XLA Ops:
  0.7 2.5 %shard_map.86 = (f32[648,128]{1,0:T(8,128)}, f32[648,128]{1,0:T(8,128)}, f32[648,128]{1,0:T(8,128)}, f32[648,128]{1,0:T(8,128)}) custom-call(bf16[2,64,2048]{2,1,0:T(8,128)(2,1)} %refs_0_.3, bf16[2,64,2048]{2,1,0:T(8,128)(2,1)} %refs_1_.3, bf16[2,64,128]{2,1,0:T(8,128)(2,1)} %refs_2_.3, bf16[2,64,128]{2,1,0:T(8,128)(2,1)} %refs_3_.3, f32[2,32,64]{2,1,0:T(8,128)} %refs_4_.3, ...), custom_call_target="tpu_custom_call" | custom-call | bytes 2457728 | tf_op jit(solution)/shard_map/pallas_call | solution.py:357
  3.2 3.0 %collective-permute-start.4 = (f32[648,128]{1,0:T(8,128)}, f32[648,128]{1,0:T(8,128)S(1)}, u32[]{:S(2)}, u32[]{:S(2)}) collective-permute-start(f32[648,128]{1,0:T(8,128)} %get-tuple-element.76), channel_id=1, source_target_pairs={{0,4},{2,6},{4,0},{6,2},{8,12},{10,14},{12,8},{14,10},{16,20},{18,... | collective-permute-start | bytes 995336 | tf_op jit(solution)/shard_map/ppermute | solution.py:338
  6.3 1.5 %collective-permute-start.5 = (f32[648,128]{1,0:T(8,128)}, f32[648,128]{1,0:T(8,128)S(1)}, u32[]{:S(2)}, u32[]{:S(2)}) collective-permute-start(f32[648,128]{1,0:T(8,128)} %get-tuple-element.77), channel_id=1, source_target_pairs={{0,2},{2,0},{4,6},{6,4},{8,10},{10,8},{12,14},{14,12},{16,18},{18,... | collective-permute-start | bytes 995336 | tf_op jit(solution)/shard_map/ppermute | solution.py:338
  8.3 2.1 %collective-permute-start.1 = (f32[520,128]{1,0:T(8,128)S(1)}, f32[520,128]{1,0:T(8,128)S(1)}, u32[]{:S(2)}, u32[]{:S(2)}) collective-permute-start(f32[520,128]{1,0:T(8,128)S(1)} %get-tuple-element.72), channel_id=1, source_target_pairs={{0,5},{1,4},{2,7},{3,6},{4,1},{5,0},{6,3},{7,2},{8,13},{9,12},{10,... | collective-permute-start | bytes 798728 | tf_op jit(solution)/shard_map/ppermute | solution.py:344
  10.4 5.4 %collective-permute-done.4.refs_1_ = f32[648,128]{1,0:T(8,128)S(1)} collective-permute-done((f32[648,128]{1,0:T(8,128)}, f32[648,128]{1,0:T(8,128)S(1)}, u32[]{:S(2)}, u32[]{:S(2)}) %collective-permute-start.4) | collective-permute-done | bytes 331808 | tf_op jit(solution)/shard_map/ppermute | solution.py:338
  15.8 1.4 %collective-permute-done.5.refs_2_ = f32[648,128]{1,0:T(8,128)S(1)} collective-permute-done((f32[648,128]{1,0:T(8,128)}, f32[648,128]{1,0:T(8,128)S(1)}, u32[]{:S(2)}, u32[]{:S(2)}) %collective-permute-start.5) | collective-permute-done | bytes 331808 | tf_op jit(solution)/shard_map/ppermute | solution.py:338
  17.2 2.6 %collective-permute-start.3 = (f32[520,128]{1,0:T(8,128)S(1)}, f32[520,128]{1,0:T(8,128)S(1)}, u32[]{:S(2)}, u32[]{:S(2)}) collective-permute-start(f32[520,128]{1,0:T(8,128)S(1)} %get-tuple-element.74), channel_id=1, source_target_pairs={{0,7},{1,6},{2,5},{3,4},{4,3},{5,2},{6,1},{7,0},{8,15},{9,14},{10,... | collective-permute-start | bytes 798728 | tf_op jit(solution)/shard_map/ppermute | solution.py:344
  19.8 4.1 %collective-permute-done.6.refs_3_ = f32[648,128]{1,0:T(8,128)S(1)} collective-permute-done((f32[648,128]{1,0:T(8,128)}, f32[648,128]{1,0:T(8,128)S(1)}, u32[]{:S(2)}, u32[]{:S(2)}) %collective-permute-start.6) | collective-permute-done | bytes 331808 | tf_op jit(solution)/shard_map/ppermute | solution.py:338
  23.8 1.1 %shard_map.87 = (bf16[256,512]{1,0:T(8,128)(2,1)S(1)}, bf16[256,512]{1,0:T(8,128)(2,1)S(1)}, f32[8,256]{1,0:T(8,128)S(1)}, f32[8,512]{1,0:T(8,128)S(1)}, bf16[25...) custom-call(f32[648,128]{1,0:T(8,128)S(1)} %copy-done.2, ...), custom_call_target="tpu_custom_call" | custom-call | bytes 2547712 | tf_op jit(solution)/shard_map/pallas_call | solution.py:357
  24.9 2.1 %collective-permute-start.7 = (f32[136,512]{1,0:T(8,128)S(1)}, f32[136,512]{1,0:T(8,128)S(1)}, u32[]{:S(2)}, u32[]{:S(2)}) collective-permute-start(f32[136,512]{1,0:T(8,128)S(1)} %get-tuple-element.99.refs_0_), channel_id=1, source_target_pairs={{0,8},{2,10},{4,12},{6,14},{8,0},{10,2},{12,4},{14,6},{16,24},{18,... | collective-permute-start | bytes 835592 | tf_op jit(solution)/shard_map/ppermute | solution.py:444
  27.0 1.4 %shard_map.88 = (f32[256,512]{1,0:T(8,128)S(1)}, f32[256,512]{1,0:T(8,128)S(1)}, f32[256,128]{1,0:T(8,128)S(1)}, f32[256,128]{1,0:T(8,128)S(1)}) custom-call(bf16[256,512]{1,0:T(8,128)(2,1)S(1)} %get-tuple-element.81.refs_0_, bf16[256,512]{1,0:T(8,128)(2,1)S(1)} %get-tuple-element.82.refs_1_, f32[8,256]{1,0:T(8,128)S(1)} %get-tuple-element.83.refs_2_.refs_0_, ...), custom_call_target="tpu_custom_call" | custom-call | bytes 1990656 | tf_op jit(solution)/shard_map/pallas_call | solution.py:357
  29.1 4.2 %collective-permute-done.3.refs_3_ = f32[520,128]{1,0:T(8,128)S(1)} collective-permute-done((f32[520,128]{1,0:T(8,128)S(1)}, f32[520,128]{1,0:T(8,128)S(1)}, u32[]{:S(2)}, u32[]{:S(2)}) %collective-permute-start.3) | collective-permute-done | bytes 266272 | tf_op jit(solution)/shard_map/ppermute | solution.py:344
  33.3 1.1 %shard_map.89 = (bf16[256,512]{1,0:T(8,128)(2,1)S(1)}, bf16[256,512]{1,0:T(8,128)(2,1)S(1)}, f32[8,256]{1,0:T(8,128)S(1)}, f32[8,512]{1,0:T(8,128)S(1)}, bf16[25...) custom-call(f32[520,128]{1,0:T(8,128)S(1)} %collective-permute-done.refs_0_, ...), custom_call_target="tpu_custom_call" | custom-call | bytes 2285568 | tf_op jit(solution)/shard_map/pallas_call | solution.py:357
  34.4 1.6 %collective-permute-start.10 = (f32[136,512]{1,0:T(8,128)S(1)}, f32[136,512]{1,0:T(8,128)S(1)}, u32[]{:S(2)}, u32[]{:S(2)}) collective-permute-start(f32[136,512]{1,0:T(8,128)S(1)} %get-tuple-element.101.refs_3_.refs_0_), channel_id=1, source_target_pairs={{0,8},{2,10},{4,12},{6,14},{8,0},{10,2},{12,4},{14,6},{16,24},{18,... | collective-permute-start | bytes 835592 | tf_op jit(solution)/shard_map/ppermute | solution.py:444
  36.0 0.8 shard_map.91
  36.9 0.7 collective-permute-start.8
  37.5 0.7 shard_map.94
  38.2 1.0 %collective-permute-start.12 = (f32[256,128]{1,0:T(8,128)S(1)}, f32[256,128]{1,0:T(8,128)S(1)}, u32[]{:S(2)}, u32[]{:S(2)}) collective-permute-start(f32[256,128]{1,0:T(8,128)S(1)} %get-tuple-element.108), channel_id=1, source_target_pairs={{0,4},{2,6},{4,0},{6,2},{8,12},{10,14},{12,8},{14,10},{16,20},{18,... | collective-permute-start | bytes 393224 | tf_op jit(solution)/shard_map/ppermute | solution.py:338
  39.3 1.5 %collective-permute-start.13 = (f32[256,128]{1,0:T(8,128)S(1)}, f32[256,128]{1,0:T(8,128)S(1)}, u32[]{:S(2)}, u32[]{:S(2)}) collective-permute-start(f32[256,128]{1,0:T(8,128)S(1)} %get-tuple-element.109), channel_id=1, source_target_pairs={{0,2},{2,0},{4,6},{6,4},{8,10},{10,8},{12,14},{14,12},{16,18},{18,... | collective-permute-start | bytes 393224 | tf_op jit(solution)/shard_map/ppermute | solution.py:338
  40.8 0.8 shard_map.95
  41.5 1.4 %shard_map.90 = (f32[256,512]{1,0:T(8,128)S(1)}, f32[256,512]{1,0:T(8,128)S(1)}, f32[256,128]{1,0:T(8,128)S(1)}, f32[256,128]{1,0:T(8,128)S(1)}) custom-call(bf16[256,512]{1,0:T(8,128)(2,1)S(1)} %get-tuple-element.87.refs_0_, bf16[256,512]{1,0:T(8,128)(2,1)S(1)} %get-tuple-element.88.refs_1_, f32[8,256]{1,0:T(8,128)S(1)} %get-tuple-element.86.refs_2_.refs_0_, ...), custom_call_target="tpu_custom_call" | custom-call | bytes 1990656 | tf_op jit(solution)/shard_map/pallas_call | solution.py:357
  42.9 0.7 collective-permute-done.10.refs_10_.refs_2_
  43.6 0.7 shard_map.96
  44.3 1.1 %collective-permute-start.11 = (f32[320,128]{1,0:T(8,128)S(1)}, f32[320,128]{1,0:T(8,128)S(1)}, u32[]{:S(2)}, u32[]{:S(2)}) collective-permute-start(f32[320,128]{1,0:T(8,128)S(1)} %get-tuple-element.105), channel_id=1, source_target_pairs={{0,5},{1,4},{2,7},{3,6},{4,1},{5,0},{6,3},{7,2},{8,13},{9,12},{10,... | collective-permute-start | bytes 491528 | tf_op jit(solution)/shard_map/ppermute | solution.py:344
  45.5 3.5 %collective-permute-start.9 = (f32[128,512]{1,0:T(8,128)S(1)}, f32[128,512]{1,0:T(8,128)S(1)}, u32[]{:S(2)}, u32[]{:S(2)}) collective-permute-start(f32[128,512]{1,0:T(8,128)S(1)} %shard_map.93), channel_id=1, source_target_pairs={{0,8},{2,10},{4,12},{6,14},{8,0},{10,2},{12,4},{14,6},{16,24},{18,... | collective-permute-start | bytes 786440 | tf_op jit(solution)/shard_map/ppermute | solution.py:457
  49.0 0.7 collective-permute-start.14
  49.7 0.7 collective-permute-start.16
  50.4 1.6 %collective-permute-start.17 = (f32[320,128]{1,0:T(8,128)S(1)}, f32[320,128]{1,0:T(8,128)S(1)}, u32[]{:S(2)}, u32[]{:S(2)}) collective-permute-start(f32[320,128]{1,0:T(8,128)S(1)} %get-tuple-element.111), channel_id=1, source_target_pairs={{0,7},{1,6},{2,5},{3,4},{4,3},{5,2},{6,1},{7,0},{8,15},{9,14},{10,... | collective-permute-start | bytes 491528 | tf_op jit(solution)/shard_map/ppermute | solution.py:344
  52.0 1.3 %collective-permute-start.15 = (f32[128,512]{1,0:T(8,128)S(1)}, f32[128,512]{1,0:T(8,128)S(1)}, u32[]{:S(2)}, u32[]{:S(2)}) collective-permute-start(f32[128,512]{1,0:T(8,128)S(1)} %shard_map.98), channel_id=1, source_target_pairs={{8,24},{10,26},{12,28},{14,30},{16,0},{18,2},{20,4},{22,6},{9,25},... | collective-permute-start | bytes 786440 | tf_op jit(solution)/shard_map/ppermute | solution.py:448
  53.3 2.1 %collective-permute-done.9.refs_11_ = f32[128,512]{1,0:T(8,128)S(1)} collective-permute-done((f32[128,512]{1,0:T(8,128)S(1)}, f32[128,512]{1,0:T(8,128)S(1)}, u32[]{:S(2)}, u32[]{:S(2)}) %collective-permute-start.9) | collective-permute-done | bytes 262176 | tf_op jit(solution)/shard_map/ppermute | solution.py:457
  55.3 0.7 shard_map.97
  56.0 1.5 %collective-permute-start.18 = (f32[256,128]{1,0:T(8,128)S(1)}, f32[256,128]{1,0:T(8,128)S(1)}, u32[]{:S(2)}, u32[]{:S(2)}) collective-permute-start(f32[256,128]{1,0:T(8,128)S(1)} %get-tuple-element.112), channel_id=1, source_target_pairs={{0,4},{2,6},{4,0},{6,2},{8,12},{10,14},{12,8},{14,10},{16,20},{18,... | collective-permute-start | bytes 393224 | tf_op jit(solution)/shard_map/ppermute | solution.py:338
  57.5 1.4 %collective-permute-start.19 = (f32[256,128]{1,0:T(8,128)S(1)}, f32[256,128]{1,0:T(8,128)S(1)}, u32[]{:S(2)}, u32[]{:S(2)}) collective-permute-start(f32[256,128]{1,0:T(8,128)S(1)} %get-tuple-element.113), channel_id=1, source_target_pairs={{0,2},{2,0},{4,6},{6,4},{8,10},{10,8},{12,14},{14,12},{16,18},{18,... | collective-permute-start | bytes 393224 | tf_op jit(solution)/shard_map/ppermute | solution.py:338
  58.9 1.2 %collective-permute-done.17.refs_14_.refs_3_ = f32[320,128]{1,0:T(8,128)S(1)} collective-permute-done((f32[320,128]{1,0:T(8,128)S(1)}, f32[320,128]{1,0:T(8,128)S(1)}, u32[]{:S(2)}, u32[]{:S(2)}) %collective-permute-start.17) | collective-permute-done | bytes 163872 | tf_op jit(solution)/shard_map/ppermute | solution.py:344
  60.1 1.1 %collective-permute-start.26 = (f32[256,128]{1,0:T(8,128)S(1)}, f32[256,128]{1,0:T(8,128)S(1)}, u32[]{:S(2)}, u32[]{:S(2)}) collective-permute-start(f32[256,128]{1,0:T(8,128)S(1)} %get-tuple-element.122), channel_id=1, source_target_pairs={{0,6},{2,4},{4,2},{6,0},{8,14},{10,12},{12,10},{14,8},{16,22},{18,... | collective-permute-start | bytes 393224 | tf_op jit(solution)/shard_map/ppermute | solution.py:338
  61.2 1.8 %collective-permute-start.25 = (f32[256,128]{1,0:T(8,128)S(1)}, f32[256,128]{1,0:T(8,128)S(1)}, u32[]{:S(2)}, u32[]{:S(2)}) collective-permute-start(f32[256,128]{1,0:T(8,128)S(1)} %get-tuple-element.120), channel_id=1, source_target_pairs={{0,6},{2,4},{4,2},{6,0},{8,14},{10,12},{12,10},{14,8},{16,22},{18,... | collective-permute-start | bytes 393224 | tf_op jit(solution)/shard_map/ppermute | solution.py:338
  63.0 1.4 %collective-permute-done.15.refs_12_ = f32[128,512]{1,0:T(8,128)S(1)} collective-permute-done((f32[128,512]{1,0:T(8,128)S(1)}, f32[128,512]{1,0:T(8,128)S(1)}, u32[]{:S(2)}, u32[]{:S(2)}) %collective-permute-start.15) | collective-permute-done | bytes 262176 | tf_op jit(solution)/shard_map/ppermute | solution.py:448
  64.4 0.7 shard_map.99
  65.6 1.1 %collective-permute-start.21 = (f32[320,128]{1,0:T(8,128)S(1)}, f32[320,128]{1,0:T(8,128)S(1)}, u32[]{:S(2)}, u32[]{:S(2)}) collective-permute-start(f32[320,128]{1,0:T(8,128)S(1)} %get-tuple-element.115), channel_id=1, source_target_pairs={{0,5},{1,4},{2,7},{3,6},{4,1},{5,0},{6,3},{7,2},{8,13},{9,12},{10,... | collective-permute-start | bytes 491528 | tf_op jit(solution)/shard_map/ppermute | solution.py:344
  67.3 1.0 %collective-permute-start.22 = (f32[320,128]{1,0:T(8,128)S(1)}, f32[320,128]{1,0:T(8,128)S(1)}, u32[]{:S(2)}, u32[]{:S(2)}) collective-permute-start(f32[320,128]{1,0:T(8,128)S(1)} %get-tuple-element.116), channel_id=1, source_target_pairs={{0,3},{1,2},{2,1},{3,0},{4,7},{5,6},{6,5},{7,4},{8,11},{9,10},{10,... | collective-permute-start | bytes 491528 | tf_op jit(solution)/shard_map/ppermute | solution.py:344
  68.3 1.6 %collective-permute-done.25.refs_3_ = f32[256,128]{1,0:T(8,128)S(1)} collective-permute-done((f32[256,128]{1,0:T(8,128)S(1)}, f32[256,128]{1,0:T(8,128)S(1)}, u32[]{:S(2)}, u32[]{:S(2)}) %collective-permute-start.25) | collective-permute-done | bytes 131104 | tf_op jit(solution)/shard_map/ppermute | solution.py:338
  69.8 1.4 %shard_map.100 = (bf16[2,64,2048]{2,1,0:T(8,128)(2,1)}, bf16[2,64,2048]{2,1,0:T(8,128)(2,1)}, f32[8,128]{1,0:T(8,128)}) custom-call(f32[256,128]{1,0:T(8,128)S(1)} %get-tuple-element.121.refs_0_, f32[256,128]{1,0:T(8,128)S(1)} %collective-permute-done.12.refs_3_.refs_1_, f32[256,128]{1,0:T(8,128)S(1)} %collective-permute-done.13.refs_4_.refs_2_, ...), custom_call_target="tpu_custom_call" | custom-call | bytes 1576960 | tf_op jit(solution)/shard_map/pallas_call | solution.py:357
  71.2 0.8 %shard_map.101 = (bf16[2,64,2048]{2,1,0:T(8,128)(2,1)}, bf16[2,64,2048]{2,1,0:T(8,128)(2,1)}, f32[8,128]{1,0:T(8,128)S(1)}) custom-call(f32[256,128]{1,0:T(8,128)S(1)} %get-tuple-element.119.refs_0_, f32[256,128]{1,0:T(8,128)S(1)} %collective-permute-done.18.refs_15_.refs_1_, ...), custom_call_target="tpu_custom_call", output_to_operand_aliasing={{0}: (4, {}), {1}: (5, {})} | custom-call | bytes 2625536 | tf_op jit(solution)/shard_map/pallas_call | solution.py:357
  72.0 0.9 %collective-permute-start.28 = (f32[32,128]{1,0:T(8,128)S(1)}, f32[32,128]{1,0:T(8,128)S(1)}, u32[]{:S(2)}, u32[]{:S(2)}) collective-permute-start(f32[32,128]{1,0:T(8,128)S(1)} %get-tuple-element.137), channel_id=1, source_target_pairs={{0,1},{1,0},{2,3},{3,2},{4,5},{5,4},{6,7},{7,6},{8,9},{9,8},{10,11... | collective-permute-start | bytes 49160 | tf_op jit(solution)/shard_map/ppermute | solution.py:532
  72.9 0.8 shard_map.102
  73.7 3.5 %collective-permute-done.23.refs_3_ = f32[320,128]{1,0:T(8,128)S(1)} collective-permute-done((f32[320,128]{1,0:T(8,128)S(1)}, f32[320,128]{1,0:T(8,128)S(1)}, u32[]{:S(2)}, u32[]{:S(2)}) %collective-permute-start.23) | collective-permute-done | bytes 163872 | tf_op jit(solution)/shard_map/ppermute | solution.py:344
  77.3 0.8 shard_map.103
  78.5 0.6 pad_maximum_fusion
  (48 shorter events, 2.9 us)
Async XLA Ops:
  0.6 7.2 %copy-start = (bf16[2,64,2048]{2,1,0:T(8,128)(2,1)S(1)}, bf16[2,64,2048]{2,1,0:T(8,128)(2,1)}, u32[]{:S(2)}) copy-start(bf16[2,64,2048]{2,1,0:T(8,128)(2,1)} %refs_0_.3) | copy-start | bytes 1572868
  0.6 7.2 %copy-start.1 = (bf16[2,64,2048]{2,1,0:T(8,128)(2,1)S(1)}, bf16[2,64,2048]{2,1,0:T(8,128)(2,1)}, u32[]{:S(2)}) copy-start(bf16[2,64,2048]{2,1,0:T(8,128)(2,1)} %refs_1_.3) | copy-start | bytes 1572868
  0.7 7.2 %copy-start.3 = (bf16[2,64,128]{2,1,0:T(8,128)(2,1)S(1)}, bf16[2,64,128]{2,1,0:T(8,128)(2,1)}, u32[]{:S(2)}) copy-start(bf16[2,64,128]{2,1,0:T(8,128)(2,1)} %refs_2_.3) | copy-start | bytes 98308
  0.7 7.2 %copy-start.4 = (bf16[2,64,128]{2,1,0:T(8,128)(2,1)S(1)}, bf16[2,64,128]{2,1,0:T(8,128)(2,1)}, u32[]{:S(2)}) copy-start(bf16[2,64,128]{2,1,0:T(8,128)(2,1)} %refs_3_.3) | copy-start | bytes 98308
  0.7 7.2 %copy-start.5 = (f32[2,32,64]{2,1,0:T(8,128)S(1)}, f32[2,32,64]{2,1,0:T(8,128)}, u32[]{:S(2)}) copy-start(f32[2,32,64]{2,1,0:T(8,128)} %refs_4_.3) | copy-start | bytes 49156
  3.2 12.6 %collective-permute-start.4 = (f32[648,128]{1,0:T(8,128)}, f32[648,128]{1,0:T(8,128)S(1)}, u32[]{:S(2)}, u32[]{:S(2)}) collective-permute-start(f32[648,128]{1,0:T(8,128)} %get-tuple-element.76), channel_id=1, source_target_pairs={{0,4},{2,6},{4,0},{6,2},{8,12},{10,14},{12,8},{14,10},{16,20},{18,... | collective-permute-start | bytes 995336 | tf_op jit(solution)/shard_map/ppermute | solution.py:338
  6.3 1.6 %copy-start.6 = (f32[32]{0:T(128)S(1)}, f32[32]{0:T(128)}, u32[]{:S(2)}) copy-start(f32[32]{0:T(128)} %param.10) | copy-start | bytes 388
  6.3 10.9 %collective-permute-start.5 = (f32[648,128]{1,0:T(8,128)}, f32[648,128]{1,0:T(8,128)S(1)}, u32[]{:S(2)}, u32[]{:S(2)}) collective-permute-start(f32[648,128]{1,0:T(8,128)} %get-tuple-element.77), channel_id=1, source_target_pairs={{0,2},{2,0},{4,6},{6,4},{8,10},{10,8},{12,14},{14,12},{16,18},{18,... | collective-permute-start | bytes 995336 | tf_op jit(solution)/shard_map/ppermute | solution.py:338
  7.8 16.1 %copy-start.2 = (f32[648,128]{1,0:T(8,128)S(1)}, f32[648,128]{1,0:T(8,128)}, u32[]{:S(2)}) copy-start(f32[648,128]{1,0:T(8,128)} %get-tuple-element.75.refs_0_) | copy-start | bytes 995332
  7.8 16.1 %collective-permute-start.6 = (f32[648,128]{1,0:T(8,128)}, f32[648,128]{1,0:T(8,128)S(1)}, u32[]{:S(2)}, u32[]{:S(2)}) collective-permute-start(f32[648,128]{1,0:T(8,128)} %get-tuple-element.78), channel_id=1, source_target_pairs={{0,6},{2,4},{4,2},{6,0},{8,14},{10,12},{12,10},{14,8},{16,22},{18,... | collective-permute-start | bytes 995336 | tf_op jit(solution)/shard_map/ppermute | solution.py:338
  8.2 20.2 %collective-permute-start = (f32[520,128]{1,0:T(8,128)S(1)}, f32[520,128]{1,0:T(8,128)S(1)}, u32[]{:S(2)}, u32[]{:S(2)}) collective-permute-start(f32[520,128]{1,0:T(8,128)S(1)} %get-tuple-element.71), channel_id=1, source_target_pairs={{0,1},{1,0},{2,3},{3,2},{4,5},{5,4},{6,7},{7,6},{8,9},{9,8},{10,11... | collective-permute-start | bytes 798728 | tf_op jit(solution)/shard_map/ppermute | solution.py:344
  8.3 20.1 %collective-permute-start.1 = (f32[520,128]{1,0:T(8,128)S(1)}, f32[520,128]{1,0:T(8,128)S(1)}, u32[]{:S(2)}, u32[]{:S(2)}) collective-permute-start(f32[520,128]{1,0:T(8,128)S(1)} %get-tuple-element.72), channel_id=1, source_target_pairs={{0,5},{1,4},{2,7},{3,6},{4,1},{5,0},{6,3},{7,2},{8,13},{9,12},{10,... | collective-permute-start | bytes 798728 | tf_op jit(solution)/shard_map/ppermute | solution.py:344
  15.8 13.3 %collective-permute-start.2 = (f32[520,128]{1,0:T(8,128)S(1)}, f32[520,128]{1,0:T(8,128)S(1)}, u32[]{:S(2)}, u32[]{:S(2)}) collective-permute-start(f32[520,128]{1,0:T(8,128)S(1)} %get-tuple-element.73), channel_id=1, source_target_pairs={{0,3},{1,2},{2,1},{3,0},{4,7},{5,6},{6,5},{7,4},{8,11},{9,10},{10,... | collective-permute-start | bytes 798728 | tf_op jit(solution)/shard_map/ppermute | solution.py:344
  17.2 16.1 %collective-permute-start.3 = (f32[520,128]{1,0:T(8,128)S(1)}, f32[520,128]{1,0:T(8,128)S(1)}, u32[]{:S(2)}, u32[]{:S(2)}) collective-permute-start(f32[520,128]{1,0:T(8,128)S(1)} %get-tuple-element.74), channel_id=1, source_target_pairs={{0,7},{1,6},{2,5},{3,4},{4,3},{5,2},{6,1},{7,0},{8,15},{9,14},{10,... | collective-permute-start | bytes 798728 | tf_op jit(solution)/shard_map/ppermute | solution.py:344
  24.9 11.9 %collective-permute-start.7 = (f32[136,512]{1,0:T(8,128)S(1)}, f32[136,512]{1,0:T(8,128)S(1)}, u32[]{:S(2)}, u32[]{:S(2)}) collective-permute-start(f32[136,512]{1,0:T(8,128)S(1)} %get-tuple-element.99.refs_0_), channel_id=1, source_target_pairs={{0,8},{2,10},{4,12},{6,14},{8,0},{10,2},{12,4},{14,6},{16,24},{18,... | collective-permute-start | bytes 835592 | tf_op jit(solution)/shard_map/ppermute | solution.py:444
  34.4 9.2 %collective-permute-start.10 = (f32[136,512]{1,0:T(8,128)S(1)}, f32[136,512]{1,0:T(8,128)S(1)}, u32[]{:S(2)}, u32[]{:S(2)}) collective-permute-start(f32[136,512]{1,0:T(8,128)S(1)} %get-tuple-element.101.refs_3_.refs_0_), channel_id=1, source_target_pairs={{0,8},{2,10},{4,12},{6,14},{8,0},{10,2},{12,4},{14,6},{16,24},{18,... | collective-permute-start | bytes 835592 | tf_op jit(solution)/shard_map/ppermute | solution.py:444
  36.9 8.6 %collective-permute-start.8 = (f32[128,512]{1,0:T(8,128)S(1)}, f32[128,512]{1,0:T(8,128)S(1)}, u32[]{:S(2)}, u32[]{:S(2)}) collective-permute-start(f32[128,512]{1,0:T(8,128)S(1)} %shard_map.92.refs_10_), channel_id=1, source_target_pairs={{0,0},{2,2},{4,4},{6,6},{8,16},{10,18},{12,20},{14,22},{16,8},{18,... | collective-permute-start | bytes 786440 | tf_op jit(solution)/shard_map/ppermute | solution.py:457
  38.2 10.7 %collective-permute-start.12 = (f32[256,128]{1,0:T(8,128)S(1)}, f32[256,128]{1,0:T(8,128)S(1)}, u32[]{:S(2)}, u32[]{:S(2)}) collective-permute-start(f32[256,128]{1,0:T(8,128)S(1)} %get-tuple-element.108), channel_id=1, source_target_pairs={{0,4},{2,6},{4,0},{6,2},{8,12},{10,14},{12,8},{14,10},{16,20},{18,... | collective-permute-start | bytes 393224 | tf_op jit(solution)/shard_map/ppermute | solution.py:338
  39.3 9.7 %collective-permute-start.13 = (f32[256,128]{1,0:T(8,128)S(1)}, f32[256,128]{1,0:T(8,128)S(1)}, u32[]{:S(2)}, u32[]{:S(2)}) collective-permute-start(f32[256,128]{1,0:T(8,128)S(1)} %get-tuple-element.109), channel_id=1, source_target_pairs={{0,2},{2,0},{4,6},{6,4},{8,10},{10,8},{12,14},{14,12},{16,18},{18,... | collective-permute-start | bytes 393224 | tf_op jit(solution)/shard_map/ppermute | solution.py:338
  44.3 7.7 %collective-permute-start.11 = (f32[320,128]{1,0:T(8,128)S(1)}, f32[320,128]{1,0:T(8,128)S(1)}, u32[]{:S(2)}, u32[]{:S(2)}) collective-permute-start(f32[320,128]{1,0:T(8,128)S(1)} %get-tuple-element.105), channel_id=1, source_target_pairs={{0,5},{1,4},{2,7},{3,6},{4,1},{5,0},{6,3},{7,2},{8,13},{9,12},{10,... | collective-permute-start | bytes 491528 | tf_op jit(solution)/shard_map/ppermute | solution.py:344
  45.5 9.8 %collective-permute-start.9 = (f32[128,512]{1,0:T(8,128)S(1)}, f32[128,512]{1,0:T(8,128)S(1)}, u32[]{:S(2)}, u32[]{:S(2)}) collective-permute-start(f32[128,512]{1,0:T(8,128)S(1)} %shard_map.93), channel_id=1, source_target_pairs={{0,8},{2,10},{4,12},{6,14},{8,0},{10,2},{12,4},{14,6},{16,24},{18,... | collective-permute-start | bytes 786440 | tf_op jit(solution)/shard_map/ppermute | solution.py:457
  49.0 12.2 %collective-permute-start.14 = (f32[128,512]{1,0:T(8,128)S(1)}, f32[128,512]{1,0:T(8,128)S(1)}, u32[]{:S(2)}, u32[]{:S(2)}) collective-permute-start(f32[128,512]{1,0:T(8,128)S(1)} %shard_map.98), channel_id=1, source_target_pairs={{0,0},{2,2},{4,4},{6,6},{8,16},{10,18},{12,20},{14,22},{16,8},{18,... | collective-permute-start | bytes 786440 | tf_op jit(solution)/shard_map/ppermute | solution.py:448
  49.7 7.9 %collective-permute-start.16 = (f32[320,128]{1,0:T(8,128)S(1)}, f32[320,128]{1,0:T(8,128)S(1)}, u32[]{:S(2)}, u32[]{:S(2)}) collective-permute-start(f32[320,128]{1,0:T(8,128)S(1)} %get-tuple-element.110), channel_id=1, source_target_pairs={{0,3},{1,2},{2,1},{3,0},{4,7},{5,6},{6,5},{7,4},{8,11},{9,10},{10,... | collective-permute-start | bytes 491528 | tf_op jit(solution)/shard_map/ppermute | solution.py:344
  50.4 9.7 %collective-permute-start.17 = (f32[320,128]{1,0:T(8,128)S(1)}, f32[320,128]{1,0:T(8,128)S(1)}, u32[]{:S(2)}, u32[]{:S(2)}) collective-permute-start(f32[320,128]{1,0:T(8,128)S(1)} %get-tuple-element.111), channel_id=1, source_target_pairs={{0,7},{1,6},{2,5},{3,4},{4,3},{5,2},{6,1},{7,0},{8,15},{9,14},{10,... | collective-permute-start | bytes 491528 | tf_op jit(solution)/shard_map/ppermute | solution.py:344
  52.0 12.4 %collective-permute-start.15 = (f32[128,512]{1,0:T(8,128)S(1)}, f32[128,512]{1,0:T(8,128)S(1)}, u32[]{:S(2)}, u32[]{:S(2)}) collective-permute-start(f32[128,512]{1,0:T(8,128)S(1)} %shard_map.98), channel_id=1, source_target_pairs={{8,24},{10,26},{12,28},{14,30},{16,0},{18,2},{20,4},{22,6},{9,25},... | collective-permute-start | bytes 786440 | tf_op jit(solution)/shard_map/ppermute | solution.py:448
  56.0 8.4 %collective-permute-start.18 = (f32[256,128]{1,0:T(8,128)S(1)}, f32[256,128]{1,0:T(8,128)S(1)}, u32[]{:S(2)}, u32[]{:S(2)}) collective-permute-start(f32[256,128]{1,0:T(8,128)S(1)} %get-tuple-element.112), channel_id=1, source_target_pairs={{0,4},{2,6},{4,0},{6,2},{8,12},{10,14},{12,8},{14,10},{16,20},{18,... | collective-permute-start | bytes 393224 | tf_op jit(solution)/shard_map/ppermute | solution.py:338
  57.5 6.8 %collective-permute-start.19 = (f32[256,128]{1,0:T(8,128)S(1)}, f32[256,128]{1,0:T(8,128)S(1)}, u32[]{:S(2)}, u32[]{:S(2)}) collective-permute-start(f32[256,128]{1,0:T(8,128)S(1)} %get-tuple-element.113), channel_id=1, source_target_pairs={{0,2},{2,0},{4,6},{6,4},{8,10},{10,8},{12,14},{14,12},{16,18},{18,... | collective-permute-start | bytes 393224 | tf_op jit(solution)/shard_map/ppermute | solution.py:338
  60.1 7.2 %collective-permute-start.26 = (f32[256,128]{1,0:T(8,128)S(1)}, f32[256,128]{1,0:T(8,128)S(1)}, u32[]{:S(2)}, u32[]{:S(2)}) collective-permute-start(f32[256,128]{1,0:T(8,128)S(1)} %get-tuple-element.122), channel_id=1, source_target_pairs={{0,6},{2,4},{4,2},{6,0},{8,14},{10,12},{12,10},{14,8},{16,22},{18,... | collective-permute-start | bytes 393224 | tf_op jit(solution)/shard_map/ppermute | solution.py:338
  61.2 8.6 %collective-permute-start.25 = (f32[256,128]{1,0:T(8,128)S(1)}, f32[256,128]{1,0:T(8,128)S(1)}, u32[]{:S(2)}, u32[]{:S(2)}) collective-permute-start(f32[256,128]{1,0:T(8,128)S(1)} %get-tuple-element.120), channel_id=1, source_target_pairs={{0,6},{2,4},{4,2},{6,0},{8,14},{10,12},{12,10},{14,8},{16,22},{18,... | collective-permute-start | bytes 393224 | tf_op jit(solution)/shard_map/ppermute | solution.py:338
  64.4 7.7 %collective-permute-start.24 = (f32[320,128]{1,0:T(8,128)S(1)}, f32[320,128]{1,0:T(8,128)S(1)}, u32[]{:S(2)}, u32[]{:S(2)}) collective-permute-start(f32[320,128]{1,0:T(8,128)S(1)} %get-tuple-element.118), channel_id=1, source_target_pairs={{0,1},{1,0},{2,3},{3,2},{4,5},{5,4},{6,7},{7,6},{8,9},{9,8},{10,11... | collective-permute-start | bytes 491528 | tf_op jit(solution)/shard_map/ppermute | solution.py:344
  65.0 8.7 %collective-permute-start.20 = (f32[320,128]{1,0:T(8,128)S(1)}, f32[320,128]{1,0:T(8,128)S(1)}, u32[]{:S(2)}, u32[]{:S(2)}) collective-permute-start(f32[320,128]{1,0:T(8,128)S(1)} %get-tuple-element.114), channel_id=1, source_target_pairs={{0,1},{1,0},{2,3},{3,2},{4,5},{5,4},{6,7},{7,6},{8,9},{9,8},{10,11... | collective-permute-start | bytes 491528 | tf_op jit(solution)/shard_map/ppermute | solution.py:344
  65.6 8.1 %collective-permute-start.21 = (f32[320,128]{1,0:T(8,128)S(1)}, f32[320,128]{1,0:T(8,128)S(1)}, u32[]{:S(2)}, u32[]{:S(2)}) collective-permute-start(f32[320,128]{1,0:T(8,128)S(1)} %get-tuple-element.115), channel_id=1, source_target_pairs={{0,5},{1,4},{2,7},{3,6},{4,1},{5,0},{6,3},{7,2},{8,13},{9,12},{10,... | collective-permute-start | bytes 491528 | tf_op jit(solution)/shard_map/ppermute | solution.py:344
  67.3 6.5 %collective-permute-start.22 = (f32[320,128]{1,0:T(8,128)S(1)}, f32[320,128]{1,0:T(8,128)S(1)}, u32[]{:S(2)}, u32[]{:S(2)}) collective-permute-start(f32[320,128]{1,0:T(8,128)S(1)} %get-tuple-element.116), channel_id=1, source_target_pairs={{0,3},{1,2},{2,1},{3,0},{4,7},{5,6},{6,5},{7,4},{8,11},{9,10},{10,... | collective-permute-start | bytes 491528 | tf_op jit(solution)/shard_map/ppermute | solution.py:344
  69.8 7.4 %collective-permute-start.23 = (f32[320,128]{1,0:T(8,128)S(1)}, f32[320,128]{1,0:T(8,128)S(1)}, u32[]{:S(2)}, u32[]{:S(2)}) collective-permute-start(f32[320,128]{1,0:T(8,128)S(1)} %get-tuple-element.117), channel_id=1, source_target_pairs={{0,7},{1,6},{2,5},{3,4},{4,3},{5,2},{6,1},{7,0},{8,15},{9,14},{10,... | collective-permute-start | bytes 491528 | tf_op jit(solution)/shard_map/ppermute | solution.py:344
  72.0 6.1 %collective-permute-start.28 = (f32[32,128]{1,0:T(8,128)S(1)}, f32[32,128]{1,0:T(8,128)S(1)}, u32[]{:S(2)}, u32[]{:S(2)}) collective-permute-start(f32[32,128]{1,0:T(8,128)S(1)} %get-tuple-element.137), channel_id=1, source_target_pairs={{0,1},{1,0},{2,3},{3,2},{4,5},{5,4},{6,7},{7,6},{8,9},{9,8},{10,11... | collective-permute-start | bytes 49160 | tf_op jit(solution)/shard_map/ppermute | solution.py:532
  77.2 1.2 %collective-permute-start.27 = (f32[32,128]{1,0:T(8,128)S(1)}, f32[32,128]{1,0:T(8,128)S(1)}, u32[]{:S(2)}, u32[]{:S(2)}) collective-permute-start(f32[32,128]{1,0:T(8,128)S(1)} %get-tuple-element.133), channel_id=1, source_target_pairs={{0,1},{1,0},{2,3},{3,2},{4,5},{5,4},{6,7},{7,6},{8,9},{9,8},{10,11... | collective-permute-start | bytes 49160 | tf_op jit(solution)/shard_map/ppermute | solution.py:532

commit v5 on v4

--- a/solution.py
+++ b/solution.py
@@ -77,7 +77,7 @@
     upto = lax.broadcasted_iota(jnp.int32, (rows, rows), 0) <= lax.broadcasted_iota(
         jnp.int32, (rows, rows), 1
     )
-    for copy in copies:
+    for copy in copies[:-4]:
         copy.wait()
     count = skip.shape[1]
     own = lax.broadcasted_iota(jnp.int32, (count, count), 0) == lax.broadcasted_iota(
@@ -94,10 +94,6 @@
     held = jnp.concatenate([logcum, jnp.broadcast_to(skips, logcum.shape)], axis=1)
     for piece, d in zip(pieces, partners(g)):
         to = lax.bitwise_xor(mine, d)
-        for k in range(tiles):
-            lanes = pl.ds(pl.multiple_of((to * tiles + k) * LANES, LANES), LANES)
-            piece[k * rows : (k + 1) * rows, :] = v_now[:, lanes].astype(F32)
-            piece[(tiles + k) * rows : (tiles + k + 1) * rows, :] = dy_now[:, lanes].astype(F32)
         part = held[:heads]
         for j in range(1, g):
             part = jnp.where(to == j, held[j * heads : (j + 1) * heads], part)
@@ -108,6 +104,15 @@
         if shared:
             piece[end + EXTRA : end + EXTRA + rows, :] = b_now[...].astype(F32)
             piece[end + EXTRA + rows : end + EXTRA + 2 * rows, :] = c_now[...].astype(F32)
+    for w, now in enumerate((v_now, dy_now)):
+        for copy in copies[len(copies) - 4 + 2 * w :][:2]:
+            copy.wait()
+        for piece, d in zip(pieces, partners(g)):
+            to = lax.bitwise_xor(mine, d)
+            for k in range(tiles):
+                lanes = pl.ds(pl.multiple_of((to * tiles + k) * LANES, LANES), LANES)
+                at = (w * tiles + k) * rows
+                piece[at : at + rows, :] = now[:, lanes].astype(F32)
 
 
 def gather_kernel(dims, shared, *refs):
@@ -289,20 +294,18 @@
     mine, core, _ = place(g)
     seq = 1 - core if last_part else core
     forward, _ = halves_of(dims, windows, half)
-    for piece, d in zip(pieces, partners(g)):
-        come = lax.bitwise_xor(mine, d)
-        for k in range(tiles):
-            lanes = pl.ds(pl.multiple_of((come * tiles + k) * LANES, LANES), LANES)
-            now[:, lanes] = piece[k * rows : (k + 1) * rows, :].astype(BF16)
+    width = tiles * LANES
 
     def send(whole):
-        part = now.shape[1] // 4
         copies = []
-        for k in range(4):
-            lanes = pl.ds(k * part, part)
-            copies.append(pltpu.make_async_copy(now.at[:, lanes], whole.at[seq, :, lanes], sent.at[k]))
-        for copy in copies:
-            copy.start()
+        for n, (piece, d) in enumerate(zip(pieces, partners(g))):
+            come = lax.bitwise_xor(mine, d)
+            for k in range(tiles):
+                lanes = pl.ds(pl.multiple_of(come * width + k * LANES, LANES), LANES)
+                now[:, lanes] = piece[k * rows : (k + 1) * rows, :].astype(BF16)
+            lanes = pl.ds(pl.multiple_of(come * width, width), width)
+            copies.append(pltpu.make_async_copy(now.at[:, lanes], whole.at[seq, :, lanes], sent.at[n]))
+            copies[-1].start()
         for copy in copies:
             copy.wait()
 
@@ -522,7 +525,7 @@
             functools.partial(unpack_kernel, dims, windows, half, n == 1, marked),
             [shape(seqs, rows, wide, dtype=BF16)] * 2 + [shape(8, LANES)] * marked,
             back[n, half] + outs,
-            [pltpu.VMEM((rows, wide), BF16), pltpu.SemaphoreType.DMA((4,))],
+            [pltpu.VMEM((rows, wide), BF16), pltpu.SemaphoreType.DMA((g,))],
             far=(g, g + 1),
             far_out=(0, 1),
             aliases={g: 0, g + 1: 1} if outs else {},

time: 80.2 us -> 80.1 us (level)
  no operation moved by 1% of the time
where the time goes in v5:
time: 80.1 us; the launch traced here: 79.1 us
  starting transfers between devices  34.6 us (43%)
  waiting for transfers between devices  27 us (34%)
  Pallas kernels  15.9 us (20%)
  between operations  0.96 us (1%)
    pallas_call x21, Pallas kernels, call(): pl.pallas_call(body, out_shape=out, in_specs=[hbm if n in far else vmem f...  15.9 us
    ppermute x9, starting transfers between devices, same(): return lax.ppermute(piece, 'seq', [(i, i ^ d) for i in range(blocks)])  13 us
    ppermute x9, waiting for transfers between devices, same(): return lax.ppermute(piece, 'seq', [(i, i ^ d) for i in range(blocks)])  12.9 us
    ppermute x12, starting transfers between devices, cross(): return lax.ppermute(piece, ('seq', 'head'), perm)  10.8 us
    ppermute x12, waiting for transfers between devices, cross(): return lax.ppermute(piece, ('seq', 'head'), perm)  9.57 us
    ppermute x2, starting transfers between devices, step(): state[n].append(lax.ppermute(moved[0], 'seq', middle if k == 1 else near))  4.17 us
    ppermute x2, starting transfers between devices, meet(): state[n] = [lax.ppermute(ends[n][0], 'seq', near)]  3.73 us
    ppermute x2, waiting for transfers between devices, step(): state[n].append(lax.ppermute(moved[0], 'seq', middle if k == 1 else near))  2.07 us
  transfers between devices with their start and end apart: 29, of which 13 were waited for; matrix products, arithmetic and copies ran while one was open for 0% of the time, Pallas kernels for 17%

profile of v5, /device:TPU:0, one launch (start us, length us, event | category | flops | bytes accessed | tf_op | source)
XLA Modules:
  0.0 79.1 jit_solution(15491714796362031699)
XLA Ops:
  0.7 2.5 %shard_map.86 = (f32[648,128]{1,0:T(8,128)}, f32[648,128]{1,0:T(8,128)}, f32[648,128]{1,0:T(8,128)}, f32[648,128]{1,0:T(8,128)}) custom-call(bf16[2,64,2048]{2,1,0:T(8,128)(2,1)} %refs_0_.3, bf16[2,64,2048]{2,1,0:T(8,128)(2,1)} %refs_1_.3, bf16[2,64,128]{2,1,0:T(8,128)(2,1)} %refs_2_.3, bf16[2,64,128]{2,1,0:T(8,128)(2,1)} %refs_3_.3, f32[2,32,64]{2,1,0:T(8,128)} %refs_4_.3, ...), custom_call_target="tpu_custom_call" | custom-call | bytes 2457728 | tf_op jit(solution)/shard_map/pallas_call | solution.py:360
  3.1 3.0 %collective-permute-start.4 = (f32[648,128]{1,0:T(8,128)}, f32[648,128]{1,0:T(8,128)S(1)}, u32[]{:S(2)}, u32[]{:S(2)}) collective-permute-start(f32[648,128]{1,0:T(8,128)} %get-tuple-element.76), channel_id=1, source_target_pairs={{0,4},{2,6},{4,0},{6,2},{8,12},{10,14},{12,8},{14,10},{16,20},{18,... | collective-permute-start | bytes 995336 | tf_op jit(solution)/shard_map/ppermute | solution.py:341
  6.2 1.5 %collective-permute-start.5 = (f32[648,128]{1,0:T(8,128)}, f32[648,128]{1,0:T(8,128)S(1)}, u32[]{:S(2)}, u32[]{:S(2)}) collective-permute-start(f32[648,128]{1,0:T(8,128)} %get-tuple-element.77), channel_id=1, source_target_pairs={{0,2},{2,0},{4,6},{6,4},{8,10},{10,8},{12,14},{14,12},{16,18},{18,... | collective-permute-start | bytes 995336 | tf_op jit(solution)/shard_map/ppermute | solution.py:341
  8.3 2.1 %collective-permute-start.1 = (f32[520,128]{1,0:T(8,128)S(1)}, f32[520,128]{1,0:T(8,128)S(1)}, u32[]{:S(2)}, u32[]{:S(2)}) collective-permute-start(f32[520,128]{1,0:T(8,128)S(1)} %get-tuple-element.72), channel_id=1, source_target_pairs={{0,5},{1,4},{2,7},{3,6},{4,1},{5,0},{6,3},{7,2},{8,13},{9,12},{10,... | collective-permute-start | bytes 798728 | tf_op jit(solution)/shard_map/ppermute | solution.py:347
  10.4 5.3 %collective-permute-done.4.refs_1_ = f32[648,128]{1,0:T(8,128)S(1)} collective-permute-done((f32[648,128]{1,0:T(8,128)}, f32[648,128]{1,0:T(8,128)S(1)}, u32[]{:S(2)}, u32[]{:S(2)}) %collective-permute-start.4) | collective-permute-done | bytes 331808 | tf_op jit(solution)/shard_map/ppermute | solution.py:341
  15.7 1.4 %collective-permute-done.5.refs_2_ = f32[648,128]{1,0:T(8,128)S(1)} collective-permute-done((f32[648,128]{1,0:T(8,128)}, f32[648,128]{1,0:T(8,128)S(1)}, u32[]{:S(2)}, u32[]{:S(2)}) %collective-permute-start.5) | collective-permute-done | bytes 331808 | tf_op jit(solution)/shard_map/ppermute | solution.py:341
  17.1 2.6 %collective-permute-start.3 = (f32[520,128]{1,0:T(8,128)S(1)}, f32[520,128]{1,0:T(8,128)S(1)}, u32[]{:S(2)}, u32[]{:S(2)}) collective-permute-start(f32[520,128]{1,0:T(8,128)S(1)} %get-tuple-element.74), channel_id=1, source_target_pairs={{0,7},{1,6},{2,5},{3,4},{4,3},{5,2},{6,1},{7,0},{8,15},{9,14},{10,... | collective-permute-start | bytes 798728 | tf_op jit(solution)/shard_map/ppermute | solution.py:347
  19.7 4.1 %collective-permute-done.6.refs_3_ = f32[648,128]{1,0:T(8,128)S(1)} collective-permute-done((f32[648,128]{1,0:T(8,128)}, f32[648,128]{1,0:T(8,128)S(1)}, u32[]{:S(2)}, u32[]{:S(2)}) %collective-permute-start.6) | collective-permute-done | bytes 331808 | tf_op jit(solution)/shard_map/ppermute | solution.py:341
  23.8 1.1 %shard_map.87 = (bf16[256,512]{1,0:T(8,128)(2,1)S(1)}, bf16[256,512]{1,0:T(8,128)(2,1)S(1)}, f32[8,256]{1,0:T(8,128)S(1)}, f32[8,512]{1,0:T(8,128)S(1)}, bf16[25...) custom-call(f32[648,128]{1,0:T(8,128)S(1)} %copy-done.2, ...), custom_call_target="tpu_custom_call" | custom-call | bytes 2547712 | tf_op jit(solution)/shard_map/pallas_call | solution.py:360
  24.9 2.1 %collective-permute-start.7 = (f32[136,512]{1,0:T(8,128)S(1)}, f32[136,512]{1,0:T(8,128)S(1)}, u32[]{:S(2)}, u32[]{:S(2)}) collective-permute-start(f32[136,512]{1,0:T(8,128)S(1)} %get-tuple-element.99.refs_0_), channel_id=1, source_target_pairs={{0,8},{2,10},{4,12},{6,14},{8,0},{10,2},{12,4},{14,6},{16,24},{18,... | collective-permute-start | bytes 835592 | tf_op jit(solution)/shard_map/ppermute | solution.py:447
  26.9 1.4 %shard_map.88 = (f32[256,512]{1,0:T(8,128)S(1)}, f32[256,512]{1,0:T(8,128)S(1)}, f32[256,128]{1,0:T(8,128)S(1)}, f32[256,128]{1,0:T(8,128)S(1)}) custom-call(bf16[256,512]{1,0:T(8,128)(2,1)S(1)} %get-tuple-element.81.refs_0_, bf16[256,512]{1,0:T(8,128)(2,1)S(1)} %get-tuple-element.82.refs_1_, f32[8,256]{1,0:T(8,128)S(1)} %get-tuple-element.83.refs_2_.refs_0_, ...), custom_call_target="tpu_custom_call" | custom-call | bytes 1990656 | tf_op jit(solution)/shard_map/pallas_call | solution.py:360
  29.0 4.2 %collective-permute-done.3.refs_3_ = f32[520,128]{1,0:T(8,128)S(1)} collective-permute-done((f32[520,128]{1,0:T(8,128)S(1)}, f32[520,128]{1,0:T(8,128)S(1)}, u32[]{:S(2)}, u32[]{:S(2)}) %collective-permute-start.3) | collective-permute-done | bytes 266272 | tf_op jit(solution)/shard_map/ppermute | solution.py:347
  33.2 1.1 %shard_map.89 = (bf16[256,512]{1,0:T(8,128)(2,1)S(1)}, bf16[256,512]{1,0:T(8,128)(2,1)S(1)}, f32[8,256]{1,0:T(8,128)S(1)}, f32[8,512]{1,0:T(8,128)S(1)}, bf16[25...) custom-call(f32[520,128]{1,0:T(8,128)S(1)} %collective-permute-done.refs_0_, ...), custom_call_target="tpu_custom_call" | custom-call | bytes 2285568 | tf_op jit(solution)/shard_map/pallas_call | solution.py:360
  34.3 1.6 %collective-permute-start.10 = (f32[136,512]{1,0:T(8,128)S(1)}, f32[136,512]{1,0:T(8,128)S(1)}, u32[]{:S(2)}, u32[]{:S(2)}) collective-permute-start(f32[136,512]{1,0:T(8,128)S(1)} %get-tuple-element.101.refs_3_.refs_0_), channel_id=1, source_target_pairs={{0,8},{2,10},{4,12},{6,14},{8,0},{10,2},{12,4},{14,6},{16,24},{18,... | collective-permute-start | bytes 835592 | tf_op jit(solution)/shard_map/ppermute | solution.py:447
  36.0 0.8 shard_map.91
  36.8 0.7 collective-permute-start.8
  37.5 0.7 shard_map.94
  38.1 1.0 %collective-permute-start.12 = (f32[256,128]{1,0:T(8,128)S(1)}, f32[256,128]{1,0:T(8,128)S(1)}, u32[]{:S(2)}, u32[]{:S(2)}) collective-permute-start(f32[256,128]{1,0:T(8,128)S(1)} %get-tuple-element.108), channel_id=1, source_target_pairs={{0,4},{2,6},{4,0},{6,2},{8,12},{10,14},{12,8},{14,10},{16,20},{18,... | collective-permute-start | bytes 393224 | tf_op jit(solution)/shard_map/ppermute | solution.py:341
  39.2 1.5 %collective-permute-start.13 = (f32[256,128]{1,0:T(8,128)S(1)}, f32[256,128]{1,0:T(8,128)S(1)}, u32[]{:S(2)}, u32[]{:S(2)}) collective-permute-start(f32[256,128]{1,0:T(8,128)S(1)} %get-tuple-element.109), channel_id=1, source_target_pairs={{0,2},{2,0},{4,6},{6,4},{8,10},{10,8},{12,14},{14,12},{16,18},{18,... | collective-permute-start | bytes 393224 | tf_op jit(solution)/shard_map/ppermute | solution.py:341
  40.7 0.8 shard_map.95
  41.4 1.4 %shard_map.90 = (f32[256,512]{1,0:T(8,128)S(1)}, f32[256,512]{1,0:T(8,128)S(1)}, f32[256,128]{1,0:T(8,128)S(1)}, f32[256,128]{1,0:T(8,128)S(1)}) custom-call(bf16[256,512]{1,0:T(8,128)(2,1)S(1)} %get-tuple-element.87.refs_0_, bf16[256,512]{1,0:T(8,128)(2,1)S(1)} %get-tuple-element.88.refs_1_, f32[8,256]{1,0:T(8,128)S(1)} %get-tuple-element.86.refs_2_.refs_0_, ...), custom_call_target="tpu_custom_call" | custom-call | bytes 1990656 | tf_op jit(solution)/shard_map/pallas_call | solution.py:360
  42.9 0.7 collective-permute-done.10.refs_10_.refs_2_
  43.6 0.7 shard_map.96
  44.2 1.1 %collective-permute-start.11 = (f32[320,128]{1,0:T(8,128)S(1)}, f32[320,128]{1,0:T(8,128)S(1)}, u32[]{:S(2)}, u32[]{:S(2)}) collective-permute-start(f32[320,128]{1,0:T(8,128)S(1)} %get-tuple-element.105), channel_id=1, source_target_pairs={{0,5},{1,4},{2,7},{3,6},{4,1},{5,0},{6,3},{7,2},{8,13},{9,12},{10,... | collective-permute-start | bytes 491528 | tf_op jit(solution)/shard_map/ppermute | solution.py:347
  45.4 3.5 %collective-permute-start.9 = (f32[128,512]{1,0:T(8,128)S(1)}, f32[128,512]{1,0:T(8,128)S(1)}, u32[]{:S(2)}, u32[]{:S(2)}) collective-permute-start(f32[128,512]{1,0:T(8,128)S(1)} %shard_map.93), channel_id=1, source_target_pairs={{0,8},{2,10},{4,12},{6,14},{8,0},{10,2},{12,4},{14,6},{16,24},{18,... | collective-permute-start | bytes 786440 | tf_op jit(solution)/shard_map/ppermute | solution.py:460
  48.9 0.7 collective-permute-start.14
  49.6 0.7 collective-permute-start.16
  50.3 1.6 %collective-permute-start.17 = (f32[320,128]{1,0:T(8,128)S(1)}, f32[320,128]{1,0:T(8,128)S(1)}, u32[]{:S(2)}, u32[]{:S(2)}) collective-permute-start(f32[320,128]{1,0:T(8,128)S(1)} %get-tuple-element.111), channel_id=1, source_target_pairs={{0,7},{1,6},{2,5},{3,4},{4,3},{5,2},{6,1},{7,0},{8,15},{9,14},{10,... | collective-permute-start | bytes 491528 | tf_op jit(solution)/shard_map/ppermute | solution.py:347
  51.9 1.3 %collective-permute-start.15 = (f32[128,512]{1,0:T(8,128)S(1)}, f32[128,512]{1,0:T(8,128)S(1)}, u32[]{:S(2)}, u32[]{:S(2)}) collective-permute-start(f32[128,512]{1,0:T(8,128)S(1)} %shard_map.98), channel_id=1, source_target_pairs={{8,24},{10,26},{12,28},{14,30},{16,0},{18,2},{20,4},{22,6},{9,25},... | collective-permute-start | bytes 786440 | tf_op jit(solution)/shard_map/ppermute | solution.py:451
  53.2 2.1 %collective-permute-done.9.refs_11_ = f32[128,512]{1,0:T(8,128)S(1)} collective-permute-done((f32[128,512]{1,0:T(8,128)S(1)}, f32[128,512]{1,0:T(8,128)S(1)}, u32[]{:S(2)}, u32[]{:S(2)}) %collective-permute-start.9) | collective-permute-done | bytes 262176 | tf_op jit(solution)/shard_map/ppermute | solution.py:460
  55.2 0.7 shard_map.97
  55.9 1.5 %collective-permute-start.18 = (f32[256,128]{1,0:T(8,128)S(1)}, f32[256,128]{1,0:T(8,128)S(1)}, u32[]{:S(2)}, u32[]{:S(2)}) collective-permute-start(f32[256,128]{1,0:T(8,128)S(1)} %get-tuple-element.112), channel_id=1, source_target_pairs={{0,4},{2,6},{4,0},{6,2},{8,12},{10,14},{12,8},{14,10},{16,20},{18,... | collective-permute-start | bytes 393224 | tf_op jit(solution)/shard_map/ppermute | solution.py:341
  57.5 1.4 %collective-permute-start.19 = (f32[256,128]{1,0:T(8,128)S(1)}, f32[256,128]{1,0:T(8,128)S(1)}, u32[]{:S(2)}, u32[]{:S(2)}) collective-permute-start(f32[256,128]{1,0:T(8,128)S(1)} %get-tuple-element.113), channel_id=1, source_target_pairs={{0,2},{2,0},{4,6},{6,4},{8,10},{10,8},{12,14},{14,12},{16,18},{18,... | collective-permute-start | bytes 393224 | tf_op jit(solution)/shard_map/ppermute | solution.py:341
  58.8 1.2 %collective-permute-done.17.refs_14_.refs_3_ = f32[320,128]{1,0:T(8,128)S(1)} collective-permute-done((f32[320,128]{1,0:T(8,128)S(1)}, f32[320,128]{1,0:T(8,128)S(1)}, u32[]{:S(2)}, u32[]{:S(2)}) %collective-permute-start.17) | collective-permute-done | bytes 163872 | tf_op jit(solution)/shard_map/ppermute | solution.py:347
  60.0 1.1 %collective-permute-start.26 = (f32[256,128]{1,0:T(8,128)S(1)}, f32[256,128]{1,0:T(8,128)S(1)}, u32[]{:S(2)}, u32[]{:S(2)}) collective-permute-start(f32[256,128]{1,0:T(8,128)S(1)} %get-tuple-element.122), channel_id=1, source_target_pairs={{0,6},{2,4},{4,2},{6,0},{8,14},{10,12},{12,10},{14,8},{16,22},{18,... | collective-permute-start | bytes 393224 | tf_op jit(solution)/shard_map/ppermute | solution.py:341
  61.1 1.8 %collective-permute-start.25 = (f32[256,128]{1,0:T(8,128)S(1)}, f32[256,128]{1,0:T(8,128)S(1)}, u32[]{:S(2)}, u32[]{:S(2)}) collective-permute-start(f32[256,128]{1,0:T(8,128)S(1)} %get-tuple-element.120), channel_id=1, source_target_pairs={{0,6},{2,4},{4,2},{6,0},{8,14},{10,12},{12,10},{14,8},{16,22},{18,... | collective-permute-start | bytes 393224 | tf_op jit(solution)/shard_map/ppermute | solution.py:341
  62.9 1.3 %collective-permute-done.15.refs_12_ = f32[128,512]{1,0:T(8,128)S(1)} collective-permute-done((f32[128,512]{1,0:T(8,128)S(1)}, f32[128,512]{1,0:T(8,128)S(1)}, u32[]{:S(2)}, u32[]{:S(2)}) %collective-permute-start.15) | collective-permute-done | bytes 262176 | tf_op jit(solution)/shard_map/ppermute | solution.py:451
  64.3 0.7 shard_map.99
  65.5 1.1 %collective-permute-start.21 = (f32[320,128]{1,0:T(8,128)S(1)}, f32[320,128]{1,0:T(8,128)S(1)}, u32[]{:S(2)}, u32[]{:S(2)}) collective-permute-start(f32[320,128]{1,0:T(8,128)S(1)} %get-tuple-element.115), channel_id=1, source_target_pairs={{0,5},{1,4},{2,7},{3,6},{4,1},{5,0},{6,3},{7,2},{8,13},{9,12},{10,... | collective-permute-start | bytes 491528 | tf_op jit(solution)/shard_map/ppermute | solution.py:347
  67.2 1.0 %collective-permute-start.22 = (f32[320,128]{1,0:T(8,128)S(1)}, f32[320,128]{1,0:T(8,128)S(1)}, u32[]{:S(2)}, u32[]{:S(2)}) collective-permute-start(f32[320,128]{1,0:T(8,128)S(1)} %get-tuple-element.116), channel_id=1, source_target_pairs={{0,3},{1,2},{2,1},{3,0},{4,7},{5,6},{6,5},{7,4},{8,11},{9,10},{10,... | collective-permute-start | bytes 491528 | tf_op jit(solution)/shard_map/ppermute | solution.py:347
  68.2 1.6 %collective-permute-done.25.refs_3_ = f32[256,128]{1,0:T(8,128)S(1)} collective-permute-done((f32[256,128]{1,0:T(8,128)S(1)}, f32[256,128]{1,0:T(8,128)S(1)}, u32[]{:S(2)}, u32[]{:S(2)}) %collective-permute-start.25) | collective-permute-done | bytes 131104 | tf_op jit(solution)/shard_map/ppermute | solution.py:341
  69.7 1.3 %shard_map.100 = (bf16[2,64,2048]{2,1,0:T(8,128)(2,1)}, bf16[2,64,2048]{2,1,0:T(8,128)(2,1)}, f32[8,128]{1,0:T(8,128)}) custom-call(f32[256,128]{1,0:T(8,128)S(1)} %get-tuple-element.121.refs_0_, f32[256,128]{1,0:T(8,128)S(1)} %collective-permute-done.12.refs_3_.refs_1_, f32[256,128]{1,0:T(8,128)S(1)} %collective-permute-done.13.refs_4_.refs_2_, ...), custom_call_target="tpu_custom_call" | custom-call | bytes 1576960 | tf_op jit(solution)/shard_map/pallas_call | solution.py:360
  71.1 0.8 shard_map.101
  71.9 0.9 %collective-permute-start.28 = (f32[32,128]{1,0:T(8,128)S(1)}, f32[32,128]{1,0:T(8,128)S(1)}, u32[]{:S(2)}, u32[]{:S(2)}) collective-permute-start(f32[32,128]{1,0:T(8,128)S(1)} %get-tuple-element.137), channel_id=1, source_target_pairs={{0,1},{1,0},{2,3},{3,2},{4,5},{5,4},{6,7},{7,6},{8,9},{9,8},{10,11... | collective-permute-start | bytes 49160 | tf_op jit(solution)/shard_map/ppermute | solution.py:535
  72.8 0.8 shard_map.102
  73.6 3.5 %collective-permute-done.23.refs_3_ = f32[320,128]{1,0:T(8,128)S(1)} collective-permute-done((f32[320,128]{1,0:T(8,128)S(1)}, f32[320,128]{1,0:T(8,128)S(1)}, u32[]{:S(2)}, u32[]{:S(2)}) %collective-permute-start.23) | collective-permute-done | bytes 163872 | tf_op jit(solution)/shard_map/ppermute | solution.py:347
  77.3 0.8 shard_map.103
  78.4 0.6 pad_maximum_fusion
  (48 shorter events, 3.1 us)
Async XLA Ops:
  0.6 7.1 %copy-start = (bf16[2,64,2048]{2,1,0:T(8,128)(2,1)S(1)}, bf16[2,64,2048]{2,1,0:T(8,128)(2,1)}, u32[]{:S(2)}) copy-start(bf16[2,64,2048]{2,1,0:T(8,128)(2,1)} %refs_0_.3) | copy-start | bytes 1572868
  0.6 7.1 %copy-start.1 = (bf16[2,64,2048]{2,1,0:T(8,128)(2,1)S(1)}, bf16[2,64,2048]{2,1,0:T(8,128)(2,1)}, u32[]{:S(2)}) copy-start(bf16[2,64,2048]{2,1,0:T(8,128)(2,1)} %refs_1_.3) | copy-start | bytes 1572868
  0.7 7.1 %copy-start.3 = (bf16[2,64,128]{2,1,0:T(8,128)(2,1)S(1)}, bf16[2,64,128]{2,1,0:T(8,128)(2,1)}, u32[]{:S(2)}) copy-start(bf16[2,64,128]{2,1,0:T(8,128)(2,1)} %refs_2_.3) | copy-start | bytes 98308
  0.7 7.1 %copy-start.4 = (bf16[2,64,128]{2,1,0:T(8,128)(2,1)S(1)}, bf16[2,64,128]{2,1,0:T(8,128)(2,1)}, u32[]{:S(2)}) copy-start(bf16[2,64,128]{2,1,0:T(8,128)(2,1)} %refs_3_.3) | copy-start | bytes 98308
  0.7 7.1 %copy-start.5 = (f32[2,32,64]{2,1,0:T(8,128)S(1)}, f32[2,32,64]{2,1,0:T(8,128)}, u32[]{:S(2)}) copy-start(f32[2,32,64]{2,1,0:T(8,128)} %refs_4_.3) | copy-start | bytes 49156
  3.1 12.6 %collective-permute-start.4 = (f32[648,128]{1,0:T(8,128)}, f32[648,128]{1,0:T(8,128)S(1)}, u32[]{:S(2)}, u32[]{:S(2)}) collective-permute-start(f32[648,128]{1,0:T(8,128)} %get-tuple-element.76), channel_id=1, source_target_pairs={{0,4},{2,6},{4,0},{6,2},{8,12},{10,14},{12,8},{14,10},{16,20},{18,... | collective-permute-start | bytes 995336 | tf_op jit(solution)/shard_map/ppermute | solution.py:341
  6.2 1.6 %copy-start.6 = (f32[32]{0:T(128)S(1)}, f32[32]{0:T(128)}, u32[]{:S(2)}) copy-start(f32[32]{0:T(128)} %param.10) | copy-start | bytes 388
  6.2 10.9 %collective-permute-start.5 = (f32[648,128]{1,0:T(8,128)}, f32[648,128]{1,0:T(8,128)S(1)}, u32[]{:S(2)}, u32[]{:S(2)}) collective-permute-start(f32[648,128]{1,0:T(8,128)} %get-tuple-element.77), channel_id=1, source_target_pairs={{0,2},{2,0},{4,6},{6,4},{8,10},{10,8},{12,14},{14,12},{16,18},{18,... | collective-permute-start | bytes 995336 | tf_op jit(solution)/shard_map/ppermute | solution.py:341
  7.7 16.1 %copy-start.2 = (f32[648,128]{1,0:T(8,128)S(1)}, f32[648,128]{1,0:T(8,128)}, u32[]{:S(2)}) copy-start(f32[648,128]{1,0:T(8,128)} %get-tuple-element.75.refs_0_) | copy-start | bytes 995332
  7.7 16.1 %collective-permute-start.6 = (f32[648,128]{1,0:T(8,128)}, f32[648,128]{1,0:T(8,128)S(1)}, u32[]{:S(2)}, u32[]{:S(2)}) collective-permute-start(f32[648,128]{1,0:T(8,128)} %get-tuple-element.78), channel_id=1, source_target_pairs={{0,6},{2,4},{4,2},{6,0},{8,14},{10,12},{12,10},{14,8},{16,22},{18,... | collective-permute-start | bytes 995336 | tf_op jit(solution)/shard_map/ppermute | solution.py:341
  8.3 20.1 %collective-permute-start = (f32[520,128]{1,0:T(8,128)S(1)}, f32[520,128]{1,0:T(8,128)S(1)}, u32[]{:S(2)}, u32[]{:S(2)}) collective-permute-start(f32[520,128]{1,0:T(8,128)S(1)} %get-tuple-element.71), channel_id=1, source_target_pairs={{0,1},{1,0},{2,3},{3,2},{4,5},{5,4},{6,7},{7,6},{8,9},{9,8},{10,11... | collective-permute-start | bytes 798728 | tf_op jit(solution)/shard_map/ppermute | solution.py:347
  8.3 20.0 %collective-permute-start.1 = (f32[520,128]{1,0:T(8,128)S(1)}, f32[520,128]{1,0:T(8,128)S(1)}, u32[]{:S(2)}, u32[]{:S(2)}) collective-permute-start(f32[520,128]{1,0:T(8,128)S(1)} %get-tuple-element.72), channel_id=1, source_target_pairs={{0,5},{1,4},{2,7},{3,6},{4,1},{5,0},{6,3},{7,2},{8,13},{9,12},{10,... | collective-permute-start | bytes 798728 | tf_op jit(solution)/shard_map/ppermute | solution.py:347
  15.7 13.3 %collective-permute-start.2 = (f32[520,128]{1,0:T(8,128)S(1)}, f32[520,128]{1,0:T(8,128)S(1)}, u32[]{:S(2)}, u32[]{:S(2)}) collective-permute-start(f32[520,128]{1,0:T(8,128)S(1)} %get-tuple-element.73), channel_id=1, source_target_pairs={{0,3},{1,2},{2,1},{3,0},{4,7},{5,6},{6,5},{7,4},{8,11},{9,10},{10,... | collective-permute-start | bytes 798728 | tf_op jit(solution)/shard_map/ppermute | solution.py:347
  17.1 16.1 %collective-permute-start.3 = (f32[520,128]{1,0:T(8,128)S(1)}, f32[520,128]{1,0:T(8,128)S(1)}, u32[]{:S(2)}, u32[]{:S(2)}) collective-permute-start(f32[520,128]{1,0:T(8,128)S(1)} %get-tuple-element.74), channel_id=1, source_target_pairs={{0,7},{1,6},{2,5},{3,4},{4,3},{5,2},{6,1},{7,0},{8,15},{9,14},{10,... | collective-permute-start | bytes 798728 | tf_op jit(solution)/shard_map/ppermute | solution.py:347
  24.9 11.9 %collective-permute-start.7 = (f32[136,512]{1,0:T(8,128)S(1)}, f32[136,512]{1,0:T(8,128)S(1)}, u32[]{:S(2)}, u32[]{:S(2)}) collective-permute-start(f32[136,512]{1,0:T(8,128)S(1)} %get-tuple-element.99.refs_0_), channel_id=1, source_target_pairs={{0,8},{2,10},{4,12},{6,14},{8,0},{10,2},{12,4},{14,6},{16,24},{18,... | collective-permute-start | bytes 835592 | tf_op jit(solution)/shard_map/ppermute | solution.py:447
  34.3 9.2 %collective-permute-start.10 = (f32[136,512]{1,0:T(8,128)S(1)}, f32[136,512]{1,0:T(8,128)S(1)}, u32[]{:S(2)}, u32[]{:S(2)}) collective-permute-start(f32[136,512]{1,0:T(8,128)S(1)} %get-tuple-element.101.refs_3_.refs_0_), channel_id=1, source_target_pairs={{0,8},{2,10},{4,12},{6,14},{8,0},{10,2},{12,4},{14,6},{16,24},{18,... | collective-permute-start | bytes 835592 | tf_op jit(solution)/shard_map/ppermute | solution.py:447
  36.8 8.6 %collective-permute-start.8 = (f32[128,512]{1,0:T(8,128)S(1)}, f32[128,512]{1,0:T(8,128)S(1)}, u32[]{:S(2)}, u32[]{:S(2)}) collective-permute-start(f32[128,512]{1,0:T(8,128)S(1)} %shard_map.92.refs_10_), channel_id=1, source_target_pairs={{0,0},{2,2},{4,4},{6,6},{8,16},{10,18},{12,20},{14,22},{16,8},{18,... | collective-permute-start | bytes 786440 | tf_op jit(solution)/shard_map/ppermute | solution.py:460
  38.1 10.7 %collective-permute-start.12 = (f32[256,128]{1,0:T(8,128)S(1)}, f32[256,128]{1,0:T(8,128)S(1)}, u32[]{:S(2)}, u32[]{:S(2)}) collective-permute-start(f32[256,128]{1,0:T(8,128)S(1)} %get-tuple-element.108), channel_id=1, source_target_pairs={{0,4},{2,6},{4,0},{6,2},{8,12},{10,14},{12,8},{14,10},{16,20},{18,... | collective-permute-start | bytes 393224 | tf_op jit(solution)/shard_map/ppermute | solution.py:341
  39.2 9.7 %collective-permute-start.13 = (f32[256,128]{1,0:T(8,128)S(1)}, f32[256,128]{1,0:T(8,128)S(1)}, u32[]{:S(2)}, u32[]{:S(2)}) collective-permute-start(f32[256,128]{1,0:T(8,128)S(1)} %get-tuple-element.109), channel_id=1, source_target_pairs={{0,2},{2,0},{4,6},{6,4},{8,10},{10,8},{12,14},{14,12},{16,18},{18,... | collective-permute-start | bytes 393224 | tf_op jit(solution)/shard_map/ppermute | solution.py:341
  44.2 7.7 %collective-permute-start.11 = (f32[320,128]{1,0:T(8,128)S(1)}, f32[320,128]{1,0:T(8,128)S(1)}, u32[]{:S(2)}, u32[]{:S(2)}) collective-permute-start(f32[320,128]{1,0:T(8,128)S(1)} %get-tuple-element.105), channel_id=1, source_target_pairs={{0,5},{1,4},{2,7},{3,6},{4,1},{5,0},{6,3},{7,2},{8,13},{9,12},{10,... | collective-permute-start | bytes 491528 | tf_op jit(solution)/shard_map/ppermute | solution.py:347
  45.4 9.8 %collective-permute-start.9 = (f32[128,512]{1,0:T(8,128)S(1)}, f32[128,512]{1,0:T(8,128)S(1)}, u32[]{:S(2)}, u32[]{:S(2)}) collective-permute-start(f32[128,512]{1,0:T(8,128)S(1)} %shard_map.93), channel_id=1, source_target_pairs={{0,8},{2,10},{4,12},{6,14},{8,0},{10,2},{12,4},{14,6},{16,24},{18,... | collective-permute-start | bytes 786440 | tf_op jit(solution)/shard_map/ppermute | solution.py:460
  48.9 12.2 %collective-permute-start.14 = (f32[128,512]{1,0:T(8,128)S(1)}, f32[128,512]{1,0:T(8,128)S(1)}, u32[]{:S(2)}, u32[]{:S(2)}) collective-permute-start(f32[128,512]{1,0:T(8,128)S(1)} %shard_map.98), channel_id=1, source_target_pairs={{0,0},{2,2},{4,4},{6,6},{8,16},{10,18},{12,20},{14,22},{16,8},{18,... | collective-permute-start | bytes 786440 | tf_op jit(solution)/shard_map/ppermute | solution.py:451
  49.6 7.9 %collective-permute-start.16 = (f32[320,128]{1,0:T(8,128)S(1)}, f32[320,128]{1,0:T(8,128)S(1)}, u32[]{:S(2)}, u32[]{:S(2)}) collective-permute-start(f32[320,128]{1,0:T(8,128)S(1)} %get-tuple-element.110), channel_id=1, source_target_pairs={{0,3},{1,2},{2,1},{3,0},{4,7},{5,6},{6,5},{7,4},{8,11},{9,10},{10,... | collective-permute-start | bytes 491528 | tf_op jit(solution)/shard_map/ppermute | solution.py:347
  50.3 9.7 %collective-permute-start.17 = (f32[320,128]{1,0:T(8,128)S(1)}, f32[320,128]{1,0:T(8,128)S(1)}, u32[]{:S(2)}, u32[]{:S(2)}) collective-permute-start(f32[320,128]{1,0:T(8,128)S(1)} %get-tuple-element.111), channel_id=1, source_target_pairs={{0,7},{1,6},{2,5},{3,4},{4,3},{5,2},{6,1},{7,0},{8,15},{9,14},{10,... | collective-permute-start | bytes 491528 | tf_op jit(solution)/shard_map/ppermute | solution.py:347
  51.9 12.4 %collective-permute-start.15 = (f32[128,512]{1,0:T(8,128)S(1)}, f32[128,512]{1,0:T(8,128)S(1)}, u32[]{:S(2)}, u32[]{:S(2)}) collective-permute-start(f32[128,512]{1,0:T(8,128)S(1)} %shard_map.98), channel_id=1, source_target_pairs={{8,24},{10,26},{12,28},{14,30},{16,0},{18,2},{20,4},{22,6},{9,25},... | collective-permute-start | bytes 786440 | tf_op jit(solution)/shard_map/ppermute | solution.py:451
  55.9 8.4 %collective-permute-start.18 = (f32[256,128]{1,0:T(8,128)S(1)}, f32[256,128]{1,0:T(8,128)S(1)}, u32[]{:S(2)}, u32[]{:S(2)}) collective-permute-start(f32[256,128]{1,0:T(8,128)S(1)} %get-tuple-element.112), channel_id=1, source_target_pairs={{0,4},{2,6},{4,0},{6,2},{8,12},{10,14},{12,8},{14,10},{16,20},{18,... | collective-permute-start | bytes 393224 | tf_op jit(solution)/shard_map/ppermute | solution.py:341
  57.5 6.8 %collective-permute-start.19 = (f32[256,128]{1,0:T(8,128)S(1)}, f32[256,128]{1,0:T(8,128)S(1)}, u32[]{:S(2)}, u32[]{:S(2)}) collective-permute-start(f32[256,128]{1,0:T(8,128)S(1)} %get-tuple-element.113), channel_id=1, source_target_pairs={{0,2},{2,0},{4,6},{6,4},{8,10},{10,8},{12,14},{14,12},{16,18},{18,... | collective-permute-start | bytes 393224 | tf_op jit(solution)/shard_map/ppermute | solution.py:341
  60.0 7.2 %collective-permute-start.26 = (f32[256,128]{1,0:T(8,128)S(1)}, f32[256,128]{1,0:T(8,128)S(1)}, u32[]{:S(2)}, u32[]{:S(2)}) collective-permute-start(f32[256,128]{1,0:T(8,128)S(1)} %get-tuple-element.122), channel_id=1, source_target_pairs={{0,6},{2,4},{4,2},{6,0},{8,14},{10,12},{12,10},{14,8},{16,22},{18,... | collective-permute-start | bytes 393224 | tf_op jit(solution)/shard_map/ppermute | solution.py:341
  61.1 8.6 %collective-permute-start.25 = (f32[256,128]{1,0:T(8,128)S(1)}, f32[256,128]{1,0:T(8,128)S(1)}, u32[]{:S(2)}, u32[]{:S(2)}) collective-permute-start(f32[256,128]{1,0:T(8,128)S(1)} %get-tuple-element.120), channel_id=1, source_target_pairs={{0,6},{2,4},{4,2},{6,0},{8,14},{10,12},{12,10},{14,8},{16,22},{18,... | collective-permute-start | bytes 393224 | tf_op jit(solution)/shard_map/ppermute | solution.py:341
  64.3 7.6 %collective-permute-start.24 = (f32[320,128]{1,0:T(8,128)S(1)}, f32[320,128]{1,0:T(8,128)S(1)}, u32[]{:S(2)}, u32[]{:S(2)}) collective-permute-start(f32[320,128]{1,0:T(8,128)S(1)} %get-tuple-element.118), channel_id=1, source_target_pairs={{0,1},{1,0},{2,3},{3,2},{4,5},{5,4},{6,7},{7,6},{8,9},{9,8},{10,11... | collective-permute-start | bytes 491528 | tf_op jit(solution)/shard_map/ppermute | solution.py:347
  64.9 8.6 %collective-permute-start.20 = (f32[320,128]{1,0:T(8,128)S(1)}, f32[320,128]{1,0:T(8,128)S(1)}, u32[]{:S(2)}, u32[]{:S(2)}) collective-permute-start(f32[320,128]{1,0:T(8,128)S(1)} %get-tuple-element.114), channel_id=1, source_target_pairs={{0,1},{1,0},{2,3},{3,2},{4,5},{5,4},{6,7},{7,6},{8,9},{9,8},{10,11... | collective-permute-start | bytes 491528 | tf_op jit(solution)/shard_map/ppermute | solution.py:347
  65.5 8.0 %collective-permute-start.21 = (f32[320,128]{1,0:T(8,128)S(1)}, f32[320,128]{1,0:T(8,128)S(1)}, u32[]{:S(2)}, u32[]{:S(2)}) collective-permute-start(f32[320,128]{1,0:T(8,128)S(1)} %get-tuple-element.115), channel_id=1, source_target_pairs={{0,5},{1,4},{2,7},{3,6},{4,1},{5,0},{6,3},{7,2},{8,13},{9,12},{10,... | collective-permute-start | bytes 491528 | tf_op jit(solution)/shard_map/ppermute | solution.py:347
  67.2 6.4 %collective-permute-start.22 = (f32[320,128]{1,0:T(8,128)S(1)}, f32[320,128]{1,0:T(8,128)S(1)}, u32[]{:S(2)}, u32[]{:S(2)}) collective-permute-start(f32[320,128]{1,0:T(8,128)S(1)} %get-tuple-element.116), channel_id=1, source_target_pairs={{0,3},{1,2},{2,1},{3,0},{4,7},{5,6},{6,5},{7,4},{8,11},{9,10},{10,... | collective-permute-start | bytes 491528 | tf_op jit(solution)/shard_map/ppermute | solution.py:347
  69.7 7.4 %collective-permute-start.23 = (f32[320,128]{1,0:T(8,128)S(1)}, f32[320,128]{1,0:T(8,128)S(1)}, u32[]{:S(2)}, u32[]{:S(2)}) collective-permute-start(f32[320,128]{1,0:T(8,128)S(1)} %get-tuple-element.117), channel_id=1, source_target_pairs={{0,7},{1,6},{2,5},{3,4},{4,3},{5,2},{6,1},{7,0},{8,15},{9,14},{10,... | collective-permute-start | bytes 491528 | tf_op jit(solution)/shard_map/ppermute | solution.py:347
  71.9 6.1 %collective-permute-start.28 = (f32[32,128]{1,0:T(8,128)S(1)}, f32[32,128]{1,0:T(8,128)S(1)}, u32[]{:S(2)}, u32[]{:S(2)}) collective-permute-start(f32[32,128]{1,0:T(8,128)S(1)} %get-tuple-element.137), channel_id=1, source_target_pairs={{0,1},{1,0},{2,3},{3,2},{4,5},{5,4},{6,7},{7,6},{8,9},{9,8},{10,11... | collective-permute-start | bytes 49160 | tf_op jit(solution)/shard_map/ppermute | solution.py:535
  77.2 1.2 %collective-permute-start.27 = (f32[32,128]{1,0:T(8,128)S(1)}, f32[32,128]{1,0:T(8,128)S(1)}, u32[]{:S(2)}, u32[]{:S(2)}) collective-permute-start(f32[32,128]{1,0:T(8,128)S(1)} %get-tuple-element.133), channel_id=1, source_target_pairs={{0,1},{1,0},{2,3},{3,2},{4,5},{5,4},{6,7},{7,6},{8,9},{9,8},{10,11... | collective-permute-start | bytes 49160 | tf_op jit(solution)/shard_map/ppermute | solution.py:535
